TPU v7x, 512 devices: a whole 4x4x16 slice. The times are simulated.
512 devices in a mesh: tiles: 32 (over z, core), dp: 16 (over y, x).
Axes of the slice: x: 4, y: 4, z: 16, core: 2. Of those that a mesh axis runs over, the one named last changes fastest.
Arguments:
- fields: bfloat16 [16, 64, 32, 32, 256], P('dp', 'tiles'), may hold values from -6 to 6
- neighbours: int32 [64, 8], P('tiles'), may hold values from -1 to 63, as said below
- kernel: float32 [7, 7, 256], replicated, may hold values from -0.875 to 0.875
- gain: float32 [256], replicated, may hold values from 0.1 to 1.9
- w_in: bfloat16 [256, 1024], replicated, may hold values from -0.375 to 0.375
- w_out: bfloat16 [1024, 256], replicated, may hold values from -0.1875 to 0.1875
- cotangent: bfloat16 [16, 64, 32, 32, 256], P('dp', 'tiles'), may hold values from -6 to 6
Outputs:
- grad_fields: bfloat16 [16, 64, 32, 32, 256], P('dp', 'tiles')
- grad_w_in: float32 [256, 1024], P(None, 'dp')
- grad_w_out: float32 [1024, 256], P('dp')
- grad_kernel: float32 [7, 7, 256], replicated
- gradient_by_gain: float32 [256], replicated
Inputs may be any that keep to these rules, and one draw needn't show every extreme that they name: `neighbours`: wet tiles of a slab of 3 rows and 32 columns (longitude wraps), numbered column by column; a neighbour's slot differs from the tile's own by at most 4 around the slot order, and this distance is reached; the relation is symmetric (b is a's neighbour in a direction exactly when a is b's in the opposite one).
All inputs are finite; a program needn't handle non-finite values.
Results may differ from a plain program's by a relative error of at most 0.0056.
Values may be sent and summed in bfloat16 or wider, within the bound.
No kernel may reach another device: no remote copies, remote signals or barrier semaphores. Data moves between devices by JAX's collectives and lax.ppermute only.
A program may use at most 64 MiB of HBM per device.

v0:
```python
import jax
import jax.numpy as jnp
from jax import lax
from jax.sharding import PartitionSpec as P

KW = 7
REACH = 2


def from_behind(block, axis, distance):
    devices = range(lax.axis_size(axis))
    route = [((i - distance) % len(devices), i) for i in devices]
    return lax.ppermute(block, axis, route)


def rims_of(tiles):
    top = tiles[..., :3, :, :]
    bottom = tiles[..., -3:, :, :]
    left = jnp.swapaxes(tiles[..., :, :3, :], -3, -2)
    right = jnp.swapaxes(tiles[..., :, -3:, :], -3, -2)
    return jnp.stack([top, bottom, left, right], axis=-4)


def assemble(tiles, near):
    north = near[..., 0, 1, :, :, :]
    south = near[..., 1, 0, :, :, :]
    west = jnp.swapaxes(near[..., 2, 3, :, :, :], -3, -2)
    east = jnp.swapaxes(near[..., 3, 2, :, :, :], -3, -2)
    corner_nw = near[..., 4, 1, :, -3:, :]
    corner_ne = near[..., 5, 1, :, :3, :]
    corner_sw = near[..., 6, 0, :, -3:, :]
    corner_se = near[..., 7, 0, :, :3, :]
    upper = jnp.concatenate([corner_nw, north, corner_ne], axis=-2)
    middle = jnp.concatenate([west, tiles, east], axis=-2)
    lower = jnp.concatenate([corner_sw, south, corner_se], axis=-2)
    return jnp.concatenate([upper, middle, lower], axis=-3)


def depthwise(padded, kern, size):
    total = jnp.zeros(padded.shape[:-3] + (size, size, padded.shape[-1]), jnp.float32)
    for row in range(KW):
        for col in range(KW):
            total = total + padded[..., row : row + size, col : col + size, :] * kern[row, col]
    return total


def gelu_exact(value):
    return jax.nn.gelu(value, approximate=False)


def window_of(tiles):
    rims = rims_of(tiles)
    pieces = {0: rims}
    for offset in [k for k in range(-REACH, REACH + 1) if k != 0]:
        pieces[offset] = from_behind(rims, "tiles", -offset)
    return jnp.concatenate([pieces[k] for k in range(-REACH, REACH + 1)], axis=1)


def body(fields, neighbours, kernel, gain, w_in, w_out, cotangent):
    tile_dev = fields.shape[1]
    size = fields.shape[2]
    samples = fields.shape[0]
    channels = fields.shape[4]
    own = lax.axis_index("tiles")
    count_tiles = lax.axis_size("tiles")
    count_dp = lax.axis_size("dp")
    valid = neighbours >= 0
    owner = jnp.floor_divide(neighbours, tile_dev)
    offset = jnp.mod(owner - own + REACH, count_tiles) - REACH
    local = (offset + REACH) * tile_dev + jnp.mod(neighbours, tile_dev)
    picked = jnp.where(valid, local, 0).reshape(-1)

    def widen(tiles):
        window = window_of(tiles)
        near = jnp.take(window, picked, axis=1)
        near = near.reshape((samples, tile_dev, 8) + window.shape[2:])
        near = jnp.where(
            valid[None, :, :, None, None, None, None], near, jnp.zeros((), tiles.dtype)
        )
        return assemble(tiles, near)

    padded = widen(fields)
    convolved_state = depthwise(padded, kernel, size)
    channel_mean = jnp.mean(convolved_state, axis=-1, keepdims=True)
    var = jnp.mean((convolved_state - channel_mean) ** 2, axis=-1, keepdims=True)
    inverse_deviation = lax.rsqrt(var + 1e-06)
    centered_standardized = (convolved_state - channel_mean) * inverse_deviation
    layer_normalized = (centered_standardized * gain).astype(jnp.bfloat16)
    rows_n = layer_normalized.reshape(-1, channels)
    pre = jnp.dot(rows_n, w_in, preferred_element_type=jnp.float32)
    act = gelu_exact(pre).astype(jnp.bfloat16)
    rows_g = cotangent.reshape(-1, channels)
    gw_out = lax.dot_general(
        act, rows_g, (((0,), (0,)), ((), ())), preferred_element_type=jnp.float32
    )
    grad_act = lax.dot_general(
        rows_g, w_out, (((1,), (1,)), ((), ())), preferred_element_type=jnp.float32
    )
    pullback = jax.vjp(gelu_exact, pre)[1]
    grad_pre = pullback(grad_act)[0].astype(jnp.bfloat16)
    gw_in_t = lax.dot_general(
        grad_pre, rows_n, (((0,), (0,)), ((), ())), preferred_element_type=jnp.float32
    )
    normalized_gradient = lax.dot_general(
        grad_pre, w_in, (((1,), (1,)), ((), ())), preferred_element_type=jnp.float32
    )
    normalized_gradient = normalized_gradient.reshape(convolved_state.shape)
    gradient_by_gain = jnp.sum(normalized_gradient * centered_standardized, axis=(0, 1, 2, 3))
    gain_scaled = normalized_gradient * gain
    convolved_gradient = inverse_deviation * (
        gain_scaled
        - jnp.mean(gain_scaled, axis=-1, keepdims=True)
        - centered_standardized
        * jnp.mean(gain_scaled * centered_standardized, axis=-1, keepdims=True)
    )
    convolved_gradient = convolved_gradient.astype(jnp.bfloat16)
    conv_f = convolved_gradient.astype(jnp.float32)
    kern_rows = []
    for row in range(KW):
        for col in range(KW):
            piece = padded[..., row : row + size, col : col + size, :].astype(jnp.float32)
            kern_rows.append(jnp.sum(piece * conv_f, axis=(0, 1, 2, 3)))
    grad_kernel = jnp.stack(kern_rows, axis=0).reshape(KW, KW, channels)
    grad_padded = widen(convolved_gradient)
    grad_x = depthwise(grad_padded, kernel[::-1, ::-1], size)
    grad_fields = (cotangent.astype(jnp.float32) + grad_x).astype(jnp.bfloat16)
    combined = jnp.concatenate([gw_in_t, gw_out], axis=1)
    summed = lax.psum(combined, "tiles")
    mine = lax.psum_scatter(summed, "dp", scatter_dimension=0, tiled=True)
    kern_total, gain_total = lax.psum((grad_kernel, gradient_by_gain), ("tiles", "dp"))
    scale = 1.0 / jnp.sqrt(jnp.float32(samples * count_dp * tile_dev * count_tiles * size * size))
    grad_w_in = mine[:, :channels].T * scale
    grad_w_out = mine[:, channels:] * scale
    return (grad_fields, grad_w_in, grad_w_out, kern_total * scale, gain_total * scale)


def solution(mesh):
    return jax.shard_map(
        body,
        mesh=mesh,
        in_specs=(
            P("dp", "tiles", None, None, None),
            P("tiles", None),
            P(),
            P(),
            P(),
            P(),
            P("dp", "tiles", None, None, None),
        ),
        out_specs=(P("dp", "tiles", None, None, None), P(None, "dp"), P("dp", None), P(), P()),
        check_vma=False,
    )
```

profile of v0, /device:TPU:1, one launch (start us, length us, event | category | flops | bytes accessed | tf_op | source)
XLA Modules:
  0.0 472.3 jit_solution(2977046117482885369)
XLA Ops:
  8.3 1.9 copy.89
  11.1 11.9 %collective-permute-start.3 = (bf16[1,2,4,3,32,256]{5,4,3,2,1,0:T(8,128)(2,1)}, bf16[1,2,4,3,32,256]{5,4,3,2,1,0:T(8,128)(2,1)}, u32[]{:S(2)}, u32[]{:S(2)}) collective-permute-start(bf16[1,2,4,3,32,256]{5,4,3,2,1,0:T(8,128)(2,1)} %pad_maximum_fusion.7), channel_id=1, source_target_pairs={{32,0},{48,16},{64,32},{80,48},{96,64},{112,80},{128,96},{144,112}... | collective-permute-start | bytes 1179656 | tf_op jit(solution)/shard_map/ppermute | solution.py:13
  24.9 1.9 collective-permute-start
  30.6 10.1 %collective-permute-done = bf16[1,2,4,3,32,256]{5,4,3,2,1,0:T(8,128)(2,1)} collective-permute-done((bf16[1,2,4,3,32,256]{5,4,3,2,1,0:T(8,128)(2,1)}, bf16[1,2,4,3,32,256]{5,4,3,2,1,0:T(8,128)(2,1)}, u32[]{:S(2)}, u32[]{:S(2)}) %collective-permute-start) | collective-permute-done | bytes 393248 | tf_op jit(solution)/shard_map/ppermute | solution.py:13
  42.8 1.1 constant_dynamic-update-slice_fusion.2
  45.9 2.5 gather_fusion
  48.5 2.3 bitcast_select_fusion.1
  53.2 19.0 %fusion.144 = (f32[2,32,32]{1,2,0:T(8,128)S(1)}, f32[1,2,32,32,256]{4,2,3,1,0:T(8,128)S(1)}) fusion(f32[256]{0:T(256)S(1)} %bitcast.215, bf16[1,2,35,38,256]{4,2,3,1,0:T(8,128)(2,1)S(1)} %get-tuple-element.115, f32[256]{0:T(256)S(1)} %bitcast.217, f32[256]{0:T(256)S(1)} %bitcast.221, f32[256]{0:T(256)S(1)} %bitcast.223, f32[256]{0:T(256)S(1)} %bitcast.225, ...), kind=kLoop, calls=%fused_computation.354 | loop fusion | flops 80214016 | bytes 47440896 | tf_op jit(solution)/shard_map/reduce_sum | solution.py:84
  74.3 19.9 %fusion = (f32[2048,1024]{1,0:T(8,128)S(1)}, f32[2048,1024]{1,0:T(8,128)S(1)}) fusion(bf16[2048,256]{1,0:T(8,128)(2,1)S(1)} %bitcast.195, bf16[256,1024]{1,0:T(8,128)(2,1)S(1)} %copy-done), kind=kOutput, calls=%fused_computation.53 | convolution fusion | flops 1203765248 | bytes 18350080 | tf_op jit(solution)/shard_map/dot_general | solution.py:90
  94.2 2.5 fusion.6
  96.7 5.2 %add_convert_fusion = bf16[2048,1024]{1,0:T(8,128)(2,1)} fusion(f32[2048,1024]{1,0:T(8,128)S(1)} %get-tuple-element.175, f32[2048,1024]{1,0:T(8,128)S(1)} %get-tuple-element.176, bf16[2048,256]{1,0:T(8,128)(2,1)S(1)} %bitcast.194, bf16[1024,256]{1,0:T(8,128)(2,1)S(1)} %copy-done.105), kind=kOutput, calls=%fused_computation.55 | convolution fusion | flops 1103101952 | bytes 22544384 | tf_op jit(solution)/shard_map/dot_general | solution.py:96
  101.9 4.7 fusion.149
  106.6 2.7 multiply_reduce_fusion.2
  109.5 4.5 multiply_reduce_fusion
  114.0 7.8 %fusion.129 = (f32[256]{0:T(256)S(1)}, f32[256]{0:T(256)S(1)}, f32[256]{0:T(256)S(1)}, f32[256]{0:T(256)S(1)}, f32[256]{0:T(256)S(1)}, /*index=5*/f32[256]{0:T(2...) fusion(bf16[1,2,35,38,256]{4,2,3,1,0:T(8,128)(2,1)S(1)} %get-tu, ...), kind=kLoop, calls=%fused_computation.245 | loop fusion | flops 33025536 | bytes 24169472 | tf_op jit(solution)/shard_map/reduce_sum | solution.py:122
  121.8 3.3 fusion.128
  126.9 1.9 collective-permute-start.7
  128.8 1.7 collective-permute-start.5
  130.5 3.4 collective-permute-start.4
  133.9 1.5 pad_maximum_fusion
  135.4 2.9 copy.111
  138.4 1.3 copy-done.2
  140.3 5.5 %fusion.101 = (f32[256]{0:T(256)S(1)}, f32[256]{0:T(256)S(1)}, f32[256]{0:T(256)S(1)}, f32[256]{0:T(256)S(1)}, f32[256]{0:T(256)S(1)}, /*index=5*/f32[256]{0:T(2...) fusion(bf16[1,2,32,32,256]{4,2,3,1,0:T(8,128)(2,1)S(1)} %get-tu, ...), kind=kLoop, calls=%fused_computation.217 | loop fusion | flops 28831232 | bytes 19941376 | tf_op jit(solution)/shard_map/reduce_sum | solution.py:122
  146.0 103.2 %all-reduce = (f32[7,7,256]{2,1,0:T(8,128)S(1)}, f32[256]{0:T(256)S(1)}) all-reduce(f32[7,7,256]{2,1,0:T(8,128)S(1)} %reshape.438, f32[256]{0:T(256)S(1)} %copy-done.101), channel_id=1, replica_groups=mesh['tiles'=32,'dp'=16] {'tiles','dp'}, use_global_device_ids=true, to_apply=%region_55.57 | all-reduce | flops 12800 | bytes 102400 | tf_op jit(solution)/shard_map/psum | solution.py:130
  252.4 1.1 constant_dynamic-update-slice_fusion.7
  255.5 2.5 gather_fusion.1
  258.1 2.3 bitcast_select_fusion
  261.4 1.8 maximum_maximum_fusion.1
  263.1 1.7 copy.112
  265.3 30.3 %add_convert_fusion.1 = bf16[1,2,32,32,256]{4,2,3,1,0:T(8,128)(2,1)S(1)} fusion(bf16[1,2,32,32,256]{4,2,3,1,0:T(8,128)(2,1)S(1)} %get-tuple-element.93, bf16[1,2,32,3,256]{4,2,3,1,0:T(8,128)(2,1)S(1)} %get-tuple-element.102, bf16[1,2,32,3,256]{4,2,3,1,0:T(8,128)(2,1)S(1)} %get-tuple-element.103, bf16[1,2,35,38,256]{4,2,3,1,0:T(8,128)(2,1)} %get-tuple-element.113, ...), kind=kLoop, calls=%fused_computation.248 | loop fusion | flops 81264640 | bytes 47432704 | tf_op jit(solution)/shard_map/convert_element_type | solution.py:126
  295.6 1.6 copy.108
  297.1 165.9 %all-reduce.3.cloned.1.call-done = f32[64,512]{0,1:T(8,128)} async-done(((f32[64,512]{0,1:T(8,128)}), f32[64,512]{0,1:T(8,128)}) %all-reduce.3.cloned.1.call-update) | async-done | bytes 131088 | tf_op jit(solution)/shard_map/psum | solution.py:128
  (285 shorter events, 26.5 us)
Async XLA Ops:
  7.2 67.1 %copy-start = (bf16[256,1024]{1,0:T(8,128)(2,1)S(1)}, bf16[256,1024]{1,0:T(8,128)(2,1)}, u32[]{:S(2)}) copy-start(bf16[256,1024]{1,0:T(8,128)(2,1)} %param.13) | copy-start | bytes 1572868
  7.2 19.6 %copy-start.20 = (f32[7,7,256]{2,1,0:T(8,128)S(1)}, f32[7,7,256]{2,1,0:T(8,128)}, u32[]{:S(2)}) copy-start(f32[7,7,256]{2,1,0:T(8,128)} %param.11) | copy-start | bytes 150532
  7.2 21.6 %copy-start.104 = (s32[2,8]{1,0:T(2,128)S(1)}, s32[2,8]{1,0:T(2,128)}, u32[]{:S(2)}) copy-start(s32[2,8]{1,0:T(2,128)} %param.10) | copy-start | bytes 196
  7.2 255.9 %reduce-scatter.4.cloned.1.call-start = ((), (), s32[]{:S(2)}) async-start(), calls=%async_computation.2 | async-start | bytes 2228224
  10.2 42.7 %copy-start.5 = (bf16[1,2,32,32,256]{4,2,3,1,0:T(8,128)(2,1)}, bf16[1,2,32,32,256]{4,2,3,1,0:T(8,128)(2,1)S(1)}, u32[]{:S(2)}) copy-start(bf16[1,2,32,32,256]{4,2,3,1,0:T(8,128)(2,1)S(1)} %copy.89) | copy-start | bytes 3145732
  10.2 12.9 %copy-start.18 = (bf16[1,2,1,3,32,256]{5,4,3,2,1,0:T(8,128)(2,1)}, bf16[1,2,1,3,32,256]{5,4,3,2,1,0:T(8,128)(2,1)S(1)}, u32[]{:S(2)}) copy-start(bf16[1,2,1,3,32,256]{5,4,3,2,1,0:T(8,128)(2,1)S(1)} %get-tuple-element.122) | copy-start | bytes 294916
  10.2 13.9 %copy-start.19 = (bf16[1,2,1,3,32,256]{5,4,3,2,1,0:T(8,128)(2,1)}, bf16[1,2,1,3,32,256]{5,4,3,2,1,0:T(8,128)(2,1)S(1)}, u32[]{:S(2)}) copy-start(bf16[1,2,1,3,32,256]{5,4,3,2,1,0:T(8,128)(2,1)S(1)} %get-tuple-element.123) | copy-start | bytes 294916
  11.1 33.7 %collective-permute-start.3 = (bf16[1,2,4,3,32,256]{5,4,3,2,1,0:T(8,128)(2,1)}, bf16[1,2,4,3,32,256]{5,4,3,2,1,0:T(8,128)(2,1)}, u32[]{:S(2)}, u32[]{:S(2)}) collective-permute-start(bf16[1,2,4,3,32,256]{5,4,3,2,1,0:T(8,128)(2,1)} %pad_maximum_fusion.7), channel_id=1, source_target_pairs={{32,0},{48,16},{64,32},{80,48},{96,64},{112,80},{128,96},{144,112}... | collective-permute-start | bytes 1179656 | tf_op jit(solution)/shard_map/ppermute | solution.py:13
  23.1 20.7 %collective-permute-start.2 = (bf16[1,2,4,3,32,256]{5,4,3,2,1,0:T(8,128)(2,1)}, bf16[1,2,4,3,32,256]{5,4,3,2,1,0:T(8,128)(2,1)}, u32[]{:S(2)}, u32[]{:S(2)}) collective-permute-start(bf16[1,2,4,3,32,256]{5,4,3,2,1,0:T(8,128)(2,1)} %pad_maximum_fusion.7), channel_id=1, source_target_pairs={{16,0},{32,16},{48,32},{64,48},{80,64},{96,80},{112,96},{128,112},... | collective-permute-start | bytes 1179656 | tf_op jit(solution)/shard_map/ppermute | solution.py:13
  24.1 17.7 %collective-permute-start.1 = (bf16[1,2,4,3,32,256]{5,4,3,2,1,0:T(8,128)(2,1)}, bf16[1,2,4,3,32,256]{5,4,3,2,1,0:T(8,128)(2,1)}, u32[]{:S(2)}, u32[]{:S(2)}) collective-permute-start(bf16[1,2,4,3,32,256]{5,4,3,2,1,0:T(8,128)(2,1)} %pad_maximum_fusion.7), channel_id=1, source_target_pairs={{496,0},{0,16},{16,32},{32,48},{48,64},{64,80},{80,96},{96,112},{1... | collective-permute-start | bytes 1179656 | tf_op jit(solution)/shard_map/ppermute | solution.py:13
  24.9 15.8 %collective-permute-start = (bf16[1,2,4,3,32,256]{5,4,3,2,1,0:T(8,128)(2,1)}, bf16[1,2,4,3,32,256]{5,4,3,2,1,0:T(8,128)(2,1)}, u32[]{:S(2)}, u32[]{:S(2)}) collective-permute-start(bf16[1,2,4,3,32,256]{5,4,3,2,1,0:T(8,128)(2,1)} %pad_maximum_fusion.7), channel_id=1, source_target_pairs={{480,0},{496,16},{0,32},{16,48},{32,64},{48,80},{64,96},{80,112},{... | collective-permute-start | bytes 1179656 | tf_op jit(solution)/shard_map/ppermute | solution.py:13
  52.8 19.4 %copy-start.1 = (bf16[1,2,35,38,256]{4,2,3,1,0:T(8,128)(2,1)}, bf16[1,2,35,38,256]{4,2,3,1,0:T(8,128)(2,1)S(1)}, u32[]{:S(2)}) copy-start(bf16[1,2,35,38,256]{4,2,3,1,0:T(8,128)(2,1)S(1)} %get-tuple-element.114) | copy-start | bytes 4085764
  74.3 19.9 %copy-start.10 = (bf16[1,2,32,32,256]{4,3,2,1,0:T(8,128)(2,1)S(1)}, bf16[1,2,32,32,256]{4,3,2,1,0:T(8,128)(2,1)}, u32[]{:S(2)}) copy-start(bf16[1,2,32,32,256]{4,3,2,1,0:T(8,128)(2,1)} %param.15) | copy-start | bytes 3145732
  101.9 4.7 copy-start.106
  109.5 4.5 copy-start.4
  109.5 4.5 copy-start.7
  114.0 7.8 %copy-start.6 = (bf16[1,2,32,32,256]{4,2,3,1,0:T(8,128)(2,1)S(1)}, bf16[1,2,32,32,256]{4,2,3,1,0:T(8,128)(2,1)}, u32[]{:S(2)}) copy-start(bf16[1,2,32,32,256]{4,2,3,1,0:T(8,128)(2,1)} %copy-done.5) | copy-start | bytes 3145732
  114.0 7.8 %copy-start.9 = (bf16[1,2,32,32,256]{4,3,2,1,0:T(8,128)(2,1)S(1)}, bf16[1,2,32,32,256]{4,3,2,1,0:T(8,128)(2,1)}, u32[]{:S(2)}) copy-start(bf16[1,2,32,32,256]{4,3,2,1,0:T(8,128)(2,1)} %param.9) | copy-start | bytes 3145732
  125.2 8.7 %copy-start.8 = (f32[1024,256]{0,1:T(8,128)S(1)}, f32[1024,256]{0,1:T(8,128)}, u32[]{:S(2)}) copy-start(f32[1024,256]{0,1:T(8,128)} %fusion.6) | copy-start | bytes 3145732
  125.2 8.7 %copy-start.11 = (f32[1024,256]{0,1:T(8,128)S(1)}, f32[1024,256]{0,1:T(8,128)}, u32[]{:S(2)}) copy-start(f32[1024,256]{0,1:T(8,128)} %fusion.149) | copy-start | bytes 3145732
  126.9 127.6 %collective-permute-start.7 = (bf16[1,2,4,3,32,256]{5,4,3,2,1,0:T(8,128)(2,1)}, bf16[1,2,4,3,32,256]{5,4,3,2,1,0:T(8,128)(2,1)}, u32[]{:S(2)}, u32[]{:S(2)}) collective-permute-start(bf16[1,2,4,3,32,256]{5,4,3,2,1,0:T(8,128)(2,1)} %pad_maximum_fusion.8), channel_id=1, source_target_pairs={{32,0},{48,16},{64,32},{80,48},{96,64},{112,80},{128,96},{144,112}... | collective-permute-start | bytes 1179656 | tf_op jit(solution)/shard_map/ppermute | solution.py:13
  128.8 124.7 %collective-permute-start.6 = (bf16[1,2,4,3,32,256]{5,4,3,2,1,0:T(8,128)(2,1)}, bf16[1,2,4,3,32,256]{5,4,3,2,1,0:T(8,128)(2,1)}, u32[]{:S(2)}, u32[]{:S(2)}) collective-permute-start(bf16[1,2,4,3,32,256]{5,4,3,2,1,0:T(8,128)(2,1)} %pad_maximum_fusion.8), channel_id=1, source_target_pairs={{16,0},{32,16},{48,32},{64,48},{80,64},{96,80},{112,96},{128,112},... | collective-permute-start | bytes 1179656 | tf_op jit(solution)/shard_map/ppermute | solution.py:13
  128.8 122.5 %collective-permute-start.5 = (bf16[1,2,4,3,32,256]{5,4,3,2,1,0:T(8,128)(2,1)}, bf16[1,2,4,3,32,256]{5,4,3,2,1,0:T(8,128)(2,1)}, u32[]{:S(2)}, u32[]{:S(2)}) collective-permute-start(bf16[1,2,4,3,32,256]{5,4,3,2,1,0:T(8,128)(2,1)} %pad_maximum_fusion.8), channel_id=1, source_target_pairs={{496,0},{0,16},{16,32},{32,48},{48,64},{64,80},{80,96},{96,112},{1... | collective-permute-start | bytes 1179656 | tf_op jit(solution)/shard_map/ppermute | solution.py:13
  130.5 119.8 %collective-permute-start.4 = (bf16[1,2,4,3,32,256]{5,4,3,2,1,0:T(8,128)(2,1)}, bf16[1,2,4,3,32,256]{5,4,3,2,1,0:T(8,128)(2,1)}, u32[]{:S(2)}, u32[]{:S(2)}) collective-permute-start(bf16[1,2,4,3,32,256]{5,4,3,2,1,0:T(8,128)(2,1)} %pad_maximum_fusion.8), channel_id=1, source_target_pairs={{480,0},{496,16},{0,32},{16,48},{32,64},{48,80},{64,96},{80,112},{... | collective-permute-start | bytes 1179656 | tf_op jit(solution)/shard_map/ppermute | solution.py:13
  138.4 324.7 %all-reduce.3.cloned.1.call-start = ((), (), s32[]{:S(2)}) async-start(), calls=%async_computation.1 | async-start | bytes 524288 | tf_op jit(solution)/shard_map/psum | solution.py:128
  140.3 5.6 %copy-start.101 = (f32[256]{0:T(256)S(1)}, f32[256]{0:T(256)}, u32[]{:S(2)}) copy-start(f32[256]{0:T(256)} %get-tuple-element.31) | copy-start | bytes 3076
  261.0 3.9 copy-start.22
  261.0 3.9 copy-start.24
  261.0 3.9 copy-start.26
  261.0 3.9 copy-start.28
  261.0 3.9 copy-start.30
  261.0 3.9 copy-start.32
  (85 other events, 216.5 us)
Sparse Core Ops, SparseCore 0:
  138.5 82.5 reduce-scatter.3
  265.0 197.9 all-reduce.2
where the time goes:
time: 473 us; the launch traced here: 472 us
  waiting for transfers between devices  176 us (37%)
  blocking collectives  103 us (22%)
  other arithmetic  89.1 us (19%)
  matrix products  35 us (7%)
  local copies, waits for them, and re-layouts  30.3 us (6%)
  starting transfers between devices  22.7 us (5%)
  between operations  16 us (3%)
    psum x1, waiting for transfers between devices, body(): summed = lax.psum(combined, 'tiles')  166 us
    psum x1, blocking collectives, body(): lax.psum((grad_kernel, gradient_by_gain), ('tiles', 'dp'))  103 us
    convert_element_type x1, other arithmetic, body(): grad_fields = (cotangent.astype(jnp.float32) + grad_x).astype(jnp.bfloat16)  30.3 us
    ppermute x8, starting transfers between devices, from_behind(): return lax.ppermute(block, axis, route)  22.6 us
    dot_general x1, matrix products, body(): pre = jnp.dot(rows_n, w_in, preferred_element_type=jnp.float32)  19.9 us
    reduce_sum x1, other arithmetic, body(): channel_mean = jnp.mean(convolved_state, axis=-1, keepdims=True)  19 us
    unnamed x226, local copies, waits for them, and re-layouts  18.1 us
    reduce_sum x4, other arithmetic, body(): kern_rows.append(jnp.sum(piece * conv_f, axis=(0, 1, 2, 3)))  17.1 us
  transfers between devices with their start and end apart: 10, of which 2 were waited for; matrix products, arithmetic and copies ran while one was open for 14% of the time, Pallas kernels for 0%

commit v1 on v0

v1 whole, which is shorter than its diff:
```python
import functools

import jax
import jax.numpy as jnp
from jax import lax
from jax.experimental import pallas as pl
from jax.experimental.pallas import tpu as pltpu
from jax.sharding import PartitionSpec as P

KW = 7
TAPS = KW * KW
RIM = KW // 2
SIZE = 32
WIDE = SIZE + 2 * RIM
HALF = SIZE // 2
TALL = HALF + 2 * RIM
CH = 256
FF = 1024
ROWS = 256
VMEM_LIMIT = 56 * 1024 * 1024
F32 = jnp.float32
BF16 = jnp.bfloat16
OFFSETS = (0, -1, 1, -2, 2)
PAIRS = (
    ((0, 1), (1, 0)),
    ((0, 0), (0, 1), (1, 0), (1, 1)),
    ((0, 0), (0, 1), (1, 0), (1, 1)),
    ((0, 0), (0, 1), (1, 1)),
    ((0, 0), (1, 0), (1, 1)),
)
COUNTS = tuple(len(p) for p in PAIRS)
RIM_OF = (0, 1, 2, 3, 0, 0, 1, 1)


def place(half, tile, part):
    return 4 * half + 2 * tile + part


def lanes_of(part):
    return slice(part * 128, part * 128 + 128)


def put_row(grid, pitch, tile, row, first, value):
    count = value.shape[0]
    for half in range(2):
        i = row - HALF * half
        if 0 <= i < TALL:
            for part in range(2):
                at = (i * pitch + first) * 8 + place(half, tile, part)
                grid[pl.ds(at, count, stride=8), :] = value[:, lanes_of(part)]


def put_column(grid, tile, col, value):
    for half in range(2):
        lo = max(0, HALF * half - RIM)
        hi = min(SIZE, HALF * half + HALF + RIM)
        for part in range(2):
            at = ((lo + RIM - HALF * half) * WIDE + col) * 8 + place(half, tile, part)
            grid[pl.ds(at, hi - lo, stride=WIDE * 8), :] = value[lo:hi, lanes_of(part)]


def fetch_strips(near_ids, own, slots, strips, near):
    def fetch(p, carry):
        t, d = p // 8, p % 8
        slot = near_ids[t, d]
        other = slot // 2
        s = slot - 2 * other
        off = lax.rem(other - own + slots // 2 + slots // 4, slots // 2) - slots // 4
        off = jnp.where(slot < 0, slots, off)

        @pl.when(slot < 0)
        def _():
            near[p] = jnp.zeros((RIM, SIZE, CH), F32)

        for strip, offset in zip(strips, OFFSETS):
            index = s if offset == 0 else 2 * s + t if abs(offset) == 1 else s + t

            @pl.when(off == offset)
            def _(strip=strip, index=index):
                near[p] = strip[index].astype(F32)

        return carry

    lax.fori_loop(0, 16, fetch, 0)


def put_halo(near, grid):
    for t in range(2):
        for i in range(RIM):
            for row, mid, west, east in ((i, 0, 4, 5), (RIM + SIZE + i, 1, 6, 7)):
                put_row(grid, WIDE, t, row, 0, near[t * 8 + west, i, SIZE - RIM : SIZE, :])
                put_row(grid, WIDE, t, row, RIM, near[t * 8 + mid, i])
                put_row(grid, WIDE, t, row, RIM + SIZE, near[t * 8 + east, i, 0:RIM, :])
        for k in range(RIM):
            put_column(grid, t, k, near[t * 8 + 2, k])
            put_column(grid, t, RIM + SIZE + k, near[t * 8 + 3, k])


def pick_rim(near_ids, own, slots, s, offset, t):
    slot = lax.rem(2 * own + 2 * offset + t + slots, slots)
    rim = jnp.int32(0)
    for d in range(8):
        rim = jnp.where(near_ids[s, d] == slot, RIM_OF[d], rim)
    return 4 * s + rim


def send_strips(near_ids, own, slots, rims, outs):
    for out, offset, pairs in zip(outs, OFFSETS, PAIRS):
        for k, (s, t) in enumerate(pairs):
            out[k] = rims[pick_rim(near_ids, own, slots, s, offset, t)]


def spread_taps(kernel_ref, taps):
    even = lax.rem(lax.broadcasted_iota(jnp.int32, (8, 128), 0), 2) == 0
    for q in range(TAPS):
        low = jnp.broadcast_to(kernel_ref[q : q + 1, 0:128], (8, 128))
        high = jnp.broadcast_to(kernel_ref[q : q + 1, 128:256], (8, 128))
        taps[q] = jnp.where(even, low, high)


def convolve(grid3, taps, flip, out3):
    def column(j, carry):
        acc = [None] * HALF
        for b in range(KW):
            cells = [grid3[i * WIDE + j + b] for i in range(TALL)]
            for a in range(KW):
                q = a * KW + b
                tap = taps[TAPS - 1 - q if flip else q]
                for r in range(HALF):
                    term = cells[r + a] * tap
                    acc[r] = term if acc[r] is None else acc[r] + term
        for r in range(HALF):
            out3[r * SIZE + j] = acc[r]
        return carry

    lax.fori_loop(0, SIZE, column, 0)


def rows_of(flat, tile, half, r):
    return jnp.concatenate(
        [flat[pl.ds(r * SIZE * 8 + place(half, tile, part), SIZE, stride=8), :] for part in range(2)], axis=1
    )


def gelu_parts(x):
    size = jnp.abs(x)
    t = pl.reciprocal(1.0 + (0.3275911 * 0.7071067811865476) * size, approx=False)
    bell = jnp.exp2((-0.5 * 1.4426950408889634) * (x * x))
    poly = 0.5 * 1.061405429 * t - 0.5 * 1.453152027
    poly = poly * t + 0.5 * 1.421413741
    poly = poly * t - 0.5 * 0.284496736
    poly = poly * t + 0.5 * 0.254829592
    tail = poly * t * bell
    cdf = jnp.where(x < 0, tail, 1.0 - tail)
    return x * cdf, cdf + x * (bell * 0.3989422804014327)


def rim_kernel(own_ref, near_ids, tile_ref, *rest, slots):
    outs, (rims, stage) = rest[:5], rest[5:]
    for s in range(2):
        rims[4 * s] = tile_ref[s, 0:RIM]
        rims[4 * s + 1] = tile_ref[s, SIZE - RIM : SIZE]
        for side, first, row in ((2, 0, 0), (3, 16, 16 - RIM)):
            for part in range(2):
                stage[part] = tile_ref[s, :, first : first + 16, lanes_of(part)].astype(F32).reshape(SIZE * 16, 128)
                for k in range(RIM):
                    rims[4 * s + side, k, :, lanes_of(part)] = stage[part, pl.ds(row + k, SIZE, stride=16), :].astype(BF16)
    send_strips(near_ids, own_ref[0], slots, rims, outs)


def grid_kernel(tile_ref, grid):
    for t in range(2):
        for i in range(SIZE):
            put_row(grid, WIDE, t, RIM + i, RIM, tile_ref[t, i].astype(F32))


def main_kernel(own_ref, near_ids, s0, s1, s2, s3, s4, kernel_ref, gain_ref, w_in_ref, w_out_ref, cot_ref, grid_in,
                gw_ref, grad_grid, o0, o1, o2, o3, o4, ggain_ref, grid,
                near, taps, conv, gwi, gwo, rims, *, slots):
    own = own_ref[0]
    grid[...] = grid_in[...]
    fetch_strips(near_ids, own, slots, (s0, s1, s2, s3, s4), near)
    put_halo(near, grid)
    spread_taps(kernel_ref, taps)
    convolve(grid.reshape(TALL * WIDE, 8, 128), taps, False, conv.reshape(HALF * SIZE, 8, 128))
    gwi[...] = jnp.zeros_like(gwi)
    gwo[...] = jnp.zeros_like(gwo)
    ggain_ref[...] = jnp.zeros_like(ggain_ref)
    gain = gain_ref[...]
    lines = ROWS // SIZE

    def chunk(n, carry):
        tile, half, first = n // 4, (n // 2) % 2, (n % 2) * lines
        spot = place(half, tile, 0)
        cv = jnp.concatenate(
            [
                jnp.concatenate(
                    [conv[pl.ds((first + r) * SIZE * 8 + spot + part, SIZE, stride=8), :] for part in range(2)], axis=1
                )
                for r in range(lines)
            ],
            axis=0,
        )
        mean = jnp.mean(cv, axis=-1, keepdims=True)
        cv = cv - mean
        inv = lax.rsqrt(jnp.mean(cv * cv, axis=-1, keepdims=True) + 1e-06)
        xhat = cv * inv
        normed = (xhat * gain).astype(BF16)
        cot = cot_ref[pl.ds(pl.multiple_of(n * ROWS, ROWS), ROWS), :]
        normed_t = normed.T
        cot_t = cot.T
        gn = jnp.zeros((ROWS, CH), F32)
        for f in range(FF // 256):
            cols = slice(f * 256, f * 256 + 256)
            pre = jnp.dot(normed, w_in_ref[:, cols], preferred_element_type=F32)
            gact = lax.dot_general(cot, w_out_ref[cols, :], (((1,), (1,)), ((), ())), preferred_element_type=F32)
            act, slope = gelu_parts(pre)
            act = act.astype(BF16)
            gpre = (gact * slope).astype(BF16)
            gwi[:, cols] += jnp.dot(normed_t, gpre, preferred_element_type=F32)
            gwo[:, cols] += jnp.dot(cot_t, act, preferred_element_type=F32)
            gn += lax.dot_general(gpre, w_in_ref[:, cols], (((1,), (1,)), ((), ())), preferred_element_type=F32)
        ggain_ref[...] += jnp.sum((gn * xhat).reshape(ROWS // 8, 8, CH), axis=0)
        gx = gn * gain
        m1 = jnp.mean(gx, axis=-1, keepdims=True)
        m2 = jnp.mean(gx * xhat, axis=-1, keepdims=True)
        gc = (inv * (gx - m1 - xhat * m2)).astype(BF16).astype(F32)
        for r in range(lines):
            piece = gc[r * SIZE : (r + 1) * SIZE]
            at = ((first + r + RIM) * WIDE + RIM) * 8 + spot
            for part in range(2):
                grad_grid[pl.ds(at + part, SIZE, stride=8), :] = piece[:, lanes_of(part)]
        return carry

    lax.fori_loop(0, 2 * SIZE * SIZE // ROWS, chunk, 0)
    low = lax.broadcasted_iota(jnp.int32, (CH, 128), 1) < 64
    for p in range(FF // 128):
        one = gwi[:, p * 128 : p * 128 + 128]
        two = gwo[:, p * 128 : p * 128 + 128]
        gw_ref[2 * p] = jnp.where(low, one, pltpu.roll(two, 64, 1)).astype(BF16)
        gw_ref[2 * p + 1] = jnp.where(low, pltpu.roll(one, 64, 1), two).astype(BF16)
    for t in range(2):
        for part in range(2):
            for r in range(RIM):
                for half, at, other in ((0, RIM + HALF + r, RIM + r), (1, r, HALF + r)):
                    mine = ((at * WIDE) + RIM) * 8 + place(half, t, part)
                    theirs = ((other * WIDE) + RIM) * 8 + place(1 - half, t, part)
                    grad_grid[pl.ds(mine, SIZE, stride=8), :] = grad_grid[pl.ds(theirs, SIZE, stride=8), :]
            lanes = lanes_of(part)
            for k in range(RIM):
                top = ((RIM + k) * WIDE + RIM) * 8 + place(0, t, part)
                bottom = ((HALF + k) * WIDE + RIM) * 8 + place(1, t, part)
                rims[4 * t, k, :, lanes] = grad_grid[pl.ds(top, SIZE, stride=8), :].astype(BF16)
                rims[4 * t + 1, k, :, lanes] = grad_grid[pl.ds(bottom, SIZE, stride=8), :].astype(BF16)
                for side, col in ((2, RIM + k), (3, SIZE + k)):
                    both = [
                        grad_grid[pl.ds((RIM * WIDE + col) * 8 + place(half, t, part), HALF, stride=WIDE * 8), :]
                        for half in range(2)
                    ]
                    rims[4 * t + side, k, :, lanes] = jnp.concatenate(both, axis=0).astype(BF16)
    send_strips(near_ids, own, slots, rims, (o0, o1, o2, o3, o4))


def taps_kernel(grid, grad_grid, ggain_ref, out_ref, acc):
    grid3 = grid.reshape(TALL * WIDE, 8, 128)
    grad3 = grad_grid.reshape(TALL * WIDE, 8, 128)
    acc[...] = jnp.zeros_like(acc)

    def column(j, carry):
        g = [grad3[(RIM + r) * WIDE + RIM + j] for r in range(HALF)]
        for b in range(KW):
            cells = [grid3[i * WIDE + j + b] for i in range(TALL)]
            for a in range(KW):
                terms = [cells[r + a] * g[r] for r in range(HALF)]
                while len(terms) > 1:
                    terms = [terms[k] + terms[k + 1] for k in range(0, len(terms), 2)]
                acc[a * KW + b] += terms[0]
        return carry

    lax.fori_loop(0, SIZE, column, 0)
    sub = lax.broadcasted_iota(jnp.int32, (8, 128), 0)
    even = lax.rem(sub, 2) == 0
    sums = [[], []]
    for q in range(TAPS):
        one = acc[q]
        sums[0].append(jnp.sum(jnp.where(even, one, 0.0), axis=0, keepdims=True))
        sums[1].append(jnp.sum(jnp.where(even, 0.0, one), axis=0, keepdims=True))
    for part in range(2):
        sums[part].append(jnp.sum(ggain_ref[:, lanes_of(part)], axis=0, keepdims=True))
        sums[part].append(jnp.zeros((64 - TAPS - 1, 128), F32))
    total = jnp.concatenate(sums[0] + sums[1], axis=0).astype(BF16)
    for d in range(16):
        out_ref[d] = total


def back_kernel(own_ref, near_ids, s0, s1, s2, s3, s4, kernel_ref, cot_ref, grid_in, out_ref, grid, near, taps, conv, *, slots):
    grid[...] = grid_in[...]
    fetch_strips(near_ids, own_ref[0], slots, (s0, s1, s2, s3, s4), near)
    put_halo(near, grid)
    spread_taps(kernel_ref, taps)
    convolve(grid.reshape(TALL * WIDE, 8, 128), taps, True, conv.reshape(HALF * SIZE, 8, 128))
    for t in range(2):
        for i in range(SIZE):
            out_ref[t, i] = (cot_ref[t, i].astype(F32) + rows_of(conv, t, i // HALF, i % HALF)).astype(BF16)


def first_sum_kernel(w_ref, k_ref, out_ref, low, stage):
    low[...] = jnp.sum(k_ref[...].astype(F32), axis=0)
    weights = jnp.sum(w_ref[...].astype(F32), axis=0)
    stage[...] = jnp.zeros_like(stage)
    for p in range(32):
        stage[p, 0:8, :] = weights[8 * p : 8 * p + 8]
        stage[p, 8:12, :] = low[4 * p : 4 * p + 4, :]
    out_ref[...] = stage[...].astype(BF16)


def second_sum_kernel(in_ref, out_ref):
    total = jnp.sum(in_ref[...].astype(F32), axis=0).astype(BF16)
    for p in range(32):
        out_ref[p] = total


def last_kernel(in_ref, w_in_ref, w_out_ref, taps_ref, gain_ref, stage, low, *, scale):
    stage[...] = in_ref[...].astype(F32) * scale
    weights = stage[:, 0:8, :].reshape(CH, 128)
    w_in_ref[...] = weights[:, 0:64]
    w_out_ref[...] = weights.T[64:128, :]
    for p in range(32):
        low[4 * p : 4 * p + 4, :] = stage[p, 8:12, :]
    for part in range(2):
        lanes = lanes_of(part)
        taps_ref[:, lanes] = low[64 * part : 64 * part + TAPS, :]
        gain_ref[:, lanes] = low[64 * part + TAPS : 64 * part + TAPS + 1, :]


SMEM = pl.BlockSpec(memory_space=pltpu.SMEM)
STRIPS = tuple(jax.ShapeDtypeStruct((n, RIM, SIZE, CH), BF16) for n in COUNTS)
RIMS = pltpu.VMEM((8, RIM, SIZE, CH), BF16)
NEAR = pltpu.VMEM((16, RIM, SIZE, CH), F32)
GRID = jax.ShapeDtypeStruct((TALL * WIDE * 8, 128), F32)
GRID_SPACE = pltpu.VMEM(GRID.shape, F32)
SPREAD = pltpu.VMEM((TAPS, 8, 128), F32)
CONV = pltpu.VMEM((HALF * SIZE * 8, 128), F32)


def call(kernel, name, out, scalars, arrays, scratch=(), flops=10**6, moved=10**6):
    vmem = pl.BlockSpec(memory_space=pltpu.VMEM)
    many = isinstance(out, tuple)
    return pl.pallas_call(
        kernel,
        out_shape=out,
        in_specs=[SMEM] * len(scalars) + [vmem] * len(arrays),
        out_specs=[vmem] * len(out) if many else vmem,
        scratch_shapes=scratch,
        compiler_params=pltpu.CompilerParams(vmem_limit_bytes=VMEM_LIMIT),
        cost_estimate=pl.CostEstimate(flops=flops, bytes_accessed=moved, transcendentals=0),
        name=name,
    )(*scalars, *arrays)


def exchange(strips):
    n = lax.axis_size("tiles")
    got = {0: strips[0]}
    for off, strip in zip(OFFSETS[1:], strips[1:]):
        got[-off] = lax.ppermute(strip, "tiles", [(i, (i + off) % n) for i in range(n)])
    return tuple(got[off] for off in OFFSETS)


def body(fields, neighbours, kernel, gain, w_in, w_out, cotangent):
    n_tiles, n_dp = lax.axis_size("tiles"), lax.axis_size("dp")
    slots = 2 * n_tiles
    scalars = (lax.axis_index("tiles").reshape(1).astype(jnp.int32), neighbours)
    taps = kernel.reshape(TAPS, CH)
    tiles, cot = fields[0], cotangent[0]
    stage = pltpu.VMEM((2, SIZE * 16, 128), F32)
    sent = call(functools.partial(rim_kernel, slots=slots), "rims", STRIPS, scalars, (tiles,), (RIMS, stage))
    grid = call(grid_kernel, "grid", GRID, (), (tiles,), moved=5 * 10**6)
    got = exchange(sent)
    outs = (jax.ShapeDtypeStruct((16, CH, 128), BF16), GRID, *STRIPS, jax.ShapeDtypeStruct((8, CH), F32), GRID)
    weights, grad_grid, *rest = call(
        functools.partial(main_kernel, slots=slots),
        "main",
        outs,
        scalars,
        (*got, taps, gain.reshape(1, CH), w_in, w_out, cot.reshape(-1, CH), grid),
        (NEAR, SPREAD, CONV, pltpu.VMEM((CH, FF), F32), pltpu.VMEM((CH, FF), F32), RIMS),
        flops=20 * 10**9,
    )
    sent, ggain, grid = rest[:5], rest[5], rest[6]
    weights = lax.all_to_all(weights, "dp", 0, 0, tiled=True)
    small = call(
        taps_kernel,
        "taps",
        jax.ShapeDtypeStruct((16, 128, 128), BF16),
        (),
        (grid, grad_grid, ggain),
        (pltpu.VMEM((TAPS, 8, 128), F32),),
        flops=8 * 10**9,
    )
    small = lax.all_to_all(small, "dp", 0, 0, tiled=True)
    got = exchange(sent)
    grad_fields = call(
        functools.partial(back_kernel, slots=slots),
        "back",
        jax.ShapeDtypeStruct((2, SIZE, SIZE, CH), BF16),
        scalars,
        (*got, taps, cot, grad_grid),
        (GRID_SPACE, NEAR, SPREAD, CONV),
        flops=8 * 10**9,
    )
    pieces = jax.ShapeDtypeStruct((32, 16, 128), BF16)
    stages = (pltpu.VMEM((128, 128), F32), pltpu.VMEM((32, 16, 128), F32))
    cut = call(first_sum_kernel, "sum_dp", pieces, (), (weights, small), stages)
    cut = lax.all_to_all(cut, "tiles", 0, 0, tiled=True)
    cut = call(second_sum_kernel, "sum_tiles", pieces, (), (cut,))
    cut = lax.all_to_all(cut, "tiles", 0, 0, tiled=True)
    scale = float((n_dp * slots * SIZE * SIZE) ** -0.5)
    g_in, g_out, g_taps, g_gain = call(
        functools.partial(last_kernel, scale=scale),
        "last",
        (
            jax.ShapeDtypeStruct((CH, 64), F32),
            jax.ShapeDtypeStruct((64, CH), F32),
            jax.ShapeDtypeStruct((TAPS, CH), F32),
            jax.ShapeDtypeStruct((1, CH), F32),
        ),
        (),
        (cut,),
        (stages[1], stages[0]),
    )
    return grad_fields[None], g_in, g_out, g_taps.reshape(KW, KW, CH), g_gain.reshape(CH)


def solution(mesh):
    return jax.shard_map(
        body,
        mesh=mesh,
        in_specs=(
            P("dp", "tiles", None, None, None),
            P("tiles", None),
            P(),
            P(),
            P(),
            P(),
            P("dp", "tiles", None, None, None),
        ),
        out_specs=(P("dp", "tiles", None, None, None), P(None, "dp"), P("dp", None), P(), P()),
        check_vma=False,
    )
```

time: 473 us -> 165 us (0.35)
  waiting for transfers between devices: 176 us -> 8.21 us
  other arithmetic: 89.1 us -> 0 us
  Pallas kernels: 0 us -> 71.7 us
  blocking collectives: 103 us -> 32.2 us
  matrix products: 35 us -> 0 us
  local copies, waits for them, and re-layouts: 30.3 us -> 7.46 us
  starting transfers between devices: 22.7 us -> 43.6 us
  between operations: 16 us -> 0.83 us
    psum x1 -> x0, waiting for transfers between devices: 166 us -> none  [body(): summed = lax.psum(combined, 'tiles')]
    psum x1 -> x0, blocking collectives: 103 us -> none  [body(): lax.psum((grad_kernel, gradient_by_gain), ('tiles', 'dp'))]
    pallas_call x0 -> x8, Pallas kernels: none -> 71.7 us  [call(): pl.pallas_call(kernel, out_shape=out, in_specs=[SMEM] * len(scalars) + [v...]
    reduce_sum x7 -> x0, other arithmetic: 41.3 us -> none  [the longest x1 19 us: body(): channel_mean = jnp.mean(convolved_state, axis=-1, keepdims=True)]
    dot_general x5 -> x0, matrix products: 35 us -> none  [the longest x1 19.9 us: body(): pre = jnp.dot(rows_n, w_in, preferred_element_type=jnp.float32)]
    all_to_all x0 -> x2, blocking collectives: none -> 32.2 us  [the longest x1 16.3 us: body(): weights = lax.all_to_all(weights, 'dp', 0, 0, tiled=True)]
    convert_element_type x2 -> x0, other arithmetic: 31 us -> none  [the longest x1 30.3 us: body(): grad_fields = (cotangent.astype(jnp.float32) + grad_x).astype(jnp.bfloat16)]
    all_to_all x0 -> x2, starting transfers between devices: none -> 20.9 us  [body(): cut = lax.all_to_all(cut, 'tiles', 0, 0, tiled=True)]
  transfers between devices with their start and end apart: 10 -> 10, of which waited for: 2 -> 2; matrix products, arithmetic and copies ran while one was open for 14% -> 1% of each run, Pallas kernels for 0% -> 12%
where the time goes in v1:
time: 165 us; the launch traced here: 164 us
  Pallas kernels  71.7 us (43%)
  starting transfers between devices  43.6 us (26%)
  blocking collectives  32.2 us (20%)
  waiting for transfers between devices  8.21 us (5%)
  local copies, waits for them, and re-layouts  7.46 us (5%)
    pallas_call x8, Pallas kernels, call(): pl.pallas_call(kernel, out_shape=out, in_specs=[SMEM] * len(scalars) + [v...  71.7 us
    ppermute x8, starting transfers between devices, exchange(): lax.ppermute(strip, 'tiles', [(i, (i + off) % n) for i in range(n)])  22.7 us
    all_to_all x2, starting transfers between devices, body(): cut = lax.all_to_all(cut, 'tiles', 0, 0, tiled=True)  20.9 us
    all_to_all x1, blocking collectives, body(): weights = lax.all_to_all(weights, 'dp', 0, 0, tiled=True)  16.3 us
    all_to_all x1, blocking collectives, body(): small = lax.all_to_all(small, 'dp', 0, 0, tiled=True)  16 us
    all_to_all x2, waiting for transfers between devices, body(): cut = lax.all_to_all(cut, 'tiles', 0, 0, tiled=True)  8.19 us
    unnamed x31, local copies, waits for them, and re-layouts  4.56 us
  transfers between devices with their start and end apart: 10, of which 2 were waited for; matrix products, arithmetic and copies ran while one was open for 1% of the time, Pallas kernels for 12%

profile of v1, /device:TPU:1, one launch (start us, length us, event | category | flops | bytes accessed | tf_op | source)
XLA Modules:
  0.0 164.0 jit_solution(13459274513489363549)
XLA Ops:
  0.6 2.3 %rims.1 = (bf16[2,3,32,256]{3,2,1,0:T(8,128)(2,1)}, bf16[4,3,32,256]{3,2,1,0:T(8,128)(2,1)}, bf16[4,3,32,256]{3,2,1,0:T(8,128)(2,1)}, bf16[3,3,32,256]{3,2,1,0:T(8,128)(2,1)}, bf16[3,3,32,256]{3,2,1,0:T(8,128)(2,1)}) custom-call(s32[1]{0:T(128)} %bitcast.own_ref, s32[2,8]{1,0:T(2,128)} %near_ids.5, bf16[2,32,32,256]{3,2,1,0:T(8,128)(2,1)} %bitcast.7), custom_call_target="tpu_custom_call" | custom-call | flops 1000000 | bytes 1000000 | tf_op jit(solution)/shard_map/rims/pallas_call | solution.py:349
  3.0 3.0 %collective-permute-start = (bf16[4,3,32,256]{3,2,1,0:T(8,128)(2,1)}, bf16[4,3,32,256]{3,2,1,0:T(8,128)(2,1)S(1)}, u32[]{:S(2)}, u32[]{:S(2)}) collective-permute-start(bf16[4,3,32,256]{3,2,1,0:T(8,128)(2,1)} %get-tuple-element.24), channel_id=1, source_target_pairs={{0,16},{16,32},{32,48},{48,64},{64,80},{80,96},{96,112},{112,128},... | collective-permute-start | bytes 589832 | tf_op jit(solution)/shard_map/ppermute | solution.py:365
  6.0 3.9 %collective-permute-start.1 = (bf16[4,3,32,256]{3,2,1,0:T(8,128)(2,1)}, bf16[4,3,32,256]{3,2,1,0:T(8,128)(2,1)S(1)}, u32[]{:S(2)}, u32[]{:S(2)}) collective-permute-start(bf16[4,3,32,256]{3,2,1,0:T(8,128)(2,1)} %get-tuple-element.25), channel_id=1, source_target_pairs={{0,496},{16,0},{32,16},{48,32},{64,48},{80,64},{96,80},{112,96},{1... | collective-permute-start | bytes 589832 | tf_op jit(solution)/shard_map/ppermute | solution.py:365
  9.9 1.9 %collective-permute-start.2 = (bf16[3,3,32,256]{3,2,1,0:T(8,128)(2,1)}, bf16[3,3,32,256]{3,2,1,0:T(8,128)(2,1)S(1)}, u32[]{:S(2)}, u32[]{:S(2)}) collective-permute-start(bf16[3,3,32,256]{3,2,1,0:T(8,128)(2,1)} %get-tuple-element.26), channel_id=1, source_target_pairs={{0,32},{16,48},{32,64},{48,80},{64,96},{80,112},{96,128},{112,144}... | collective-permute-start | bytes 442376 | tf_op jit(solution)/shard_map/ppermute | solution.py:365
  11.8 5.7 %collective-permute-start.3 = (bf16[3,3,32,256]{3,2,1,0:T(8,128)(2,1)}, bf16[3,3,32,256]{3,2,1,0:T(8,128)(2,1)S(1)}, u32[]{:S(2)}, u32[]{:S(2)}) collective-permute-start(bf16[3,3,32,256]{3,2,1,0:T(8,128)(2,1)} %get-tuple-element.27), channel_id=1, source_target_pairs={{0,480},{16,496},{32,0},{48,16},{64,32},{80,48},{96,64},{112,80},{... | collective-permute-start | bytes 442376 | tf_op jit(solution)/shard_map/ppermute | solution.py:365
  17.5 1.5 reshape.26.kernel_ref
  19.0 3.4 %grid.1.grid_in = f32[6688,128]{1,0:T(8,128)} custom-call(bf16[2,32,32,256]{3,2,1,0:T(8,128)(2,1)} %bitcast.8), custom_call_target="tpu_custom_call" | custom-call | flops 1000000 | bytes 5000000 | tf_op jit(solution)/shard_map/grid/pallas_call | solution.py:349
  22.5 0.6 copy-done.13
  23.1 0.1 copy-done.7
  23.2 0.1 copy-done.8
  23.3 35.0 %main.1 = (bf16[16,256,128]{2,1,0:T(8,128)(2,1)}, f32[6688,128]{1,0:T(8,128)}, bf16[2,3,32,256]{3,2,1,0:T(8,128)(2,1)}, bf16[4,3,32,256]{3,2,1,0:T(8,128)(2,1)},...) custom-call(s32[1]{0:T(128)} %bitcast.own_ref, ...), custom_call_target="tpu_custom_call" | custom-call | flops 20000000000 | bytes 1000000 | tf_op jit(solution)/shard_map/main/pallas_call | solution.py:349
  58.2 10.9 %taps.1 = bf16[16,128,128]{2,1,0:T(8,128)(2,1)} custom-call(f32[6688,128]{1,0:T(8,128)} %get-tuple-element.35.grid, f32[6688,128]{1,0:T(8,128)} %get-tuple-element.33.grid_in.grad_grid, f32[8,256]{1,0:T(8,128)} %get-tuple-element.36.ggain_ref), custom_call_target="tpu_custom_call" | custom-call | flops 8000000000 | bytes 1000000 | tf_op jit(solution)/shard_map/taps/pallas_call | solution.py:349
  69.2 16.0 %all_to_all.20.k_ref = bf16[16,128,128]{2,1,0:T(8,128)(2,1)} all-to-all(bf16[16,128,128]{2,1,0:T(8,128)(2,1)} %taps.1), channel_id=1, replica_groups=mesh['tiles'=32,'dp'=16] {'dp'}, dimensions={0} | all-to-all | bytes 1048576 | tf_op jit(solution)/shard_map/all_to_all | solution.py:400
  85.2 16.3 %all_to_all.21.w_ref = bf16[16,256,128]{2,1,0:T(8,128)(2,1)} all-to-all(bf16[16,256,128]{2,1,0:T(8,128)(2,1)S(1)} %copy-done), channel_id=1, replica_groups=mesh['tiles'=32,'dp'=16] {'dp'}, dimensions={0} | all-to-all | bytes 2097152 | tf_op jit(solution)/shard_map/all_to_all | solution.py:390
  101.4 2.3 %sum_dp.1 = bf16[32,16,128]{2,1,0:T(8,128)(2,1)} custom-call(bf16[16,256,128]{2,1,0:T(8,128)(2,1)} %all_to_all.21.w_ref, bf16[16,128,128]{2,1,0:T(8,128)(2,1)} %all_to_all.20.k_ref), custom_call_target="tpu_custom_call" | custom-call | flops 1000000 | bytes 1000000 | tf_op jit(solution)/shard_map/sum_dp/pallas_call | solution.py:349
  103.7 14.5 %all-to-all-start.2 = ((bf16[32,16,128]{2,1,0:T(8,128)(2,1)}), bf16[32,16,128]{2,1,0:T(8,128)(2,1)S(1)}, u32[]{:S(2)}, u32[]{:S(2)}) async-start(bf16[32,16,128]{2,1,0:T(8,128)(2,1)} %sum_dp.1), calls=%async_computation.2 | async-start | bytes 262144 | tf_op jit(solution)/shard_map/all_to_all | solution.py:414
  118.3 1.6 %collective-permute-start.4 = (bf16[4,3,32,256]{3,2,1,0:T(8,128)(2,1)S(1)}, bf16[4,3,32,256]{3,2,1,0:T(8,128)(2,1)S(1)}, u32[]{:S(2)}, u32[]{:S(2)}) collective-permute-start(bf16[4,3,32,256]{3,2,1,0:T(8,128)(2,1)S(1)} %copy-done.4), channel_id=1, source_target_pairs={{0,16},{16,32},{32,48},{48,64},{64,80},{80,96},{96,112},{112,128},... | collective-permute-start | bytes 589832 | tf_op jit(solution)/shard_map/ppermute | solution.py:365
  119.9 3.1 %collective-permute-start.6 = (bf16[3,3,32,256]{3,2,1,0:T(8,128)(2,1)S(1)}, bf16[3,3,32,256]{3,2,1,0:T(8,128)(2,1)S(1)}, u32[]{:S(2)}, u32[]{:S(2)}) collective-permute-start(bf16[3,3,32,256]{3,2,1,0:T(8,128)(2,1)S(1)} %copy-done.10), channel_id=1, source_target_pairs={{0,32},{16,48},{32,64},{48,80},{64,96},{80,112},{96,128},{112,144}... | collective-permute-start | bytes 442376 | tf_op jit(solution)/shard_map/ppermute | solution.py:365
  123.1 3.4 %collective-permute-start.7 = (bf16[3,3,32,256]{3,2,1,0:T(8,128)(2,1)S(1)}, bf16[3,3,32,256]{3,2,1,0:T(8,128)(2,1)S(1)}, u32[]{:S(2)}, u32[]{:S(2)}) collective-permute-start(bf16[3,3,32,256]{3,2,1,0:T(8,128)(2,1)S(1)} %copy-done.9), channel_id=1, source_target_pairs={{0,480},{16,496},{32,0},{48,16},{64,32},{80,48},{96,64},{112,80},{... | collective-permute-start | bytes 442376 | tf_op jit(solution)/shard_map/ppermute | solution.py:365
  126.5 7.7 %all-to-all-done.2.in_ref = bf16[32,16,128]{2,1,0:T(8,128)(2,1)S(1)} async-done(((bf16[32,16,128]{2,1,0:T(8,128)(2,1)}), bf16[32,16,128]{2,1,0:T(8,128)(2,1)S(1)}, u32[]{:S(2)}, u32[]{:S(2)}) %all-to-all-start.2) | async-done | bytes 131104 | tf_op jit(solution)/shard_map/all_to_all | solution.py:414
  134.1 0.7 copy-done.2
  134.8 1.6 sum_tiles.1
  136.4 6.4 %all-to-all-start.3 = ((bf16[32,16,128]{2,1,0:T(8,128)(2,1)}), bf16[32,16,128]{2,1,0:T(8,128)(2,1)S(1)}, u32[]{:S(2)}, u32[]{:S(2)}) async-start(bf16[32,16,128]{2,1,0:T(8,128)(2,1)} %sum_tiles.1), calls=%async_computation.3 | async-start | bytes 262144 | tf_op jit(solution)/shard_map/all_to_all | solution.py:416
  142.9 0.6 copy-done.11
  143.5 0.1 copy-done.5
  143.6 0.1 copy-done.6
  143.7 14.5 %back.1 = bf16[2,32,32,256]{3,2,1,0:T(8,128)(2,1)} custom-call(s32[1]{0:T(128)} %bitcast.own_ref, s32[2,8]{1,0:T(2,128)} %near_ids.5, bf16[2,3,32,256]{3,2,1,0:T(8,128)(2,1)} %get-tuple-element.28.s0, bf16[4,3,32,256]{3,2,1,0:T(8,128)(2,1)} %copy-done.5, bf16[4,3,32,256]{3,2,1,0:T(8,128)(2,1)} %copy-done.6, bf16[3,3,32,256]{3,2,1,0:T(8,128)(2,1)} %copy-done.11, ...), custom_call_target="tpu_custom_call" | custom-call | flops 8000000000 | bytes 1000000 | tf_op jit(solution)/shard_map/back/pallas_call | solution.py:349
  158.1 0.5 all-to-all-done.3.in_ref
  158.6 0.6 copy-done.1
  159.3 1.7 %last.1 = (f32[256,64]{1,0:T(8,128)}, f32[64,256]{1,0:T(8,128)}, f32[49,256]{1,0:T(8,128)}, f32[1,256]{1,0:T(1,128)}) custom-call(bf16[32,16,128]{2,1,0:T(8,128)(2,1)} %copy-done.1), custom_call_target="tpu_custom_call" | custom-call | flops 1000000 | bytes 1000000 | tf_op jit(solution)/shard_map/last/pallas_call | solution.py:349
  160.9 1.6 copy.12
  162.6 1.4 reshape.28
  (31 shorter events, 0.2 us)
Async XLA Ops:
  3.0 19.4 %collective-permute-start = (bf16[4,3,32,256]{3,2,1,0:T(8,128)(2,1)}, bf16[4,3,32,256]{3,2,1,0:T(8,128)(2,1)S(1)}, u32[]{:S(2)}, u32[]{:S(2)}) collective-permute-start(bf16[4,3,32,256]{3,2,1,0:T(8,128)(2,1)} %get-tuple-element.24), channel_id=1, source_target_pairs={{0,16},{16,32},{32,48},{48,64},{64,80},{80,96},{96,112},{112,128},... | collective-permute-start | bytes 589832 | tf_op jit(solution)/shard_map/ppermute | solution.py:365
  6.0 16.4 %collective-permute-start.1 = (bf16[4,3,32,256]{3,2,1,0:T(8,128)(2,1)}, bf16[4,3,32,256]{3,2,1,0:T(8,128)(2,1)S(1)}, u32[]{:S(2)}, u32[]{:S(2)}) collective-permute-start(bf16[4,3,32,256]{3,2,1,0:T(8,128)(2,1)} %get-tuple-element.25), channel_id=1, source_target_pairs={{0,496},{16,0},{32,16},{48,32},{64,48},{80,64},{96,80},{112,96},{1... | collective-permute-start | bytes 589832 | tf_op jit(solution)/shard_map/ppermute | solution.py:365
  9.9 12.5 %collective-permute-start.2 = (bf16[3,3,32,256]{3,2,1,0:T(8,128)(2,1)}, bf16[3,3,32,256]{3,2,1,0:T(8,128)(2,1)S(1)}, u32[]{:S(2)}, u32[]{:S(2)}) collective-permute-start(bf16[3,3,32,256]{3,2,1,0:T(8,128)(2,1)} %get-tuple-element.26), channel_id=1, source_target_pairs={{0,32},{16,48},{32,64},{48,80},{64,96},{80,112},{96,128},{112,144}... | collective-permute-start | bytes 442376 | tf_op jit(solution)/shard_map/ppermute | solution.py:365
  11.8 10.6 %collective-permute-start.3 = (bf16[3,3,32,256]{3,2,1,0:T(8,128)(2,1)}, bf16[3,3,32,256]{3,2,1,0:T(8,128)(2,1)S(1)}, u32[]{:S(2)}, u32[]{:S(2)}) collective-permute-start(bf16[3,3,32,256]{3,2,1,0:T(8,128)(2,1)} %get-tuple-element.27), channel_id=1, source_target_pairs={{0,480},{16,496},{32,0},{48,16},{64,32},{80,48},{96,64},{112,80},{... | collective-permute-start | bytes 442376 | tf_op jit(solution)/shard_map/ppermute | solution.py:365
  22.4 0.7 copy-start.13
  22.4 0.7 copy-start.14
  22.4 0.8 copy-start.7
  22.4 0.8 copy-start.8
  58.2 26.9 %copy-start = (bf16[16,256,128]{2,1,0:T(8,128)(2,1)S(1)}, bf16[16,256,128]{2,1,0:T(8,128)(2,1)}, u32[]{:S(2)}) copy-start(bf16[16,256,128]{2,1,0:T(8,128)(2,1)} %get-tuple-element.34) | copy-start | bytes 3145732
  69.2 49.1 %copy-start.4 = (bf16[4,3,32,256]{3,2,1,0:T(8,128)(2,1)S(1)}, bf16[4,3,32,256]{3,2,1,0:T(8,128)(2,1)}, u32[]{:S(2)}) copy-start(bf16[4,3,32,256]{3,2,1,0:T(8,128)(2,1)} %get-tuple-element.29) | copy-start | bytes 589828
  69.2 50.8 %copy-start.3 = (bf16[4,3,32,256]{3,2,1,0:T(8,128)(2,1)S(1)}, bf16[4,3,32,256]{3,2,1,0:T(8,128)(2,1)}, u32[]{:S(2)}) copy-start(bf16[4,3,32,256]{3,2,1,0:T(8,128)(2,1)} %get-tuple-element.30) | copy-start | bytes 589828
  69.2 50.8 %copy-start.10 = (bf16[3,3,32,256]{3,2,1,0:T(8,128)(2,1)S(1)}, bf16[3,3,32,256]{3,2,1,0:T(8,128)(2,1)}, u32[]{:S(2)}) copy-start(bf16[3,3,32,256]{3,2,1,0:T(8,128)(2,1)} %get-tuple-element.31) | copy-start | bytes 442372
  69.2 53.9 %copy-start.9 = (bf16[3,3,32,256]{3,2,1,0:T(8,128)(2,1)S(1)}, bf16[3,3,32,256]{3,2,1,0:T(8,128)(2,1)}, u32[]{:S(2)}) copy-start(bf16[3,3,32,256]{3,2,1,0:T(8,128)(2,1)} %get-tuple-element.32) | copy-start | bytes 442372
  103.7 30.4 %all-to-all-start.2 = ((bf16[32,16,128]{2,1,0:T(8,128)(2,1)}), bf16[32,16,128]{2,1,0:T(8,128)(2,1)S(1)}, u32[]{:S(2)}, u32[]{:S(2)}) async-start(bf16[32,16,128]{2,1,0:T(8,128)(2,1)} %sum_dp.1), calls=%async_computation.2 | async-start | bytes 262144 | tf_op jit(solution)/shard_map/all_to_all | solution.py:414
  118.3 24.5 %collective-permute-start.4 = (bf16[4,3,32,256]{3,2,1,0:T(8,128)(2,1)S(1)}, bf16[4,3,32,256]{3,2,1,0:T(8,128)(2,1)S(1)}, u32[]{:S(2)}, u32[]{:S(2)}) collective-permute-start(bf16[4,3,32,256]{3,2,1,0:T(8,128)(2,1)S(1)} %copy-done.4), channel_id=1, source_target_pairs={{0,16},{16,32},{32,48},{48,64},{64,80},{80,96},{96,112},{112,128},... | collective-permute-start | bytes 589832 | tf_op jit(solution)/shard_map/ppermute | solution.py:365
  119.9 22.9 %collective-permute-start.5 = (bf16[4,3,32,256]{3,2,1,0:T(8,128)(2,1)S(1)}, bf16[4,3,32,256]{3,2,1,0:T(8,128)(2,1)S(1)}, u32[]{:S(2)}, u32[]{:S(2)}) collective-permute-start(bf16[4,3,32,256]{3,2,1,0:T(8,128)(2,1)S(1)} %copy-done.3), channel_id=1, source_target_pairs={{0,496},{16,0},{32,16},{48,32},{64,48},{80,64},{96,80},{112,96},{1... | collective-permute-start | bytes 589832 | tf_op jit(solution)/shard_map/ppermute | solution.py:365
  119.9 22.8 %collective-permute-start.6 = (bf16[3,3,32,256]{3,2,1,0:T(8,128)(2,1)S(1)}, bf16[3,3,32,256]{3,2,1,0:T(8,128)(2,1)S(1)}, u32[]{:S(2)}, u32[]{:S(2)}) collective-permute-start(bf16[3,3,32,256]{3,2,1,0:T(8,128)(2,1)S(1)} %copy-done.10), channel_id=1, source_target_pairs={{0,32},{16,48},{32,64},{48,80},{64,96},{80,112},{96,128},{112,144}... | collective-permute-start | bytes 442376 | tf_op jit(solution)/shard_map/ppermute | solution.py:365
  123.1 19.8 %collective-permute-start.7 = (bf16[3,3,32,256]{3,2,1,0:T(8,128)(2,1)S(1)}, bf16[3,3,32,256]{3,2,1,0:T(8,128)(2,1)S(1)}, u32[]{:S(2)}, u32[]{:S(2)}) collective-permute-start(bf16[3,3,32,256]{3,2,1,0:T(8,128)(2,1)S(1)} %copy-done.9), channel_id=1, source_target_pairs={{0,480},{16,496},{32,0},{48,16},{64,32},{80,48},{96,64},{112,80},{... | collective-permute-start | bytes 442376 | tf_op jit(solution)/shard_map/ppermute | solution.py:365
  134.1 0.7 copy-start.2
  136.4 22.2 %all-to-all-start.3 = ((bf16[32,16,128]{2,1,0:T(8,128)(2,1)}), bf16[32,16,128]{2,1,0:T(8,128)(2,1)S(1)}, u32[]{:S(2)}, u32[]{:S(2)}) async-start(bf16[32,16,128]{2,1,0:T(8,128)(2,1)} %sum_tiles.1), calls=%async_computation.3 | async-start | bytes 262144 | tf_op jit(solution)/shard_map/all_to_all | solution.py:416
  142.8 0.6 copy-start.11
  142.8 0.7 copy-start.12
  142.8 0.7 copy-start.5
  142.9 0.8 copy-start.6
  158.6 0.7 copy-start.1

commit v2 on v1

--- a/solution.py
+++ b/solution.py
@@ -16,8 +16,8 @@
 TALL = HALF + 2 * RIM
 CH = 256
 FF = 1024
+PART_ROWS = 56
 ROWS = 256
-VMEM_LIMIT = 56 * 1024 * 1024
 F32 = jnp.float32
 BF16 = jnp.bfloat16
 OFFSETS = (0, -1, 1, -2, 2)
@@ -112,23 +112,21 @@
 
 def spread_taps(kernel_ref, taps):
     even = lax.rem(lax.broadcasted_iota(jnp.int32, (8, 128), 0), 2) == 0
-    for q in range(TAPS):
-        low = jnp.broadcast_to(kernel_ref[q : q + 1, 0:128], (8, 128))
-        high = jnp.broadcast_to(kernel_ref[q : q + 1, 128:256], (8, 128))
-        taps[q] = jnp.where(even, low, high)
+    for a in range(KW):
+        for b in range(KW):
+            low = jnp.broadcast_to(kernel_ref[a, b : b + 1, 0:128], (8, 128))
+            high = jnp.broadcast_to(kernel_ref[a, b : b + 1, 128:256], (8, 128))
+            taps[a * KW + b] = jnp.where(even, low, high)
 
 
 def convolve(grid3, taps, flip, out3):
     def column(j, carry):
         acc = [None] * HALF
-        for b in range(KW):
-            cells = [grid3[i * WIDE + j + b] for i in range(TALL)]
-            for a in range(KW):
-                q = a * KW + b
-                tap = taps[TAPS - 1 - q if flip else q]
-                for r in range(HALF):
-                    term = cells[r + a] * tap
-                    acc[r] = term if acc[r] is None else acc[r] + term
+        for q in range(TAPS):
+            tap = taps[TAPS - 1 - q if flip else q]
+            for r in range(HALF):
+                term = grid3[(r + q // KW) * WIDE + j + q % KW] * tap
+                acc[r] = term if acc[r] is None else acc[r] + term
         for r in range(HALF):
             out3[r * SIZE + j] = acc[r]
         return carry
@@ -174,24 +172,34 @@
             put_row(grid, WIDE, t, RIM + i, RIM, tile_ref[t, i].astype(F32))
 
 
-def main_kernel(own_ref, near_ids, s0, s1, s2, s3, s4, kernel_ref, gain_ref, w_in_ref, w_out_ref, cot_ref, grid_in,
-                gw_ref, grad_grid, o0, o1, o2, o3, o4, ggain_ref, grid,
-                near, taps, conv, gwi, gwo, rims, *, slots):
+def main_kernel(own_ref, near_ids, s0, s1, s2, s3, s4, kernel_ref, gain_ref, w_in_hbm, w_out_hbm, cot_hbm, grid_hbm,
+                share_ref, grad_grid, o0, o1, o2, o3, o4,
+                grid, near, taps, conv, gwi, gwo, rims, normed_ref, xhat_ref, inv_ref, gn_ref,
+                cot_ref, w_in_ref, w_out_ref, acc, sems, *, slots):
     own = own_ref[0]
-    grid[...] = grid_in[...]
+    copies = [
+        pltpu.make_async_copy(src, dst, sems.at[k])
+        for k, (src, dst) in enumerate(
+            ((grid_hbm, grid), (w_in_hbm, w_in_ref), (w_out_hbm, w_out_ref), (cot_hbm, cot_ref))
+        )
+    ]
+    for copy in copies:
+        copy.start()
     fetch_strips(near_ids, own, slots, (s0, s1, s2, s3, s4), near)
+    spread_taps(kernel_ref, taps)
+    copies[0].wait()
     put_halo(near, grid)
-    spread_taps(kernel_ref, taps)
-    convolve(grid.reshape(TALL * WIDE, 8, 128), taps, False, conv.reshape(HALF * SIZE, 8, 128))
-    gwi[...] = jnp.zeros_like(gwi)
-    gwo[...] = jnp.zeros_like(gwo)
-    ggain_ref[...] = jnp.zeros_like(ggain_ref)
+    grid3 = grid.reshape(TALL * WIDE, 8, 128)
+    convolve(grid3, taps, False, conv.reshape(HALF * SIZE, 8, 128))
     gain = gain_ref[...]
     lines = ROWS // SIZE
 
-    def chunk(n, carry):
-        tile, half, first = n // 4, (n // 2) % 2, (n % 2) * lines
-        spot = place(half, tile, 0)
+    def where(n):
+        return (n % 2) * lines, place((n // 2) % 2, n // 4, 0)
+
+    def normalise(n, carry):
+        first, spot = where(n)
+        cells = pl.ds(pl.multiple_of(n * ROWS, ROWS), ROWS)
         cv = jnp.concatenate(
             [
                 jnp.concatenate(
@@ -201,26 +209,57 @@
             ],
             axis=0,
         )
-        mean = jnp.mean(cv, axis=-1, keepdims=True)
-        cv = cv - mean
+        cv = cv - jnp.mean(cv, axis=-1, keepdims=True)
         inv = lax.rsqrt(jnp.mean(cv * cv, axis=-1, keepdims=True) + 1e-06)
         xhat = cv * inv
-        normed = (xhat * gain).astype(BF16)
-        cot = cot_ref[pl.ds(pl.multiple_of(n * ROWS, ROWS), ROWS), :]
-        normed_t = normed.T
-        cot_t = cot.T
-        gn = jnp.zeros((ROWS, CH), F32)
-        for f in range(FF // 256):
-            cols = slice(f * 256, f * 256 + 256)
-            pre = jnp.dot(normed, w_in_ref[:, cols], preferred_element_type=F32)
-            gact = lax.dot_general(cot, w_out_ref[cols, :], (((1,), (1,)), ((), ())), preferred_element_type=F32)
-            act, slope = gelu_parts(pre)
-            act = act.astype(BF16)
-            gpre = (gact * slope).astype(BF16)
-            gwi[:, cols] += jnp.dot(normed_t, gpre, preferred_element_type=F32)
-            gwo[:, cols] += jnp.dot(cot_t, act, preferred_element_type=F32)
-            gn += lax.dot_general(gpre, w_in_ref[:, cols], (((1,), (1,)), ((), ())), preferred_element_type=F32)
-        ggain_ref[...] += jnp.sum((gn * xhat).reshape(ROWS // 8, 8, CH), axis=0)
+        xhat_ref[cells, :] = xhat
+        inv_ref[cells, :] = jnp.broadcast_to(inv, (ROWS, 128))
+        normed_ref[cells, :] = (xhat * gain).astype(BF16)
+        return carry
+
+    lax.fori_loop(0, 2 * SIZE * SIZE // ROWS, normalise, 0)
+    for copy in copies[1:]:
+        copy.wait()
+    steps = [(t, slice(f * 256, f * 256 + 256)) for t in range(2) for f in range(FF // 256)]
+    cells_of = [slice(t * SIZE * SIZE, (t + 1) * SIZE * SIZE) for t in range(2)]
+    across = (((1,), (1,)), ((), ()))
+
+    def forward(step):
+        t, cols = step
+        pre = jnp.dot(normed_ref[cells_of[t], :], w_in_ref[:, cols], preferred_element_type=F32)
+        return pre, lax.dot_general(cot_ref[cells_of[t], :], w_out_ref[cols, :], across, preferred_element_type=F32)
+
+    ahead = forward(steps[0])
+    for k, (t, cols) in enumerate(steps):
+        pre, gact = ahead
+        if k + 1 < len(steps):
+            ahead = forward(steps[k + 1])
+        if cols.start == 0:
+            normed_t = normed_ref[cells_of[t], :].T
+            cot_t = cot_ref[cells_of[t], :].T
+        act, slope = gelu_parts(pre)
+        act = act.astype(BF16)
+        gpre = (gact * slope).astype(BF16)
+        one = jnp.dot(normed_t, gpre, preferred_element_type=F32)
+        two = jnp.dot(cot_t, act, preferred_element_type=F32)
+        gn = lax.dot_general(gpre, w_in_ref[:, cols], across, preferred_element_type=F32)
+        if t == 0:
+            gwi[:, cols] = one
+            gwo[:, cols] = two
+        else:
+            gwi[:, cols] += one
+            gwo[:, cols] += two
+        if cols.start == 0:
+            gn_ref[cells_of[t], :] = gn
+        else:
+            gn_ref[cells_of[t], :] += gn
+
+    def denormalise(n, ggain):
+        first, spot = where(n)
+        cells = pl.ds(pl.multiple_of(n * ROWS, ROWS), ROWS)
+        gn, xhat = gn_ref[cells, :], xhat_ref[cells, :]
+        inv = inv_ref[cells, 0:1]
+        ggain = ggain + jnp.sum((gn * xhat).reshape(ROWS // 8, 8, CH), axis=0)
         gx = gn * gain
         m1 = jnp.mean(gx, axis=-1, keepdims=True)
         m2 = jnp.mean(gx * xhat, axis=-1, keepdims=True)
@@ -230,15 +269,16 @@
             at = ((first + r + RIM) * WIDE + RIM) * 8 + spot
             for part in range(2):
                 grad_grid[pl.ds(at + part, SIZE, stride=8), :] = piece[:, lanes_of(part)]
-        return carry
-
-    lax.fori_loop(0, 2 * SIZE * SIZE // ROWS, chunk, 0)
+        return ggain
+
+    ggain = lax.fori_loop(0, 2 * SIZE * SIZE // ROWS, denormalise, jnp.zeros((8, CH), F32))
     low = lax.broadcasted_iota(jnp.int32, (CH, 128), 1) < 64
     for p in range(FF // 128):
         one = gwi[:, p * 128 : p * 128 + 128]
         two = gwo[:, p * 128 : p * 128 + 128]
-        gw_ref[2 * p] = jnp.where(low, one, pltpu.roll(two, 64, 1)).astype(BF16)
-        gw_ref[2 * p + 1] = jnp.where(low, pltpu.roll(one, 64, 1), two).astype(BF16)
+        share_ref[2 * p, 0:CH] = jnp.where(low, one, pltpu.roll(two, 64, 1)).astype(BF16)
+        share_ref[2 * p + 1, 0:CH] = jnp.where(low, pltpu.roll(one, 64, 1), two).astype(BF16)
+    tap_gradients(grid3, grad_grid.reshape(TALL * WIDE, 8, 128), ggain, acc, share_ref)
     for t in range(2):
         for part in range(2):
             for r in range(RIM):
@@ -261,56 +301,54 @@
     send_strips(near_ids, own, slots, rims, (o0, o1, o2, o3, o4))
 
 
-def taps_kernel(grid, grad_grid, ggain_ref, out_ref, acc):
-    grid3 = grid.reshape(TALL * WIDE, 8, 128)
-    grad3 = grad_grid.reshape(TALL * WIDE, 8, 128)
+def tap_gradients(grid3, grad3, ggain, acc, share_ref):
     acc[...] = jnp.zeros_like(acc)
 
     def column(j, carry):
         g = [grad3[(RIM + r) * WIDE + RIM + j] for r in range(HALF)]
-        for b in range(KW):
-            cells = [grid3[i * WIDE + j + b] for i in range(TALL)]
-            for a in range(KW):
-                terms = [cells[r + a] * g[r] for r in range(HALF)]
-                while len(terms) > 1:
-                    terms = [terms[k] + terms[k + 1] for k in range(0, len(terms), 2)]
-                acc[a * KW + b] += terms[0]
+        for q in range(TAPS):
+            terms = [grid3[(r + q // KW) * WIDE + j + q % KW] * g[r] for r in range(HALF)]
+            while len(terms) > 1:
+                terms = [terms[k] + terms[k + 1] for k in range(0, len(terms), 2)]
+            acc[q] += terms[0]
         return carry
 
     lax.fori_loop(0, SIZE, column, 0)
-    sub = lax.broadcasted_iota(jnp.int32, (8, 128), 0)
-    even = lax.rem(sub, 2) == 0
+    even = lax.rem(lax.broadcasted_iota(jnp.int32, (8, 128), 0), 2) == 0
     sums = [[], []]
     for q in range(TAPS):
         one = acc[q]
         sums[0].append(jnp.sum(jnp.where(even, one, 0.0), axis=0, keepdims=True))
         sums[1].append(jnp.sum(jnp.where(even, 0.0, one), axis=0, keepdims=True))
     for part in range(2):
-        sums[part].append(jnp.sum(ggain_ref[:, lanes_of(part)], axis=0, keepdims=True))
-        sums[part].append(jnp.zeros((64 - TAPS - 1, 128), F32))
+        sums[part].append(jnp.sum(ggain[:, lanes_of(part)], axis=0, keepdims=True))
+        sums[part].append(jnp.zeros((PART_ROWS - TAPS - 1, 128), F32))
     total = jnp.concatenate(sums[0] + sums[1], axis=0).astype(BF16)
     for d in range(16):
-        out_ref[d] = total
-
-
-def back_kernel(own_ref, near_ids, s0, s1, s2, s3, s4, kernel_ref, cot_ref, grid_in, out_ref, grid, near, taps, conv, *, slots):
-    grid[...] = grid_in[...]
+        share_ref[d, CH : CH + 2 * PART_ROWS] = total
+
+
+def back_kernel(own_ref, near_ids, s0, s1, s2, s3, s4, kernel_ref, cot_ref, grid_hbm, out_ref, grid, near, taps, conv, sem, *, slots):
+    copy = pltpu.make_async_copy(grid_hbm, grid, sem)
+    copy.start()
     fetch_strips(near_ids, own_ref[0], slots, (s0, s1, s2, s3, s4), near)
+    spread_taps(kernel_ref, taps)
+    copy.wait()
     put_halo(near, grid)
-    spread_taps(kernel_ref, taps)
     convolve(grid.reshape(TALL * WIDE, 8, 128), taps, True, conv.reshape(HALF * SIZE, 8, 128))
     for t in range(2):
         for i in range(SIZE):
             out_ref[t, i] = (cot_ref[t, i].astype(F32) + rows_of(conv, t, i // HALF, i % HALF)).astype(BF16)
 
 
-def first_sum_kernel(w_ref, k_ref, out_ref, low, stage):
-    low[...] = jnp.sum(k_ref[...].astype(F32), axis=0)
-    weights = jnp.sum(w_ref[...].astype(F32), axis=0)
+def first_sum_kernel(in_ref, out_ref, stage):
+    weights = jnp.sum(in_ref[:, 0:CH, :].astype(F32), axis=0)
+    small = jnp.sum(in_ref[:, CH : CH + 2 * PART_ROWS, :].astype(F32), axis=0)
     stage[...] = jnp.zeros_like(stage)
     for p in range(32):
         stage[p, 0:8, :] = weights[8 * p : 8 * p + 8]
-        stage[p, 8:12, :] = low[4 * p : 4 * p + 4, :]
+        if 4 * p < 2 * PART_ROWS:
+            stage[p, 8:12, :] = small[4 * p : 4 * p + 4]
     out_ref[...] = stage[...].astype(BF16)
 
 
@@ -322,15 +360,18 @@
 
 def last_kernel(in_ref, w_in_ref, w_out_ref, taps_ref, gain_ref, stage, low, *, scale):
     stage[...] = in_ref[...].astype(F32) * scale
-    weights = stage[:, 0:8, :].reshape(CH, 128)
-    w_in_ref[...] = weights[:, 0:64]
-    w_out_ref[...] = weights.T[64:128, :]
-    for p in range(32):
+    weights = stage[:, 0:8, :].reshape(CH, 128).T
+    w_in_ref[...] = weights[0:64, :]
+    w_out_ref[...] = weights[64:128, :]
+    for p in range(PART_ROWS // 2):
         low[4 * p : 4 * p + 4, :] = stage[p, 8:12, :]
     for part in range(2):
         lanes = lanes_of(part)
-        taps_ref[:, lanes] = low[64 * part : 64 * part + TAPS, :]
-        gain_ref[:, lanes] = low[64 * part + TAPS : 64 * part + TAPS + 1, :]
+        for a in range(KW):
+            at = part * PART_ROWS + a * KW
+            taps_ref[a, :, lanes] = low[at : at + KW, :]
+        at = part * PART_ROWS + TAPS
+        gain_ref[:, lanes] = low[at : at + 1, :]
 
 
 SMEM = pl.BlockSpec(memory_space=pltpu.SMEM)
@@ -343,19 +384,19 @@
 CONV = pltpu.VMEM((HALF * SIZE * 8, 128), F32)
 
 
-def call(kernel, name, out, scalars, arrays, scratch=(), flops=10**6, moved=10**6):
+def call(kernel, name, out, scalars, arrays, scratch=(), far=(), flops=10**6, moved=10**6, vmem_mib=24):
     vmem = pl.BlockSpec(memory_space=pltpu.VMEM)
-    many = isinstance(out, tuple)
+    anywhere = pl.BlockSpec(memory_space=pl.ANY)
     return pl.pallas_call(
         kernel,
         out_shape=out,
-        in_specs=[SMEM] * len(scalars) + [vmem] * len(arrays),
-        out_specs=[vmem] * len(out) if many else vmem,
+        in_specs=[SMEM] * len(scalars) + [vmem] * len(arrays) + [anywhere] * len(far),
+        out_specs=[vmem] * len(out) if isinstance(out, tuple) else vmem,
         scratch_shapes=scratch,
-        compiler_params=pltpu.CompilerParams(vmem_limit_bytes=VMEM_LIMIT),
+        compiler_params=pltpu.CompilerParams(vmem_limit_bytes=vmem_mib * 1024 * 1024),
         cost_estimate=pl.CostEstimate(flops=flops, bytes_accessed=moved, transcendentals=0),
         name=name,
-    )(*scalars, *arrays)
+    )(*scalars, *arrays, *far)
 
 
 def exchange(strips):
@@ -370,47 +411,43 @@
     n_tiles, n_dp = lax.axis_size("tiles"), lax.axis_size("dp")
     slots = 2 * n_tiles
     scalars = (lax.axis_index("tiles").reshape(1).astype(jnp.int32), neighbours)
-    taps = kernel.reshape(TAPS, CH)
     tiles, cot = fields[0], cotangent[0]
     stage = pltpu.VMEM((2, SIZE * 16, 128), F32)
     sent = call(functools.partial(rim_kernel, slots=slots), "rims", STRIPS, scalars, (tiles,), (RIMS, stage))
     grid = call(grid_kernel, "grid", GRID, (), (tiles,), moved=5 * 10**6)
     got = exchange(sent)
-    outs = (jax.ShapeDtypeStruct((16, CH, 128), BF16), GRID, *STRIPS, jax.ShapeDtypeStruct((8, CH), F32), GRID)
-    weights, grad_grid, *rest = call(
+    cells = 2 * SIZE * SIZE
+    share, grad_grid, *sent = call(
         functools.partial(main_kernel, slots=slots),
         "main",
-        outs,
+        (jax.ShapeDtypeStruct((16, CH + 2 * PART_ROWS, 128), BF16), GRID, *STRIPS),
         scalars,
-        (*got, taps, gain.reshape(1, CH), w_in, w_out, cot.reshape(-1, CH), grid),
-        (NEAR, SPREAD, CONV, pltpu.VMEM((CH, FF), F32), pltpu.VMEM((CH, FF), F32), RIMS),
-        flops=20 * 10**9,
+        (*got, kernel, gain.reshape(1, CH)),
+        (
+            GRID_SPACE, NEAR, SPREAD, CONV, pltpu.VMEM((CH, FF), F32), pltpu.VMEM((CH, FF), F32), RIMS,
+            pltpu.VMEM((cells, CH), BF16), pltpu.VMEM((cells, CH), F32), pltpu.VMEM((cells, 128), F32),
+            pltpu.VMEM((cells, CH), F32), pltpu.VMEM((cells, CH), BF16), pltpu.VMEM((CH, FF), BF16),
+            pltpu.VMEM((FF, CH), BF16), pltpu.VMEM((TAPS, 8, 128), F32), pltpu.SemaphoreType.DMA((4,)),
+        ),
+        far=(w_in, w_out, cot.reshape(cells, CH), grid),
+        flops=40 * 10**9,
+        vmem_mib=48,
     )
-    sent, ggain, grid = rest[:5], rest[5], rest[6]
-    weights = lax.all_to_all(weights, "dp", 0, 0, tiled=True)
-    small = call(
-        taps_kernel,
-        "taps",
-        jax.ShapeDtypeStruct((16, 128, 128), BF16),
-        (),
-        (grid, grad_grid, ggain),
-        (pltpu.VMEM((TAPS, 8, 128), F32),),
-        flops=8 * 10**9,
-    )
-    small = lax.all_to_all(small, "dp", 0, 0, tiled=True)
+    share = lax.all_to_all(share, "dp", 0, 0, tiled=True)
     got = exchange(sent)
     grad_fields = call(
         functools.partial(back_kernel, slots=slots),
         "back",
         jax.ShapeDtypeStruct((2, SIZE, SIZE, CH), BF16),
         scalars,
-        (*got, taps, cot, grad_grid),
-        (GRID_SPACE, NEAR, SPREAD, CONV),
-        flops=8 * 10**9,
+        (*got, kernel, cot),
+        (GRID_SPACE, NEAR, SPREAD, CONV, pltpu.SemaphoreType.DMA(())),
+        far=(grad_grid,),
+        flops=12 * 10**9,
     )
     pieces = jax.ShapeDtypeStruct((32, 16, 128), BF16)
-    stages = (pltpu.VMEM((128, 128), F32), pltpu.VMEM((32, 16, 128), F32))
-    cut = call(first_sum_kernel, "sum_dp", pieces, (), (weights, small), stages)
+    stage = pltpu.VMEM((32, 16, 128), F32)
+    cut = call(first_sum_kernel, "sum_dp", pieces, (), (share,), (stage,))
     cut = lax.all_to_all(cut, "tiles", 0, 0, tiled=True)
     cut = call(second_sum_kernel, "sum_tiles", pieces, (), (cut,))
     cut = lax.all_to_all(cut, "tiles", 0, 0, tiled=True)
@@ -419,16 +456,16 @@
         functools.partial(last_kernel, scale=scale),
         "last",
         (
-            jax.ShapeDtypeStruct((CH, 64), F32),
             jax.ShapeDtypeStruct((64, CH), F32),
-            jax.ShapeDtypeStruct((TAPS, CH), F32),
+            jax.ShapeDtypeStruct((64, CH), F32),
+            jax.ShapeDtypeStruct((KW, KW, CH), F32),
             jax.ShapeDtypeStruct((1, CH), F32),
         ),
         (),
         (cut,),
-        (stages[1], stages[0]),
+        (stage, pltpu.VMEM((2 * PART_ROWS, 128), F32)),
     )
-    return grad_fields[None], g_in, g_out, g_taps.reshape(KW, KW, CH), g_gain.reshape(CH)
+    return grad_fields[None], g_in.T, g_out, g_taps, g_gain.reshape(CH)
 
 
 def solution(mesh):

time: 165 us -> 135 us (0.82)
  Pallas kernels: 71.7 us -> 48 us
  blocking collectives: 32.2 us -> 25.3 us
  waiting for transfers between devices: 8.21 us -> 10.7 us
    pallas_call x8 -> x7, Pallas kernels: 71.7 us -> 48 us  [call(): pl.pallas_call(kernel, out_shape=out, in_specs=[SMEM] * len(scalars) + [v...]
    all_to_all x2 -> x1, blocking collectives: 32.2 us -> 25.3 us  [body(): share = lax.all_to_all(share, 'dp', 0, 0, tiled=True)]
    reshape x2 -> x0, local copies, waits for them, and re-layouts: 2.9 us -> none  [the longest x1 1.45 us: body(): taps = kernel.reshape(TAPS, CH)]
    all_to_all x2, waiting for transfers between devices: 8.19 us -> 10.7 us  [body(): cut = lax.all_to_all(cut, 'tiles', 0, 0, tiled=True)]
    unnamed x31 -> x22, local copies, waits for them, and re-layouts: 4.56 us -> 6.85 us
  transfers between devices with their start and end apart: 10 -> 10, of which waited for: 2 -> 2; matrix products, arithmetic and copies ran while one was open for 1% -> 0% of each run, Pallas kernels for 12% -> 9%
where the time goes in v2:
time: 135 us; the launch traced here: 134 us
  Pallas kernels  48 us (36%)
  starting transfers between devices  42.7 us (32%)
  blocking collectives  25.3 us (19%)
  waiting for transfers between devices  10.7 us (8%)
  local copies, waits for them, and re-layouts  6.85 us (5%)
    pallas_call x7, Pallas kernels, call(): pl.pallas_call(kernel, out_shape=out, in_specs=[SMEM] * len(scalars) + [v...  48 us
    all_to_all x1, blocking collectives, body(): share = lax.all_to_all(share, 'dp', 0, 0, tiled=True)  25.3 us
    ppermute x8, starting transfers between devices, exchange(): lax.ppermute(strip, 'tiles', [(i, (i + off) % n) for i in range(n)])  22.7 us
    all_to_all x2, starting transfers between devices, body(): cut = lax.all_to_all(cut, 'tiles', 0, 0, tiled=True)  20 us
    all_to_all x2, waiting for transfers between devices, body(): cut = lax.all_to_all(cut, 'tiles', 0, 0, tiled=True)  10.7 us
    unnamed x22, local copies, waits for them, and re-layouts  6.85 us
  transfers between devices with their start and end apart: 10, of which 2 were waited for; matrix products, arithmetic and copies ran while one was open for 0% of the time, Pallas kernels for 9%

profile of v2, /device:TPU:1, one launch (start us, length us, event | category | flops | bytes accessed | tf_op | source)
XLA Modules:
  0.0 134.4 jit_solution(985961493693616228)
XLA Ops:
  0.7 0.0 copy-start
  0.7 1.2 copy-done
  1.9 0.7 copy-done.3
  2.6 0.9 rims.1
  3.4 3.0 %collective-permute-start = (bf16[4,3,32,256]{3,2,1,0:T(8,128)(2,1)S(1)}, bf16[4,3,32,256]{3,2,1,0:T(8,128)(2,1)S(1)}, u32[]{:S(2)}, u32[]{:S(2)}) collective-permute-start(bf16[4,3,32,256]{3,2,1,0:T(8,128)(2,1)S(1)} %get-tuple-element.22), channel_id=1, source_target_pairs={{0,16},{16,32},{32,48},{48,64},{64,80},{80,96},{96,112},{112,128},... | collective-permute-start | bytes 589832 | tf_op jit(solution)/shard_map/ppermute | solution.py:406
  6.5 3.9 %collective-permute-start.1 = (bf16[4,3,32,256]{3,2,1,0:T(8,128)(2,1)S(1)}, bf16[4,3,32,256]{3,2,1,0:T(8,128)(2,1)S(1)}, u32[]{:S(2)}, u32[]{:S(2)}) collective-permute-start(bf16[4,3,32,256]{3,2,1,0:T(8,128)(2,1)S(1)} %get-tuple-element.23), channel_id=1, source_target_pairs={{0,496},{16,0},{32,16},{48,32},{64,48},{80,64},{96,80},{112,96},{1... | collective-permute-start | bytes 589832 | tf_op jit(solution)/shard_map/ppermute | solution.py:406
  10.4 1.9 %collective-permute-start.2 = (bf16[3,3,32,256]{3,2,1,0:T(8,128)(2,1)S(1)}, bf16[3,3,32,256]{3,2,1,0:T(8,128)(2,1)S(1)}, u32[]{:S(2)}, u32[]{:S(2)}) collective-permute-start(bf16[3,3,32,256]{3,2,1,0:T(8,128)(2,1)S(1)} %get-tuple-element.24), channel_id=1, source_target_pairs={{0,32},{16,48},{32,64},{48,80},{64,96},{80,112},{96,128},{112,144}... | collective-permute-start | bytes 442376 | tf_op jit(solution)/shard_map/ppermute | solution.py:406
  12.3 5.7 %collective-permute-start.3 = (bf16[3,3,32,256]{3,2,1,0:T(8,128)(2,1)S(1)}, bf16[3,3,32,256]{3,2,1,0:T(8,128)(2,1)S(1)}, u32[]{:S(2)}, u32[]{:S(2)}) collective-permute-start(bf16[3,3,32,256]{3,2,1,0:T(8,128)(2,1)S(1)} %get-tuple-element.25), channel_id=1, source_target_pairs={{0,480},{16,496},{32,0},{48,16},{64,32},{80,48},{96,64},{112,80},{... | collective-permute-start | bytes 442376 | tf_op jit(solution)/shard_map/ppermute | solution.py:406
  18.0 0.0 copy-start.1
  18.0 1.2 copy-done.1
  19.3 0.4 grid.1.grid_hbm
  19.7 1.7 %copy-done.2 = f32[6688,128]{1,0:T(8,128)} copy-done((f32[6688,128]{1,0:T(8,128)}, f32[6688,128]{1,0:T(8,128)S(1)}, u32[]{:S(2)}) %copy-start.2) | copy-done | bytes 3424280
  21.4 0.0 collective-permute-done.2.s3
  21.4 0.0 collective-permute-done.3.s4
  21.4 0.0 collective-permute-done.s1
  21.4 0.0 collective-permute-done.1.s2
  21.5 33.5 %main.1 = (bf16[16,368,128]{2,1,0:T(8,128)(2,1)S(1)}, f32[6688,128]{1,0:T(8,128)}, bf16[2,3,32,256]{3,2,1,0:T(8,128)(2,1)S(1)}, bf16[4,3,32,256]{3,2,1,0:T(8,128...) custom-call(s32[1]{0:T(128)} %bitcast.own_ref, ...), custom_call_target="tpu_custom_call" | custom-call | flops 40000000000 | bytes 1000000 | tf_op jit(solution)/shard_map/main/pallas_call | solution.py:390
  55.0 25.3 %all_to_all.15.in_ref = bf16[16,368,128]{2,1,0:T(8,128)(2,1)S(1)} all-to-all(bf16[16,368,128]{2,1,0:T(8,128)(2,1)S(1)} %get-tuple-element.32), channel_id=1, replica_groups=mesh['tiles'=32,'dp'=16] {'dp'}, dimensions={0} | all-to-all | bytes 3014656 | tf_op jit(solution)/shard_map/all_to_all | solution.py:436
  80.3 0.9 sum_dp.1
  81.3 13.6 %all-to-all-start.1 = ((bf16[32,16,128]{2,1,0:T(8,128)(2,1)}), bf16[32,16,128]{2,1,0:T(8,128)(2,1)S(1)}, u32[]{:S(2)}, u32[]{:S(2)}) async-start(bf16[32,16,128]{2,1,0:T(8,128)(2,1)} %sum_dp.1), calls=%async_computation.1 | async-start | bytes 262144 | tf_op jit(solution)/shard_map/all_to_all | solution.py:451
  94.9 1.6 %collective-permute-start.4 = (bf16[4,3,32,256]{3,2,1,0:T(8,128)(2,1)S(1)}, bf16[4,3,32,256]{3,2,1,0:T(8,128)(2,1)S(1)}, u32[]{:S(2)}, u32[]{:S(2)}) collective-permute-start(bf16[4,3,32,256]{3,2,1,0:T(8,128)(2,1)S(1)} %get-tuple-element.27), channel_id=1, source_target_pairs={{0,16},{16,32},{32,48},{48,64},{64,80},{80,96},{96,112},{112,128},... | collective-permute-start | bytes 589832 | tf_op jit(solution)/shard_map/ppermute | solution.py:406
  96.5 3.1 %collective-permute-start.6 = (bf16[3,3,32,256]{3,2,1,0:T(8,128)(2,1)S(1)}, bf16[3,3,32,256]{3,2,1,0:T(8,128)(2,1)S(1)}, u32[]{:S(2)}, u32[]{:S(2)}) collective-permute-start(bf16[3,3,32,256]{3,2,1,0:T(8,128)(2,1)S(1)} %get-tuple-element.29), channel_id=1, source_target_pairs={{0,32},{16,48},{32,64},{48,80},{64,96},{80,112},{96,128},{112,144}... | collective-permute-start | bytes 442376 | tf_op jit(solution)/shard_map/ppermute | solution.py:406
  99.6 3.4 %collective-permute-start.7 = (bf16[3,3,32,256]{3,2,1,0:T(8,128)(2,1)S(1)}, bf16[3,3,32,256]{3,2,1,0:T(8,128)(2,1)S(1)}, u32[]{:S(2)}, u32[]{:S(2)}) collective-permute-start(bf16[3,3,32,256]{3,2,1,0:T(8,128)(2,1)S(1)} %get-tuple-element.30), channel_id=1, source_target_pairs={{0,480},{16,496},{32,0},{48,16},{64,32},{80,48},{96,64},{112,80},{... | collective-permute-start | bytes 442376 | tf_op jit(solution)/shard_map/ppermute | solution.py:406
  103.0 7.7 %all-to-all-done.1.in_ref = bf16[32,16,128]{2,1,0:T(8,128)(2,1)S(1)} async-done(((bf16[32,16,128]{2,1,0:T(8,128)(2,1)}), bf16[32,16,128]{2,1,0:T(8,128)(2,1)S(1)}, u32[]{:S(2)}, u32[]{:S(2)}) %all-to-all-start.1) | async-done | bytes 131104 | tf_op jit(solution)/shard_map/all_to_all | solution.py:451
  110.7 0.7 sum_tiles.1
  111.4 6.4 %all-to-all-start.2 = ((bf16[32,16,128]{2,1,0:T(8,128)(2,1)}), bf16[32,16,128]{2,1,0:T(8,128)(2,1)S(1)}, u32[]{:S(2)}, u32[]{:S(2)}) async-start(bf16[32,16,128]{2,1,0:T(8,128)(2,1)} %sum_tiles.1), calls=%async_computation.2 | async-start | bytes 262144 | tf_op jit(solution)/shard_map/all_to_all | solution.py:453
  117.8 0.0 collective-permute-done.7.s4
  117.8 0.0 collective-permute-done.4.s1
  117.9 2.0 %copy-done.10 = f32[6688,128]{1,0:T(8,128)S(1)} copy-done((f32[6688,128]{1,0:T(8,128)S(1)}, f32[6688,128]{1,0:T(8,128)}, u32[]{:S(2)}) %copy-start.10) | copy-done | bytes 3424280
  119.8 10.8 %back.1 = bf16[2,32,32,256]{3,2,1,0:T(8,128)(2,1)} custom-call(s32[1]{0:T(128)} %bitcast.own_ref, s32[2,8]{1,0:T(2,128)S(1)} %copy-done.4, bf16[2,3,32,256]{3,2,1,0:T(8,128)(2,1)S(1)} %get-tuple-element.26.s0, bf16[4,3,32,256]{3,2,1,0:T(8,128)(2,1)S(1)} %collective-permute-done.4.s1, bf16[4,3,32,256]{3,2,1,0:T(8,128)(2,1)S(1)} %collective-permute-done.5.s2, ...), custom_call_target="tpu_custom_call" | custom-call | flops 12000000000 | bytes 1000000 | tf_op jit(solution)/shard_map/back/pallas_call | solution.py:390
  130.7 3.0 %all-to-all-done.2.in_ref = bf16[32,16,128]{2,1,0:T(8,128)(2,1)S(1)} async-done(((bf16[32,16,128]{2,1,0:T(8,128)(2,1)}), bf16[32,16,128]{2,1,0:T(8,128)(2,1)S(1)}, u32[]{:S(2)}, u32[]{:S(2)}) %all-to-all-start.2) | async-done | bytes 131104 | tf_op jit(solution)/shard_map/all_to_all | solution.py:453
  133.7 0.8 last.1
  (18 shorter events, 0.0 us)
Async XLA Ops:
  0.6 20.8 %copy-start.4 = (s32[2,8]{1,0:T(2,128)S(1)}, s32[2,8]{1,0:T(2,128)}, u32[]{:S(2)}) copy-start(s32[2,8]{1,0:T(2,128)} %near_ids.5) | copy-start | bytes 196
  0.6 20.8 %copy-start.9 = (f32[256]{0:T(256)S(1)}, f32[256]{0:T(256)}, u32[]{:S(2)}) copy-start(f32[256]{0:T(256)} %param.10) | copy-start | bytes 3076
  0.7 1.2 copy-start
  1.9 0.7 copy-start.3
  2.6 18.9 %copy-start.5 = (bf16[1,2,32,32,256]{4,3,2,1,0:T(8,128)(2,1)S(1)}, bf16[1,2,32,32,256]{4,3,2,1,0:T(8,128)(2,1)}, u32[]{:S(2)}) copy-start(bf16[1,2,32,32,256]{4,3,2,1,0:T(8,128)(2,1)} %param.13) | copy-start | bytes 3145732
  3.4 18.0 %collective-permute-start = (bf16[4,3,32,256]{3,2,1,0:T(8,128)(2,1)S(1)}, bf16[4,3,32,256]{3,2,1,0:T(8,128)(2,1)S(1)}, u32[]{:S(2)}, u32[]{:S(2)}) collective-permute-start(bf16[4,3,32,256]{3,2,1,0:T(8,128)(2,1)S(1)} %get-tuple-element.22), channel_id=1, source_target_pairs={{0,16},{16,32},{32,48},{48,64},{64,80},{80,96},{96,112},{112,128},... | collective-permute-start | bytes 589832 | tf_op jit(solution)/shard_map/ppermute | solution.py:406
  6.5 15.0 %collective-permute-start.1 = (bf16[4,3,32,256]{3,2,1,0:T(8,128)(2,1)S(1)}, bf16[4,3,32,256]{3,2,1,0:T(8,128)(2,1)S(1)}, u32[]{:S(2)}, u32[]{:S(2)}) collective-permute-start(bf16[4,3,32,256]{3,2,1,0:T(8,128)(2,1)S(1)} %get-tuple-element.23), channel_id=1, source_target_pairs={{0,496},{16,0},{32,16},{48,32},{64,48},{80,64},{96,80},{112,96},{1... | collective-permute-start | bytes 589832 | tf_op jit(solution)/shard_map/ppermute | solution.py:406
  10.4 11.1 %collective-permute-start.2 = (bf16[3,3,32,256]{3,2,1,0:T(8,128)(2,1)S(1)}, bf16[3,3,32,256]{3,2,1,0:T(8,128)(2,1)S(1)}, u32[]{:S(2)}, u32[]{:S(2)}) collective-permute-start(bf16[3,3,32,256]{3,2,1,0:T(8,128)(2,1)S(1)} %get-tuple-element.24), channel_id=1, source_target_pairs={{0,32},{16,48},{32,64},{48,80},{64,96},{80,112},{96,128},{112,144}... | collective-permute-start | bytes 442376 | tf_op jit(solution)/shard_map/ppermute | solution.py:406
  12.3 9.2 %collective-permute-start.3 = (bf16[3,3,32,256]{3,2,1,0:T(8,128)(2,1)S(1)}, bf16[3,3,32,256]{3,2,1,0:T(8,128)(2,1)S(1)}, u32[]{:S(2)}, u32[]{:S(2)}) collective-permute-start(bf16[3,3,32,256]{3,2,1,0:T(8,128)(2,1)S(1)} %get-tuple-element.25), channel_id=1, source_target_pairs={{0,480},{16,496},{32,0},{48,16},{64,32},{80,48},{96,64},{112,80},{... | collective-permute-start | bytes 442376 | tf_op jit(solution)/shard_map/ppermute | solution.py:406
  18.0 1.2 copy-start.1
  19.3 2.2 %copy-start.6 = (bf16[256,1024]{1,0:T(8,128)(2,1)S(1)}, bf16[256,1024]{1,0:T(8,128)(2,1)}, u32[]{:S(2)}) copy-start(bf16[256,1024]{1,0:T(8,128)(2,1)} %w_in_hbm.1) | copy-start | bytes 1572868
  19.3 2.2 %copy-start.7 = (bf16[1024,256]{1,0:T(8,128)(2,1)S(1)}, bf16[1024,256]{1,0:T(8,128)(2,1)}, u32[]{:S(2)}) copy-start(bf16[1024,256]{1,0:T(8,128)(2,1)} %w_out_hbm.1) | copy-start | bytes 1572868
  19.3 2.2 %copy-start.8 = (f32[7,7,256]{2,1,0:T(8,128)S(1)}, f32[7,7,256]{2,1,0:T(8,128)}, u32[]{:S(2)}) copy-start(f32[7,7,256]{2,1,0:T(8,128)} %kernel_ref.3) | copy-start | bytes 150532
  19.7 1.7 %copy-start.2 = (f32[6688,128]{1,0:T(8,128)}, f32[6688,128]{1,0:T(8,128)S(1)}, u32[]{:S(2)}) copy-start(f32[6688,128]{1,0:T(8,128)S(1)} %grid.1.grid_hbm) | copy-start | bytes 10272772
  81.3 29.5 %all-to-all-start.1 = ((bf16[32,16,128]{2,1,0:T(8,128)(2,1)}), bf16[32,16,128]{2,1,0:T(8,128)(2,1)S(1)}, u32[]{:S(2)}, u32[]{:S(2)}) async-start(bf16[32,16,128]{2,1,0:T(8,128)(2,1)} %sum_dp.1), calls=%async_computation.1 | async-start | bytes 262144 | tf_op jit(solution)/shard_map/all_to_all | solution.py:451
  94.9 22.9 %collective-permute-start.4 = (bf16[4,3,32,256]{3,2,1,0:T(8,128)(2,1)S(1)}, bf16[4,3,32,256]{3,2,1,0:T(8,128)(2,1)S(1)}, u32[]{:S(2)}, u32[]{:S(2)}) collective-permute-start(bf16[4,3,32,256]{3,2,1,0:T(8,128)(2,1)S(1)} %get-tuple-element.27), channel_id=1, source_target_pairs={{0,16},{16,32},{32,48},{48,64},{64,80},{80,96},{96,112},{112,128},... | collective-permute-start | bytes 589832 | tf_op jit(solution)/shard_map/ppermute | solution.py:406
  96.5 21.3 %collective-permute-start.5 = (bf16[4,3,32,256]{3,2,1,0:T(8,128)(2,1)S(1)}, bf16[4,3,32,256]{3,2,1,0:T(8,128)(2,1)S(1)}, u32[]{:S(2)}, u32[]{:S(2)}) collective-permute-start(bf16[4,3,32,256]{3,2,1,0:T(8,128)(2,1)S(1)} %get-tuple-element.28), channel_id=1, source_target_pairs={{0,496},{16,0},{32,16},{48,32},{64,48},{80,64},{96,80},{112,96},{1... | collective-permute-start | bytes 589832 | tf_op jit(solution)/shard_map/ppermute | solution.py:406
  96.5 21.3 %collective-permute-start.6 = (bf16[3,3,32,256]{3,2,1,0:T(8,128)(2,1)S(1)}, bf16[3,3,32,256]{3,2,1,0:T(8,128)(2,1)S(1)}, u32[]{:S(2)}, u32[]{:S(2)}) collective-permute-start(bf16[3,3,32,256]{3,2,1,0:T(8,128)(2,1)S(1)} %get-tuple-element.29), channel_id=1, source_target_pairs={{0,32},{16,48},{32,64},{48,80},{64,96},{80,112},{96,128},{112,144}... | collective-permute-start | bytes 442376 | tf_op jit(solution)/shard_map/ppermute | solution.py:406
  99.6 18.2 %collective-permute-start.7 = (bf16[3,3,32,256]{3,2,1,0:T(8,128)(2,1)S(1)}, bf16[3,3,32,256]{3,2,1,0:T(8,128)(2,1)S(1)}, u32[]{:S(2)}, u32[]{:S(2)}) collective-permute-start(bf16[3,3,32,256]{3,2,1,0:T(8,128)(2,1)S(1)} %get-tuple-element.30), channel_id=1, source_target_pairs={{0,480},{16,496},{32,0},{48,16},{64,32},{80,48},{96,64},{112,80},{... | collective-permute-start | bytes 442376 | tf_op jit(solution)/shard_map/ppermute | solution.py:406
  111.4 22.2 %all-to-all-start.2 = ((bf16[32,16,128]{2,1,0:T(8,128)(2,1)}), bf16[32,16,128]{2,1,0:T(8,128)(2,1)S(1)}, u32[]{:S(2)}, u32[]{:S(2)}) async-start(bf16[32,16,128]{2,1,0:T(8,128)(2,1)} %sum_tiles.1), calls=%async_computation.2 | async-start | bytes 262144 | tf_op jit(solution)/shard_map/all_to_all | solution.py:453
  117.9 2.0 %copy-start.10 = (f32[6688,128]{1,0:T(8,128)S(1)}, f32[6688,128]{1,0:T(8,128)}, u32[]{:S(2)}) copy-start(f32[6688,128]{1,0:T(8,128)} %get-tuple-element.31.grid_hbm) | copy-start | bytes 10272772

commit v3 on v2

--- a/solution.py
+++ b/solution.py
@@ -16,7 +16,9 @@
 TALL = HALF + 2 * RIM
 CH = 256
 FF = 1024
-PART_ROWS = 56
+NEAR_GROUP = 8
+PIECE = 48
+PART_ROWS = 64
 ROWS = 256
 F32 = jnp.float32
 BF16 = jnp.bfloat16
@@ -276,8 +278,11 @@
     for p in range(FF // 128):
         one = gwi[:, p * 128 : p * 128 + 128]
         two = gwo[:, p * 128 : p * 128 + 128]
-        share_ref[2 * p, 0:CH] = jnp.where(low, one, pltpu.roll(two, 64, 1)).astype(BF16)
-        share_ref[2 * p + 1, 0:CH] = jnp.where(low, pltpu.roll(one, 64, 1), two).astype(BF16)
+        even = jnp.where(low, one, pltpu.roll(two, 64, 1)).astype(BF16)
+        odd = jnp.where(low, pltpu.roll(one, 64, 1), two).astype(BF16)
+        for k in range(NEAR_GROUP):
+            share_ref[2 * p, PIECE * k : PIECE * k + 32] = even[32 * k : 32 * k + 32]
+            share_ref[2 * p + 1, PIECE * k : PIECE * k + 32] = odd[32 * k : 32 * k + 32]
     tap_gradients(grid3, grad_grid.reshape(TALL * WIDE, 8, 128), ggain, acc, share_ref)
     for t in range(2):
         for part in range(2):
@@ -325,7 +330,8 @@
         sums[part].append(jnp.zeros((PART_ROWS - TAPS - 1, 128), F32))
     total = jnp.concatenate(sums[0] + sums[1], axis=0).astype(BF16)
     for d in range(16):
-        share_ref[d, CH : CH + 2 * PART_ROWS] = total
+        for k in range(NEAR_GROUP):
+            share_ref[d, PIECE * k + 32 : PIECE * k + 48] = total[16 * k : 16 * k + 16]
 
 
 def back_kernel(own_ref, near_ids, s0, s1, s2, s3, s4, kernel_ref, cot_ref, grid_hbm, out_ref, grid, near, taps, conv, sem, *, slots):
@@ -341,30 +347,11 @@
             out_ref[t, i] = (cot_ref[t, i].astype(F32) + rows_of(conv, t, i // HALF, i % HALF)).astype(BF16)
 
 
-def first_sum_kernel(in_ref, out_ref, stage):
-    weights = jnp.sum(in_ref[:, 0:CH, :].astype(F32), axis=0)
-    small = jnp.sum(in_ref[:, CH : CH + 2 * PART_ROWS, :].astype(F32), axis=0)
-    stage[...] = jnp.zeros_like(stage)
-    for p in range(32):
-        stage[p, 0:8, :] = weights[8 * p : 8 * p + 8]
-        if 4 * p < 2 * PART_ROWS:
-            stage[p, 8:12, :] = small[4 * p : 4 * p + 4]
-    out_ref[...] = stage[...].astype(BF16)
-
-
-def second_sum_kernel(in_ref, out_ref):
-    total = jnp.sum(in_ref[...].astype(F32), axis=0).astype(BF16)
-    for p in range(32):
-        out_ref[p] = total
-
-
-def last_kernel(in_ref, w_in_ref, w_out_ref, taps_ref, gain_ref, stage, low, *, scale):
-    stage[...] = in_ref[...].astype(F32) * scale
-    weights = stage[:, 0:8, :].reshape(CH, 128).T
+def last_kernel(in_ref, w_in_ref, w_out_ref, taps_ref, gain_ref, low, *, scale):
+    weights = (in_ref[:, 0:32, :].astype(F32) * scale).reshape(CH, 128).T
     w_in_ref[...] = weights[0:64, :]
     w_out_ref[...] = weights[64:128, :]
-    for p in range(PART_ROWS // 2):
-        low[4 * p : 4 * p + 4, :] = stage[p, 8:12, :]
+    low[...] = (in_ref[:, 32:48, :].astype(F32) * scale).reshape(2 * PART_ROWS, 128)
     for part in range(2):
         lanes = lanes_of(part)
         for a in range(KW):
@@ -407,6 +394,18 @@
     return tuple(got[off] for off in OFFSETS)
 
 
+def sum_of(pieces):
+    return jnp.sum(pieces.astype(F32), axis=0)
+
+
+def copies_of(piece, count):
+    return jnp.broadcast_to(piece[None], (count, *piece.shape))
+
+
+def group_exchange(pieces, groups):
+    return lax.all_to_all(pieces, "tiles", 0, 0, tiled=True, axis_index_groups=groups)
+
+
 def body(fields, neighbours, kernel, gain, w_in, w_out, cotangent):
     n_tiles, n_dp = lax.axis_size("tiles"), lax.axis_size("dp")
     slots = 2 * n_tiles
@@ -420,7 +419,7 @@
     share, grad_grid, *sent = call(
         functools.partial(main_kernel, slots=slots),
         "main",
-        (jax.ShapeDtypeStruct((16, CH + 2 * PART_ROWS, 128), BF16), GRID, *STRIPS),
+        (jax.ShapeDtypeStruct((16, NEAR_GROUP * PIECE, 128), BF16), GRID, *STRIPS),
         scalars,
         (*got, kernel, gain.reshape(1, CH)),
         (
@@ -434,7 +433,7 @@
         vmem_mib=48,
     )
     share = lax.all_to_all(share, "dp", 0, 0, tiled=True)
-    got = exchange(sent)
+    share, got = lax.optimization_barrier((share, exchange(sent)))
     grad_fields = call(
         functools.partial(back_kernel, slots=slots),
         "back",
@@ -445,12 +444,13 @@
         far=(grad_grid,),
         flops=12 * 10**9,
     )
-    pieces = jax.ShapeDtypeStruct((32, 16, 128), BF16)
-    stage = pltpu.VMEM((32, 16, 128), F32)
-    cut = call(first_sum_kernel, "sum_dp", pieces, (), (share,), (stage,))
-    cut = lax.all_to_all(cut, "tiles", 0, 0, tiled=True)
-    cut = call(second_sum_kernel, "sum_tiles", pieces, (), (cut,))
-    cut = lax.all_to_all(cut, "tiles", 0, 0, tiled=True)
+    cut = sum_of(share)
+    near = [list(range(g, g + NEAR_GROUP)) for g in range(0, n_tiles, NEAR_GROUP)]
+    far = [list(range(g, n_tiles, NEAR_GROUP)) for g in range(NEAR_GROUP)]
+    cut = group_exchange(cut.astype(BF16).reshape(NEAR_GROUP, PIECE, 128), near)
+    cut = group_exchange(copies_of(sum_of(cut), len(far[0])), far)
+    cut, grad_fields = lax.optimization_barrier((cut, grad_fields))
+    cut = group_exchange(copies_of(sum_of(cut).astype(BF16), NEAR_GROUP), near)
     scale = float((n_dp * slots * SIZE * SIZE) ** -0.5)
     g_in, g_out, g_taps, g_gain = call(
         functools.partial(last_kernel, scale=scale),
@@ -463,7 +463,7 @@
         ),
         (),
         (cut,),
-        (stage, pltpu.VMEM((2 * PART_ROWS, 128), F32)),
+        (pltpu.VMEM((2 * PART_ROWS, 128), F32),),
     )
     return grad_fields[None], g_in.T, g_out, g_taps, g_gain.reshape(CH)
 

time: 135 us -> 132 us (0.978)
  starting transfers between devices: 42.7 us -> 40.4 us
  other arithmetic: 0 us -> 1.66 us
    all_to_all x2, starting transfers between devices: 20 us -> 16.1 us  [the longest x1 9.25 us: group_exchange(): lax.all_to_all(pieces, 'tiles', 0, 0, tiled=True, axis_index_groups=groups)]
    all_to_all x2, waiting for transfers between devices: 10.7 us -> 7.68 us  [the longest x1 7.68 us: body(): share = lax.all_to_all(share, 'dp', 0, 0, tiled=True)]
    ppermute x8, waiting for transfers between devices: 0.02 us -> 2.1 us  [exchange(): lax.ppermute(strip, 'tiles', [(i, (i + off) % n) for i in range(n)])]
    reduce_sum x0 -> x3, other arithmetic: none -> 1.66 us  [sum_of(): return jnp.sum(pieces.astype(F32), axis=0)]
    ppermute x8, starting transfers between devices: 22.7 us -> 24.3 us  [exchange(): lax.ppermute(strip, 'tiles', [(i, (i + off) % n) for i in range(n)])]
    all_to_all x1 -> x2, blocking collectives: 25.3 us -> 24.1 us  [group_exchange(): lax.all_to_all(pieces, 'tiles', 0, 0, tiled=True, axis_index_groups=groups)]
    pallas_call x7 -> x5, Pallas kernels: 48 us -> 46.9 us  [call(): pl.pallas_call(kernel, out_shape=out, in_specs=[SMEM] * len(scalars) + [v...]
  transfers between devices with their start and end apart: 10 -> 10, of which waited for: 2 -> 3; matrix products, arithmetic and copies ran while one was open for 0% -> 0% of each run, Pallas kernels for 9% -> 9%
where the time goes in v3:
time: 132 us; the launch traced here: 131 us
  Pallas kernels  46.9 us (36%)
  starting transfers between devices  40.4 us (31%)
  blocking collectives  24.1 us (18%)
  waiting for transfers between devices  9.78 us (7%)
  local copies, waits for them, and re-layouts  7.53 us (6%)
  other arithmetic  1.66 us (1%)
    pallas_call x5, Pallas kernels, call(): pl.pallas_call(kernel, out_shape=out, in_specs=[SMEM] * len(scalars) + [v...  46.9 us
    ppermute x8, starting transfers between devices, exchange(): lax.ppermute(strip, 'tiles', [(i, (i + off) % n) for i in range(n)])  24.3 us
    all_to_all x2, blocking collectives, group_exchange(): lax.all_to_all(pieces, 'tiles', 0, 0, tiled=True, axis_index_groups=groups)  24.1 us
    all_to_all x1, starting transfers between devices, group_exchange(): lax.all_to_all(pieces, 'tiles', 0, 0, tiled=True, axis_index_groups=groups)  9.25 us
    all_to_all x1, waiting for transfers between devices, body(): share = lax.all_to_all(share, 'dp', 0, 0, tiled=True)  7.68 us
    unnamed x22, local copies, waits for them, and re-layouts  6.87 us
    all_to_all x1, starting transfers between devices, body(): share = lax.all_to_all(share, 'dp', 0, 0, tiled=True)  6.81 us
  transfers between devices with their start and end apart: 10, of which 3 were waited for; matrix products, arithmetic and copies ran while one was open for 0% of the time, Pallas kernels for 9%

profile of v3, /device:TPU:1, one launch (start us, length us, event | category | flops | bytes accessed | tf_op | source)
XLA Modules:
  0.0 131.2 jit_solution(8268458713017552292)
XLA Ops:
  0.7 0.0 copy-start
  0.7 1.2 copy-done
  1.9 0.7 copy-done.3
  2.6 0.9 rims.1
  3.4 3.0 %collective-permute-start = (bf16[4,3,32,256]{3,2,1,0:T(8,128)(2,1)S(1)}, bf16[4,3,32,256]{3,2,1,0:T(8,128)(2,1)S(1)}, u32[]{:S(2)}, u32[]{:S(2)}) collective-permute-start(bf16[4,3,32,256]{3,2,1,0:T(8,128)(2,1)S(1)} %get-tuple-element.30), channel_id=1, source_target_pairs={{0,16},{16,32},{32,48},{48,64},{64,80},{80,96},{96,112},{112,128},... | collective-permute-start | bytes 589832 | tf_op jit(solution)/shard_map/ppermute | solution.py:393
  6.5 3.9 %collective-permute-start.1 = (bf16[4,3,32,256]{3,2,1,0:T(8,128)(2,1)S(1)}, bf16[4,3,32,256]{3,2,1,0:T(8,128)(2,1)S(1)}, u32[]{:S(2)}, u32[]{:S(2)}) collective-permute-start(bf16[4,3,32,256]{3,2,1,0:T(8,128)(2,1)S(1)} %get-tuple-element.31), channel_id=1, source_target_pairs={{0,496},{16,0},{32,16},{48,32},{64,48},{80,64},{96,80},{112,96},{1... | collective-permute-start | bytes 589832 | tf_op jit(solution)/shard_map/ppermute | solution.py:393
  10.4 1.9 %collective-permute-start.2 = (bf16[3,3,32,256]{3,2,1,0:T(8,128)(2,1)S(1)}, bf16[3,3,32,256]{3,2,1,0:T(8,128)(2,1)S(1)}, u32[]{:S(2)}, u32[]{:S(2)}) collective-permute-start(bf16[3,3,32,256]{3,2,1,0:T(8,128)(2,1)S(1)} %get-tuple-element.32), channel_id=1, source_target_pairs={{0,32},{16,48},{32,64},{48,80},{64,96},{80,112},{96,128},{112,144}... | collective-permute-start | bytes 442376 | tf_op jit(solution)/shard_map/ppermute | solution.py:393
  12.3 5.7 %collective-permute-start.3 = (bf16[3,3,32,256]{3,2,1,0:T(8,128)(2,1)S(1)}, bf16[3,3,32,256]{3,2,1,0:T(8,128)(2,1)S(1)}, u32[]{:S(2)}, u32[]{:S(2)}) collective-permute-start(bf16[3,3,32,256]{3,2,1,0:T(8,128)(2,1)S(1)} %get-tuple-element.33), channel_id=1, source_target_pairs={{0,480},{16,496},{32,0},{48,16},{64,32},{80,48},{96,64},{112,80},{... | collective-permute-start | bytes 442376 | tf_op jit(solution)/shard_map/ppermute | solution.py:393
  18.0 0.0 copy-start.1
  18.0 1.2 copy-done.1
  19.3 0.4 grid.1.grid_hbm
  19.7 1.8 %copy-done.2 = f32[6688,128]{1,0:T(8,128)} copy-done((f32[6688,128]{1,0:T(8,128)}, f32[6688,128]{1,0:T(8,128)S(1)}, u32[]{:S(2)}) %copy-start.2) | copy-done | bytes 3424280
  21.4 0.0 collective-permute-done.2.s3
  21.5 0.0 collective-permute-done.3.s4
  21.5 0.0 collective-permute-done.1.s2
  21.5 34.0 %main.1 = (bf16[16,384,128]{2,1,0:T(8,128)(2,1)}, f32[6688,128]{1,0:T(8,128)}, bf16[2,3,32,256]{3,2,1,0:T(8,128)(2,1)S(1)}, bf16[4,3,32,256]{3,2,1,0:T(8,128)(2,...) custom-call(s32[1]{0:T(128)} %bitcast.own_ref, ...), custom_call_target="tpu_custom_call" | custom-call | flops 40000000000 | bytes 1000000 | tf_op jit(solution)/shard_map/main/pallas_call | solution.py:377
  55.5 6.8 %all-to-all-start = ((bf16[16,384,128]{2,1,0:T(8,128)(2,1)}), bf16[16,384,128]{2,1,0:T(8,128)(2,1)}, u32[]{:S(2)}, u32[]{:S(2)}) async-start(bf16[16,384,128]{2,1,0:T(8,128)(2,1)} %get-tuple-element.34), calls=%async_computation | async-start | bytes 3145728 | tf_op jit(solution)/shard_map/all_to_all | solution.py:435
  62.3 1.6 %collective-permute-start.4 = (bf16[4,3,32,256]{3,2,1,0:T(8,128)(2,1)S(1)}, bf16[4,3,32,256]{3,2,1,0:T(8,128)(2,1)S(1)}, u32[]{:S(2)}, u32[]{:S(2)}) collective-permute-start(bf16[4,3,32,256]{3,2,1,0:T(8,128)(2,1)S(1)} %get-tuple-element.36), channel_id=1, source_target_pairs={{0,16},{16,32},{32,48},{48,64},{64,80},{80,96},{96,112},{112,128},... | collective-permute-start | bytes 589832 | tf_op jit(solution)/shard_map/ppermute | solution.py:393
  64.0 1.6 %collective-permute-start.5 = (bf16[4,3,32,256]{3,2,1,0:T(8,128)(2,1)S(1)}, bf16[4,3,32,256]{3,2,1,0:T(8,128)(2,1)S(1)}, u32[]{:S(2)}, u32[]{:S(2)}) collective-permute-start(bf16[4,3,32,256]{3,2,1,0:T(8,128)(2,1)S(1)} %get-tuple-element.37), channel_id=1, source_target_pairs={{0,496},{16,0},{32,16},{48,32},{64,48},{80,64},{96,80},{112,96},{1... | collective-permute-start | bytes 589832 | tf_op jit(solution)/shard_map/ppermute | solution.py:393
  65.6 1.9 %collective-permute-start.6 = (bf16[3,3,32,256]{3,2,1,0:T(8,128)(2,1)S(1)}, bf16[3,3,32,256]{3,2,1,0:T(8,128)(2,1)S(1)}, u32[]{:S(2)}, u32[]{:S(2)}) collective-permute-start(bf16[3,3,32,256]{3,2,1,0:T(8,128)(2,1)S(1)} %get-tuple-element.38), channel_id=1, source_target_pairs={{0,32},{16,48},{32,64},{48,80},{64,96},{80,112},{96,128},{112,144}... | collective-permute-start | bytes 442376 | tf_op jit(solution)/shard_map/ppermute | solution.py:393
  67.5 4.6 %collective-permute-start.7 = (bf16[3,3,32,256]{3,2,1,0:T(8,128)(2,1)S(1)}, bf16[3,3,32,256]{3,2,1,0:T(8,128)(2,1)S(1)}, u32[]{:S(2)}, u32[]{:S(2)}) collective-permute-start(bf16[3,3,32,256]{3,2,1,0:T(8,128)(2,1)S(1)} %get-tuple-element.39), channel_id=1, source_target_pairs={{0,480},{16,496},{32,0},{48,16},{64,32},{80,48},{96,64},{112,80},{... | collective-permute-start | bytes 442376 | tf_op jit(solution)/shard_map/ppermute | solution.py:393
  72.1 1.1 collective-permute-done.6.s3
  73.2 1.0 collective-permute-done.7.s4
  74.2 7.7 %all-to-all-done = bf16[16,384,128]{2,1,0:T(8,128)(2,1)} async-done(((bf16[16,384,128]{2,1,0:T(8,128)(2,1)}), bf16[16,384,128]{2,1,0:T(8,128)(2,1)}, u32[]{:S(2)}, u32[]{:S(2)}) %all-to-all-start) | async-done | bytes 1572896 | tf_op jit(solution)/shard_map/all_to_all | solution.py:435
  81.9 1.6 %reduce_sum.30 = bf16[384,128]{1,0:T(8,128)(2,1)S(1)} reduce(bf16[16,384,128]{2,1,0:T(8,128)(2,1)} %all-to-all-done, bf16[]{:T(256)} %constant.8.clone.1), dimensions={0}, to_apply=%region_0.0 | reduce | flops 737280 | bytes 1671170 | tf_op jit(solution)/shard_map/reduce_sum | solution.py:398
  83.5 13.4 %all_to_all.20 = bf16[8,48,128]{2,1,0:T(8,128)(2,1)S(1)} all-to-all(bf16[8,48,128]{2,1,0:T(8,128)(2,1)S(1)} %bitcast.14), channel_id=1, replica_groups={{0,16,32,48,64,80,96,112},{128,144,160,176,192,208,224,240},{256,272,28..., dimensions={0} | all-to-all | bytes 196608 | tf_op jit(solution)/shard_map/all_to_all | solution.py:406
  96.9 0.6 broadcast_in_dim.6
  97.5 9.3 %all-to-all-start.2 = ((f32[4,48,128]{2,1,0:T(8,128)}), f32[4,48,128]{2,1,0:T(8,128)S(1)}, u32[]{:S(2)}, u32[]{:S(2)}) async-start(f32[4,48,128]{2,1,0:T(8,128)} %broadcast_in_dim.6), calls=%async_computation.2 | async-start | bytes 196608 | tf_op jit(solution)/shard_map/all_to_all | solution.py:406
  106.8 2.0 %copy-done.10 = f32[6688,128]{1,0:T(8,128)S(1)} copy-done((f32[6688,128]{1,0:T(8,128)S(1)}, f32[6688,128]{1,0:T(8,128)}, u32[]{:S(2)}) %copy-start.10) | copy-done | bytes 3424280
  108.8 10.8 %back.1 = bf16[2,32,32,256]{3,2,1,0:T(8,128)(2,1)} custom-call(s32[1]{0:T(128)} %bitcast.own_ref, s32[2,8]{1,0:T(2,128)S(1)} %copy-done.4, bf16[2,3,32,256]{3,2,1,0:T(8,128)(2,1)S(1)} %get-tuple-element.41.s0, bf16[4,3,32,256]{3,2,1,0:T(8,128)(2,1)S(1)} %collective-permute-done.4.s1, bf16[4,3,32,256]{3,2,1,0:T(8,128)(2,1)S(1)} %collective-permute-done.5.s2, ...), custom_call_target="tpu_custom_call" | custom-call | flops 12000000000 | bytes 1000000 | tf_op jit(solution)/shard_map/back/pallas_call | solution.py:377
  119.7 10.7 %all_to_all.21.in_ref = bf16[8,48,128]{2,1,0:T(8,128)(2,1)S(1)} all-to-all(bf16[8,48,128]{2,1,0:T(8,128)(2,1)S(1)} %broadcast_in_dim.8), channel_id=1, replica_groups={{0,16,32,48,64,80,96,112},{128,144,160,176,192,208,224,240},{256,272,28..., dimensions={0} | all-to-all | bytes 196608 | tf_op jit(solution)/shard_map/all_to_all | solution.py:406
  130.4 0.8 last.1
  (22 shorter events, 0.1 us)
Async XLA Ops:
  0.6 20.8 %copy-start.4 = (s32[2,8]{1,0:T(2,128)S(1)}, s32[2,8]{1,0:T(2,128)}, u32[]{:S(2)}) copy-start(s32[2,8]{1,0:T(2,128)} %near_ids.5) | copy-start | bytes 196
  0.6 20.8 %copy-start.9 = (f32[256]{0:T(256)S(1)}, f32[256]{0:T(256)}, u32[]{:S(2)}) copy-start(f32[256]{0:T(256)} %param.10) | copy-start | bytes 3076
  0.7 1.2 copy-start
  1.9 0.7 copy-start.3
  2.6 18.9 %copy-start.5 = (bf16[1,2,32,32,256]{4,3,2,1,0:T(8,128)(2,1)S(1)}, bf16[1,2,32,32,256]{4,3,2,1,0:T(8,128)(2,1)}, u32[]{:S(2)}) copy-start(bf16[1,2,32,32,256]{4,3,2,1,0:T(8,128)(2,1)} %param.13) | copy-start | bytes 3145732
  3.4 18.0 %collective-permute-start = (bf16[4,3,32,256]{3,2,1,0:T(8,128)(2,1)S(1)}, bf16[4,3,32,256]{3,2,1,0:T(8,128)(2,1)S(1)}, u32[]{:S(2)}, u32[]{:S(2)}) collective-permute-start(bf16[4,3,32,256]{3,2,1,0:T(8,128)(2,1)S(1)} %get-tuple-element.30), channel_id=1, source_target_pairs={{0,16},{16,32},{32,48},{48,64},{64,80},{80,96},{96,112},{112,128},... | collective-permute-start | bytes 589832 | tf_op jit(solution)/shard_map/ppermute | solution.py:393
  6.5 15.0 %collective-permute-start.1 = (bf16[4,3,32,256]{3,2,1,0:T(8,128)(2,1)S(1)}, bf16[4,3,32,256]{3,2,1,0:T(8,128)(2,1)S(1)}, u32[]{:S(2)}, u32[]{:S(2)}) collective-permute-start(bf16[4,3,32,256]{3,2,1,0:T(8,128)(2,1)S(1)} %get-tuple-element.31), channel_id=1, source_target_pairs={{0,496},{16,0},{32,16},{48,32},{64,48},{80,64},{96,80},{112,96},{1... | collective-permute-start | bytes 589832 | tf_op jit(solution)/shard_map/ppermute | solution.py:393
  10.4 11.1 %collective-permute-start.2 = (bf16[3,3,32,256]{3,2,1,0:T(8,128)(2,1)S(1)}, bf16[3,3,32,256]{3,2,1,0:T(8,128)(2,1)S(1)}, u32[]{:S(2)}, u32[]{:S(2)}) collective-permute-start(bf16[3,3,32,256]{3,2,1,0:T(8,128)(2,1)S(1)} %get-tuple-element.32), channel_id=1, source_target_pairs={{0,32},{16,48},{32,64},{48,80},{64,96},{80,112},{96,128},{112,144}... | collective-permute-start | bytes 442376 | tf_op jit(solution)/shard_map/ppermute | solution.py:393
  12.3 9.2 %collective-permute-start.3 = (bf16[3,3,32,256]{3,2,1,0:T(8,128)(2,1)S(1)}, bf16[3,3,32,256]{3,2,1,0:T(8,128)(2,1)S(1)}, u32[]{:S(2)}, u32[]{:S(2)}) collective-permute-start(bf16[3,3,32,256]{3,2,1,0:T(8,128)(2,1)S(1)} %get-tuple-element.33), channel_id=1, source_target_pairs={{0,480},{16,496},{32,0},{48,16},{64,32},{80,48},{96,64},{112,80},{... | collective-permute-start | bytes 442376 | tf_op jit(solution)/shard_map/ppermute | solution.py:393
  18.0 1.2 copy-start.1
  19.3 2.2 %copy-start.6 = (bf16[256,1024]{1,0:T(8,128)(2,1)S(1)}, bf16[256,1024]{1,0:T(8,128)(2,1)}, u32[]{:S(2)}) copy-start(bf16[256,1024]{1,0:T(8,128)(2,1)} %w_in_hbm.1) | copy-start | bytes 1572868
  19.3 2.3 %copy-start.7 = (bf16[1024,256]{1,0:T(8,128)(2,1)S(1)}, bf16[1024,256]{1,0:T(8,128)(2,1)}, u32[]{:S(2)}) copy-start(bf16[1024,256]{1,0:T(8,128)(2,1)} %w_out_hbm.1) | copy-start | bytes 1572868
  19.3 2.3 %copy-start.8 = (f32[7,7,256]{2,1,0:T(8,128)S(1)}, f32[7,7,256]{2,1,0:T(8,128)}, u32[]{:S(2)}) copy-start(f32[7,7,256]{2,1,0:T(8,128)} %kernel_ref.3) | copy-start | bytes 150532
  19.7 1.8 %copy-start.2 = (f32[6688,128]{1,0:T(8,128)}, f32[6688,128]{1,0:T(8,128)S(1)}, u32[]{:S(2)}) copy-start(f32[6688,128]{1,0:T(8,128)S(1)} %grid.1.grid_hbm) | copy-start | bytes 10272772
  55.5 26.3 %all-to-all-start = ((bf16[16,384,128]{2,1,0:T(8,128)(2,1)}), bf16[16,384,128]{2,1,0:T(8,128)(2,1)}, u32[]{:S(2)}, u32[]{:S(2)}) async-start(bf16[16,384,128]{2,1,0:T(8,128)(2,1)} %get-tuple-element.34), calls=%async_computation | async-start | bytes 3145728 | tf_op jit(solution)/shard_map/all_to_all | solution.py:435
  62.3 11.8 %collective-permute-start.4 = (bf16[4,3,32,256]{3,2,1,0:T(8,128)(2,1)S(1)}, bf16[4,3,32,256]{3,2,1,0:T(8,128)(2,1)S(1)}, u32[]{:S(2)}, u32[]{:S(2)}) collective-permute-start(bf16[4,3,32,256]{3,2,1,0:T(8,128)(2,1)S(1)} %get-tuple-element.36), channel_id=1, source_target_pairs={{0,16},{16,32},{32,48},{48,64},{64,80},{80,96},{96,112},{112,128},... | collective-permute-start | bytes 589832 | tf_op jit(solution)/shard_map/ppermute | solution.py:393
  64.0 10.2 %collective-permute-start.5 = (bf16[4,3,32,256]{3,2,1,0:T(8,128)(2,1)S(1)}, bf16[4,3,32,256]{3,2,1,0:T(8,128)(2,1)S(1)}, u32[]{:S(2)}, u32[]{:S(2)}) collective-permute-start(bf16[4,3,32,256]{3,2,1,0:T(8,128)(2,1)S(1)} %get-tuple-element.37), channel_id=1, source_target_pairs={{0,496},{16,0},{32,16},{48,32},{64,48},{80,64},{96,80},{112,96},{1... | collective-permute-start | bytes 589832 | tf_op jit(solution)/shard_map/ppermute | solution.py:393
  65.6 7.6 %collective-permute-start.6 = (bf16[3,3,32,256]{3,2,1,0:T(8,128)(2,1)S(1)}, bf16[3,3,32,256]{3,2,1,0:T(8,128)(2,1)S(1)}, u32[]{:S(2)}, u32[]{:S(2)}) collective-permute-start(bf16[3,3,32,256]{3,2,1,0:T(8,128)(2,1)S(1)} %get-tuple-element.38), channel_id=1, source_target_pairs={{0,32},{16,48},{32,64},{48,80},{64,96},{80,112},{96,128},{112,144}... | collective-permute-start | bytes 442376 | tf_op jit(solution)/shard_map/ppermute | solution.py:393
  67.5 6.7 %collective-permute-start.7 = (bf16[3,3,32,256]{3,2,1,0:T(8,128)(2,1)S(1)}, bf16[3,3,32,256]{3,2,1,0:T(8,128)(2,1)S(1)}, u32[]{:S(2)}, u32[]{:S(2)}) collective-permute-start(bf16[3,3,32,256]{3,2,1,0:T(8,128)(2,1)S(1)} %get-tuple-element.39), channel_id=1, source_target_pairs={{0,480},{16,496},{32,0},{48,16},{64,32},{80,48},{96,64},{112,80},{... | collective-permute-start | bytes 442376 | tf_op jit(solution)/shard_map/ppermute | solution.py:393
  97.5 22.1 %all-to-all-start.2 = ((f32[4,48,128]{2,1,0:T(8,128)}), f32[4,48,128]{2,1,0:T(8,128)S(1)}, u32[]{:S(2)}, u32[]{:S(2)}) async-start(f32[4,48,128]{2,1,0:T(8,128)} %broadcast_in_dim.6), calls=%async_computation.2 | async-start | bytes 196608 | tf_op jit(solution)/shard_map/all_to_all | solution.py:406
  106.8 2.0 %copy-start.10 = (f32[6688,128]{1,0:T(8,128)S(1)}, f32[6688,128]{1,0:T(8,128)}, u32[]{:S(2)}) copy-start(f32[6688,128]{1,0:T(8,128)} %get-tuple-element.46.grid_hbm) | copy-start | bytes 10272772

commit v4 on v3

--- a/solution.py
+++ b/solution.py
@@ -86,6 +86,24 @@
     lax.fori_loop(0, 16, fetch, 0)
 
 
+def load(sources, targets, sems):
+    copies = [pltpu.make_async_copy(src, dst, sems.at[k]) for k, (src, dst) in enumerate(zip(sources, targets))]
+    for copy in copies:
+        copy.start()
+    return copies
+
+
+def wait_all(copies):
+    for copy in copies:
+        copy.wait()
+
+
+def put_tiles(tile_ref, grid):
+    for t in range(2):
+        for i in range(SIZE):
+            put_row(grid, WIDE, t, RIM + i, RIM, tile_ref[t, i].astype(F32))
+
+
 def put_halo(near, grid):
     for t in range(2):
         for i in range(RIM):
@@ -155,8 +173,9 @@
     return x * cdf, cdf + x * (bell * 0.3989422804014327)
 
 
-def rim_kernel(own_ref, near_ids, tile_ref, *rest, slots):
-    outs, (rims, stage) = rest[:5], rest[5:]
+def rim_kernel(own_ref, near_hbm, tile_hbm, *rest, slots):
+    outs, (near_ids, tile_ref, rims, stage, sems) = rest[:5], rest[5:]
+    wait_all(load((near_hbm, tile_hbm), (near_ids, tile_ref), sems))
     for s in range(2):
         rims[4 * s] = tile_ref[s, 0:RIM]
         rims[4 * s + 1] = tile_ref[s, SIZE - RIM : SIZE]
@@ -168,28 +187,22 @@
     send_strips(near_ids, own_ref[0], slots, rims, outs)
 
 
-def grid_kernel(tile_ref, grid):
-    for t in range(2):
-        for i in range(SIZE):
-            put_row(grid, WIDE, t, RIM + i, RIM, tile_ref[t, i].astype(F32))
-
-
-def main_kernel(own_ref, near_ids, s0, s1, s2, s3, s4, kernel_ref, gain_ref, w_in_hbm, w_out_hbm, cot_hbm, grid_hbm,
-                share_ref, grad_grid, o0, o1, o2, o3, o4,
+def main_kernel(own_ref, near_hbm, h0, h1, h2, h3, h4, tile_hbm, kernel_hbm, gain_hbm, w_in_hbm, w_out_hbm, cot_hbm,
+                share_hbm, grad_hbm, o0, o1, o2, o3, o4,
+                near_ids, s0, s1, s2, s3, s4, tile_ref, kernel_ref, gain_ref, w_in_ref, w_out_ref, cot_ref,
                 grid, near, taps, conv, gwi, gwo, rims, normed_ref, xhat_ref, inv_ref, gn_ref,
-                cot_ref, w_in_ref, w_out_ref, acc, sems, *, slots):
+                acc, share_ref, grad_grid, grad_ref, sems, out_sems, *, slots):
     own = own_ref[0]
-    copies = [
-        pltpu.make_async_copy(src, dst, sems.at[k])
-        for k, (src, dst) in enumerate(
-            ((grid_hbm, grid), (w_in_hbm, w_in_ref), (w_out_hbm, w_out_ref), (cot_hbm, cot_ref))
-        )
-    ]
-    for copy in copies:
-        copy.start()
+    copies = load(
+        (tile_hbm, near_hbm, h0, h1, h2, h3, h4, kernel_hbm, gain_hbm, w_in_hbm, w_out_hbm, cot_hbm),
+        (tile_ref, near_ids, s0, s1, s2, s3, s4, kernel_ref, gain_ref, w_in_ref, w_out_ref, cot_ref),
+        sems,
+    )
+    copies[0].wait()
+    put_tiles(tile_ref, grid)
+    wait_all(copies[1:9])
     fetch_strips(near_ids, own, slots, (s0, s1, s2, s3, s4), near)
     spread_taps(kernel_ref, taps)
-    copies[0].wait()
     put_halo(near, grid)
     grid3 = grid.reshape(TALL * WIDE, 8, 128)
     convolve(grid3, taps, False, conv.reshape(HALF * SIZE, 8, 128))
@@ -220,8 +233,7 @@
         return carry
 
     lax.fori_loop(0, 2 * SIZE * SIZE // ROWS, normalise, 0)
-    for copy in copies[1:]:
-        copy.wait()
+    wait_all(copies[9:])
     steps = [(t, slice(f * 256, f * 256 + 256)) for t in range(2) for f in range(FF // 256)]
     cells_of = [slice(t * SIZE * SIZE, (t + 1) * SIZE * SIZE) for t in range(2)]
     across = (((1,), (1,)), ((), ()))
@@ -265,7 +277,9 @@
         gx = gn * gain
         m1 = jnp.mean(gx, axis=-1, keepdims=True)
         m2 = jnp.mean(gx * xhat, axis=-1, keepdims=True)
-        gc = (inv * (gx - m1 - xhat * m2)).astype(BF16).astype(F32)
+        gc = (inv * (gx - m1 - xhat * m2)).astype(BF16)
+        grad_ref[cells, :] = gc
+        gc = gc.astype(F32)
         for r in range(lines):
             piece = gc[r * SIZE : (r + 1) * SIZE]
             at = ((first + r + RIM) * WIDE + RIM) * 8 + spot
@@ -274,6 +288,15 @@
         return ggain
 
     ggain = lax.fori_loop(0, 2 * SIZE * SIZE // ROWS, denormalise, jnp.zeros((8, CH), F32))
+    results = [pltpu.make_async_copy(grad_ref, grad_hbm, out_sems.at[0])]
+    results[0].start()
+
+    def send_rows(first, count, sem):
+        for k in range(NEAR_GROUP):
+            rows = pl.ds(PIECE * k + first, count)
+            results.append(pltpu.make_async_copy(share_ref.at[:, rows], share_hbm.at[:, rows], out_sems.at[sem + k]))
+            results[-1].start()
+
     low = lax.broadcasted_iota(jnp.int32, (CH, 128), 1) < 64
     for p in range(FF // 128):
         one = gwi[:, p * 128 : p * 128 + 128]
@@ -283,14 +306,11 @@
         for k in range(NEAR_GROUP):
             share_ref[2 * p, PIECE * k : PIECE * k + 32] = even[32 * k : 32 * k + 32]
             share_ref[2 * p + 1, PIECE * k : PIECE * k + 32] = odd[32 * k : 32 * k + 32]
+    send_rows(0, 32, 1)
     tap_gradients(grid3, grad_grid.reshape(TALL * WIDE, 8, 128), ggain, acc, share_ref)
+    send_rows(32, 16, 1 + NEAR_GROUP)
     for t in range(2):
         for part in range(2):
-            for r in range(RIM):
-                for half, at, other in ((0, RIM + HALF + r, RIM + r), (1, r, HALF + r)):
-                    mine = ((at * WIDE) + RIM) * 8 + place(half, t, part)
-                    theirs = ((other * WIDE) + RIM) * 8 + place(1 - half, t, part)
-                    grad_grid[pl.ds(mine, SIZE, stride=8), :] = grad_grid[pl.ds(theirs, SIZE, stride=8), :]
             lanes = lanes_of(part)
             for k in range(RIM):
                 top = ((RIM + k) * WIDE + RIM) * 8 + place(0, t, part)
@@ -304,6 +324,7 @@
                     ]
                     rims[4 * t + side, k, :, lanes] = jnp.concatenate(both, axis=0).astype(BF16)
     send_strips(near_ids, own, slots, rims, (o0, o1, o2, o3, o4))
+    wait_all(results)
 
 
 def tap_gradients(grid3, grad3, ggain, acc, share_ref):
@@ -334,17 +355,27 @@
             share_ref[d, PIECE * k + 32 : PIECE * k + 48] = total[16 * k : 16 * k + 16]
 
 
-def back_kernel(own_ref, near_ids, s0, s1, s2, s3, s4, kernel_ref, cot_ref, grid_hbm, out_ref, grid, near, taps, conv, sem, *, slots):
-    copy = pltpu.make_async_copy(grid_hbm, grid, sem)
-    copy.start()
+def back_kernel(own_ref, near_hbm, h0, h1, h2, h3, h4, grad_hbm, kernel_hbm, cot_hbm, out_ref,
+                near_ids, s0, s1, s2, s3, s4, grad_ref, kernel_ref, cot_ref, grid, near, taps, conv, sems, *, slots):
+    copies = load(
+        (grad_hbm, near_hbm, h0, h1, h2, h3, h4, kernel_hbm, cot_hbm),
+        (grad_ref, near_ids, s0, s1, s2, s3, s4, kernel_ref, cot_ref),
+        sems,
+    )
+    copies[0].wait()
+    put_tiles(grad_ref, grid)
+    wait_all(copies[1:])
     fetch_strips(near_ids, own_ref[0], slots, (s0, s1, s2, s3, s4), near)
     spread_taps(kernel_ref, taps)
-    copy.wait()
     put_halo(near, grid)
     convolve(grid.reshape(TALL * WIDE, 8, 128), taps, True, conv.reshape(HALF * SIZE, 8, 128))
     for t in range(2):
         for i in range(SIZE):
             out_ref[t, i] = (cot_ref[t, i].astype(F32) + rows_of(conv, t, i // HALF, i % HALF)).astype(BF16)
+
+
+def sum_kernel(in_ref, out_ref):
+    out_ref[...] = jnp.sum(in_ref[...].astype(F32), axis=0).astype(BF16)
 
 
 def last_kernel(in_ref, w_in_ref, w_out_ref, taps_ref, gain_ref, low, *, scale):
@@ -368,17 +399,48 @@
 GRID = jax.ShapeDtypeStruct((TALL * WIDE * 8, 128), F32)
 GRID_SPACE = pltpu.VMEM(GRID.shape, F32)
 SPREAD = pltpu.VMEM((TAPS, 8, 128), F32)
+CELLS = 2 * SIZE * SIZE
+SHARE = jax.ShapeDtypeStruct((16, NEAR_GROUP * PIECE, 128), BF16)
 CONV = pltpu.VMEM((HALF * SIZE * 8, 128), F32)
 
 
-def call(kernel, name, out, scalars, arrays, scratch=(), far=(), flops=10**6, moved=10**6, vmem_mib=24):
+IDS = pltpu.SMEM((2, 8), jnp.int32)
+TILES = pltpu.VMEM((2, SIZE, SIZE, CH), BF16)
+LANDED = (IDS, *(pltpu.VMEM(x.shape, BF16) for x in STRIPS), TILES, pltpu.VMEM((KW, KW, CH), F32))
+MAIN_SCRATCH = (
+    *LANDED,
+    pltpu.VMEM((1, CH), F32),
+    pltpu.VMEM((CH, FF), BF16),
+    pltpu.VMEM((FF, CH), BF16),
+    pltpu.VMEM((CELLS, CH), BF16),
+    GRID_SPACE,
+    NEAR,
+    SPREAD,
+    CONV,
+    pltpu.VMEM((CH, FF), F32),
+    pltpu.VMEM((CH, FF), F32),
+    RIMS,
+    pltpu.VMEM((CELLS, CH), BF16),
+    pltpu.VMEM((CELLS, CH), F32),
+    pltpu.VMEM((CELLS, 128), F32),
+    pltpu.VMEM((CELLS, CH), F32),
+    SPREAD,
+    pltpu.VMEM(SHARE.shape, BF16),
+    GRID_SPACE,
+    pltpu.VMEM((CELLS, CH), BF16),
+    pltpu.SemaphoreType.DMA((12,)),
+    pltpu.SemaphoreType.DMA((1 + 2 * NEAR_GROUP,)),
+)
+
+
+def call(kernel, name, out, scalars, arrays, scratch=(), far=(), far_outs=0, flops=10**6, moved=10**6, vmem_mib=24):
     vmem = pl.BlockSpec(memory_space=pltpu.VMEM)
-    anywhere = pl.BlockSpec(memory_space=pl.ANY)
+    hbm = pl.BlockSpec(memory_space=pltpu.HBM)
     return pl.pallas_call(
         kernel,
         out_shape=out,
-        in_specs=[SMEM] * len(scalars) + [vmem] * len(arrays) + [anywhere] * len(far),
-        out_specs=[vmem] * len(out) if isinstance(out, tuple) else vmem,
+        in_specs=[SMEM] * len(scalars) + [vmem] * len(arrays) + [hbm] * len(far),
+        out_specs=[hbm] * far_outs + [vmem] * (len(out) - far_outs) if isinstance(out, tuple) else vmem,
         scratch_shapes=scratch,
         compiler_params=pltpu.CompilerParams(vmem_limit_bytes=vmem_mib * 1024 * 1024),
         cost_estimate=pl.CostEstimate(flops=flops, bytes_accessed=moved, transcendentals=0),
@@ -409,28 +471,31 @@
 def body(fields, neighbours, kernel, gain, w_in, w_out, cotangent):
     n_tiles, n_dp = lax.axis_size("tiles"), lax.axis_size("dp")
     slots = 2 * n_tiles
-    scalars = (lax.axis_index("tiles").reshape(1).astype(jnp.int32), neighbours)
+    own = (lax.axis_index("tiles").reshape(1).astype(jnp.int32),)
     tiles, cot = fields[0], cotangent[0]
     stage = pltpu.VMEM((2, SIZE * 16, 128), F32)
-    sent = call(functools.partial(rim_kernel, slots=slots), "rims", STRIPS, scalars, (tiles,), (RIMS, stage))
-    grid = call(grid_kernel, "grid", GRID, (), (tiles,), moved=5 * 10**6)
+    sent = call(
+        functools.partial(rim_kernel, slots=slots),
+        "rims",
+        STRIPS,
+        own,
+        (),
+        (IDS, TILES, RIMS, stage, pltpu.SemaphoreType.DMA((2,))),
+        far=(neighbours, tiles),
+        vmem_mib=60,
+    )
     got = exchange(sent)
-    cells = 2 * SIZE * SIZE
-    share, grad_grid, *sent = call(
+    share, grad, *sent = call(
         functools.partial(main_kernel, slots=slots),
         "main",
-        (jax.ShapeDtypeStruct((16, NEAR_GROUP * PIECE, 128), BF16), GRID, *STRIPS),
-        scalars,
-        (*got, kernel, gain.reshape(1, CH)),
-        (
-            GRID_SPACE, NEAR, SPREAD, CONV, pltpu.VMEM((CH, FF), F32), pltpu.VMEM((CH, FF), F32), RIMS,
-            pltpu.VMEM((cells, CH), BF16), pltpu.VMEM((cells, CH), F32), pltpu.VMEM((cells, 128), F32),
-            pltpu.VMEM((cells, CH), F32), pltpu.VMEM((cells, CH), BF16), pltpu.VMEM((CH, FF), BF16),
-            pltpu.VMEM((FF, CH), BF16), pltpu.VMEM((TAPS, 8, 128), F32), pltpu.SemaphoreType.DMA((4,)),
-        ),
-        far=(w_in, w_out, cot.reshape(cells, CH), grid),
+        (SHARE, jax.ShapeDtypeStruct((CELLS, CH), BF16), *STRIPS),
+        own,
+        (),
+        MAIN_SCRATCH,
+        far=(neighbours, *got, tiles, kernel, gain.reshape(1, CH), w_in, w_out, cot.reshape(CELLS, CH)),
+        far_outs=2,
         flops=40 * 10**9,
-        vmem_mib=48,
+        vmem_mib=60,
     )
     share = lax.all_to_all(share, "dp", 0, 0, tiled=True)
     share, got = lax.optimization_barrier((share, exchange(sent)))
@@ -438,16 +503,17 @@
         functools.partial(back_kernel, slots=slots),
         "back",
         jax.ShapeDtypeStruct((2, SIZE, SIZE, CH), BF16),
-        scalars,
-        (*got, kernel, cot),
-        (GRID_SPACE, NEAR, SPREAD, CONV, pltpu.SemaphoreType.DMA(())),
-        far=(grad_grid,),
+        own,
+        (),
+        (*LANDED, TILES, GRID_SPACE, NEAR, SPREAD, CONV, pltpu.SemaphoreType.DMA((9,))),
+        far=(neighbours, *got, grad.reshape(tiles.shape), kernel, cot),
         flops=12 * 10**9,
-    )
-    cut = sum_of(share)
+        vmem_mib=60,
+    )
+    cut = call(sum_kernel, "sum_dp", jax.ShapeDtypeStruct(SHARE.shape[1:], BF16), (), (share,), vmem_mib=16)
     near = [list(range(g, g + NEAR_GROUP)) for g in range(0, n_tiles, NEAR_GROUP)]
     far = [list(range(g, n_tiles, NEAR_GROUP)) for g in range(NEAR_GROUP)]
-    cut = group_exchange(cut.astype(BF16).reshape(NEAR_GROUP, PIECE, 128), near)
+    cut = group_exchange(cut.reshape(NEAR_GROUP, PIECE, 128), near)
     cut = group_exchange(copies_of(sum_of(cut), len(far[0])), far)
     cut, grad_fields = lax.optimization_barrier((cut, grad_fields))
     cut = group_exchange(copies_of(sum_of(cut).astype(BF16), NEAR_GROUP), near)

time: 132 us -> 130 us (0.985)
  local copies, waits for them, and re-layouts: 7.53 us -> 1.45 us
  waiting for transfers between devices: 9.78 us -> 11.7 us
  other arithmetic: 1.66 us -> 0.03 us
  Pallas kernels: 46.9 us -> 48.4 us
  blocking collectives: 24.1 us -> 25.5 us
    unnamed x22 -> x24, local copies, waits for them, and re-layouts: 6.87 us -> 0.8 us
    ppermute x8, waiting for transfers between devices: 2.1 us -> 4.48 us  [exchange(): lax.ppermute(strip, 'tiles', [(i, (i + off) % n) for i in range(n)])]
    reduce_sum x3 -> x2, other arithmetic: 1.66 us -> 0.03 us  [sum_of(): return jnp.sum(pieces.astype(F32), axis=0)]
    pallas_call x5, Pallas kernels: 46.9 us -> 48.4 us  [call(): pl.pallas_call(kernel, out_shape=out, in_specs=[SMEM] * len(scalars) + [v...]
    all_to_all x2, blocking collectives: 24.1 us -> 25.5 us  [group_exchange(): lax.all_to_all(pieces, 'tiles', 0, 0, tiled=True, axis_index_groups=groups)]
  transfers between devices with their start and end apart: 10 -> 10, of which waited for: 3 -> 6; matrix products, arithmetic and copies ran while one was open for 0% -> 0% of each run, Pallas kernels for 9% -> 9%
where the time goes in v4:
time: 130 us
  Pallas kernels  48.4 us (37%)
  starting transfers between devices  41.7 us (32%)
  blocking collectives  25.5 us (20%)
  waiting for transfers between devices  11.7 us (9%)
  local copies, waits for them, and re-layouts  1.45 us (1%)
    pallas_call x5, Pallas kernels, call(): pl.pallas_call(kernel, out_shape=out, in_specs=[SMEM] * len(scalars) + [v...  48.4 us
    ppermute x8, starting transfers between devices, exchange(): lax.ppermute(strip, 'tiles', [(i, (i + off) % n) for i in range(n)])  25.5 us
    all_to_all x2, blocking collectives, group_exchange(): lax.all_to_all(pieces, 'tiles', 0, 0, tiled=True, axis_index_groups=groups)  25.5 us
    all_to_all x1, starting transfers between devices, group_exchange(): lax.all_to_all(pieces, 'tiles', 0, 0, tiled=True, axis_index_groups=groups)  9.28 us
    all_to_all x1, starting transfers between devices, body(): share = lax.all_to_all(share, 'dp', 0, 0, tiled=True)  6.89 us
    all_to_all x1, waiting for transfers between devices, body(): share = lax.all_to_all(share, 'dp', 0, 0, tiled=True)  6.38 us
    ppermute x8, waiting for transfers between devices, exchange(): lax.ppermute(strip, 'tiles', [(i, (i + off) % n) for i in range(n)])  4.48 us
  transfers between devices with their start and end apart: 10, of which 6 were waited for; matrix products, arithmetic and copies ran while one was open for 0% of the time, Pallas kernels for 9%

profile of v4, /device:TPU:1, one launch (start us, length us, event | category | flops | bytes accessed | tf_op | source)
XLA Modules:
  0.0 129.7 jit_solution(14410093123392170701)
XLA Ops:
  0.6 2.3 %rims.1 = (bf16[2,3,32,256]{3,2,1,0:T(8,128)(2,1)}, bf16[4,3,32,256]{3,2,1,0:T(8,128)(2,1)}, bf16[4,3,32,256]{3,2,1,0:T(8,128)(2,1)}, bf16[3,3,32,256]{3,2,1,0:T(8,128)(2,1)}, bf16[3,3,32,256]{3,2,1,0:T(8,128)(2,1)}) custom-call(s32[1]{0:T(128)} %bitcast.own_ref, s32[2,8]{1,0:T(2,128)} %near_hbm.5, bf16[2,32,32,256]{3,2,1,0:T(8,128)(2,1)} %bitcast.11), custom_call_target="tpu_custom_call" | custom-call | flops 1000000 | bytes 1000000 | tf_op jit(solution)/shard_map/rims/pallas_call | solution.py:439
  3.0 3.0 %collective-permute-start = (bf16[4,3,32,256]{3,2,1,0:T(8,128)(2,1)}, bf16[4,3,32,256]{3,2,1,0:T(8,128)(2,1)S(1)}, u32[]{:S(2)}, u32[]{:S(2)}) collective-permute-start(bf16[4,3,32,256]{3,2,1,0:T(8,128)(2,1)} %get-tuple-element.30), channel_id=1, source_target_pairs={{0,16},{16,32},{32,48},{48,64},{64,80},{80,96},{96,112},{112,128},... | collective-permute-start | bytes 589832 | tf_op jit(solution)/shard_map/ppermute | solution.py:455
  6.0 3.9 %collective-permute-start.1 = (bf16[4,3,32,256]{3,2,1,0:T(8,128)(2,1)}, bf16[4,3,32,256]{3,2,1,0:T(8,128)(2,1)S(1)}, u32[]{:S(2)}, u32[]{:S(2)}) collective-permute-start(bf16[4,3,32,256]{3,2,1,0:T(8,128)(2,1)} %get-tuple-element.31), channel_id=1, source_target_pairs={{0,496},{16,0},{32,16},{48,32},{64,48},{80,64},{96,80},{112,96},{1... | collective-permute-start | bytes 589832 | tf_op jit(solution)/shard_map/ppermute | solution.py:455
  9.9 1.9 %collective-permute-start.2 = (bf16[3,3,32,256]{3,2,1,0:T(8,128)(2,1)}, bf16[3,3,32,256]{3,2,1,0:T(8,128)(2,1)S(1)}, u32[]{:S(2)}, u32[]{:S(2)}) collective-permute-start(bf16[3,3,32,256]{3,2,1,0:T(8,128)(2,1)} %get-tuple-element.32), channel_id=1, source_target_pairs={{0,32},{16,48},{32,64},{48,80},{64,96},{80,112},{96,128},{112,144}... | collective-permute-start | bytes 442376 | tf_op jit(solution)/shard_map/ppermute | solution.py:455
  11.8 5.7 %collective-permute-start.3 = (bf16[3,3,32,256]{3,2,1,0:T(8,128)(2,1)}, bf16[3,3,32,256]{3,2,1,0:T(8,128)(2,1)S(1)}, u32[]{:S(2)}, u32[]{:S(2)}) collective-permute-start(bf16[3,3,32,256]{3,2,1,0:T(8,128)(2,1)} %get-tuple-element.33), channel_id=1, source_target_pairs={{0,480},{16,496},{32,0},{48,16},{64,32},{80,48},{96,64},{112,80},{... | collective-permute-start | bytes 442376 | tf_op jit(solution)/shard_map/ppermute | solution.py:455
  17.6 0.8 collective-permute-done.2.h3
  18.4 1.6 %collective-permute-done.3.h4 = bf16[3,3,32,256]{3,2,1,0:T(8,128)(2,1)S(1)} collective-permute-done((bf16[3,3,32,256]{3,2,1,0:T(8,128)(2,1)}, bf16[3,3,32,256]{3,2,1,0:T(8,128)(2,1)S(1)}, u32[]{:S(2)}, u32[]{:S(2)}) %collective-permute-start.3) | collective-permute-done | bytes 147488 | tf_op jit(solution)/shard_map/ppermute | solution.py:455
  20.0 0.0 collective-permute-done.h1
  20.0 0.0 collective-permute-done.1.h2
  20.0 0.0 copy-start.5
  20.0 0.6 copy-done.11
  20.6 0.1 copy-done.4
  20.7 0.0 copy-done.5
  20.8 33.3 %main.1 = (bf16[16,384,128]{2,1,0:T(8,128)(2,1)}, bf16[2048,256]{1,0:T(8,128)(2,1)}, bf16[2,3,32,256]{3,2,1,0:T(8,128)(2,1)}, bf16[4,3,32,256]{3,2,1,0:T(8,128)(...) custom-call(s32[1]{0:T(128)} %bitcast.own_ref, ...), custom_call_target="tpu_custom_call" | custom-call | flops 40000000000 | bytes 1000000 | tf_op jit(solution)/shard_map/main/pallas_call | solution.py:439
  54.1 6.9 %all-to-all-start = ((bf16[16,384,128]{2,1,0:T(8,128)(2,1)}), bf16[16,384,128]{2,1,0:T(8,128)(2,1)S(1)}, u32[]{:S(2)}, u32[]{:S(2)}) async-start(bf16[16,384,128]{2,1,0:T(8,128)(2,1)} %get-tuple-element.34), calls=%async_computation | async-start | bytes 3145728 | tf_op jit(solution)/shard_map/all_to_all | solution.py:500
  61.0 2.2 %collective-permute-start.4 = (bf16[4,3,32,256]{3,2,1,0:T(8,128)(2,1)S(1)}, bf16[4,3,32,256]{3,2,1,0:T(8,128)(2,1)S(1)}, u32[]{:S(2)}, u32[]{:S(2)}) collective-permute-start(bf16[4,3,32,256]{3,2,1,0:T(8,128)(2,1)S(1)} %copy-done.3), channel_id=1, source_target_pairs={{0,16},{16,32},{32,48},{48,64},{64,80},{80,96},{96,112},{112,128},... | collective-permute-start | bytes 589832 | tf_op jit(solution)/shard_map/ppermute | solution.py:455
  63.3 1.6 %collective-permute-start.5 = (bf16[4,3,32,256]{3,2,1,0:T(8,128)(2,1)S(1)}, bf16[4,3,32,256]{3,2,1,0:T(8,128)(2,1)S(1)}, u32[]{:S(2)}, u32[]{:S(2)}) collective-permute-start(bf16[4,3,32,256]{3,2,1,0:T(8,128)(2,1)S(1)} %copy-done.2), channel_id=1, source_target_pairs={{0,496},{16,0},{32,16},{48,32},{64,48},{80,64},{96,80},{112,96},{1... | collective-permute-start | bytes 589832 | tf_op jit(solution)/shard_map/ppermute | solution.py:455
  64.9 1.9 %collective-permute-start.6 = (bf16[3,3,32,256]{3,2,1,0:T(8,128)(2,1)S(1)}, bf16[3,3,32,256]{3,2,1,0:T(8,128)(2,1)S(1)}, u32[]{:S(2)}, u32[]{:S(2)}) collective-permute-start(bf16[3,3,32,256]{3,2,1,0:T(8,128)(2,1)S(1)} %copy-done.9), channel_id=1, source_target_pairs={{0,32},{16,48},{32,64},{48,80},{64,96},{80,112},{96,128},{112,144}... | collective-permute-start | bytes 442376 | tf_op jit(solution)/shard_map/ppermute | solution.py:455
  66.8 5.2 %collective-permute-start.7 = (bf16[3,3,32,256]{3,2,1,0:T(8,128)(2,1)S(1)}, bf16[3,3,32,256]{3,2,1,0:T(8,128)(2,1)S(1)}, u32[]{:S(2)}, u32[]{:S(2)}) collective-permute-start(bf16[3,3,32,256]{3,2,1,0:T(8,128)(2,1)S(1)} %copy-done.8), channel_id=1, source_target_pairs={{0,480},{16,496},{32,0},{48,16},{64,32},{80,48},{96,64},{112,80},{... | collective-permute-start | bytes 442376 | tf_op jit(solution)/shard_map/ppermute | solution.py:455
  72.0 0.9 collective-permute-done.6.h3
  72.9 1.2 collective-permute-done.7.h4
  74.1 0.0 collective-permute-done.4.h1
  74.1 0.0 collective-permute-done.5.h2
  74.1 6.4 %all-to-all-done.in_ref = bf16[16,384,128]{2,1,0:T(8,128)(2,1)S(1)} async-done(((bf16[16,384,128]{2,1,0:T(8,128)(2,1)}), bf16[16,384,128]{2,1,0:T(8,128)(2,1)S(1)}, u32[]{:S(2)}, u32[]{:S(2)}) %all-to-all-start) | async-done | bytes 1572896 | tf_op jit(solution)/shard_map/all_to_all | solution.py:500
  80.5 0.2 sum_dp.1
  80.7 14.6 %all_to_all.20 = bf16[8,48,128]{2,1,0:T(8,128)(2,1)S(1)} all-to-all(bf16[8,48,128]{2,1,0:T(8,128)(2,1)S(1)} %bitcast.10), channel_id=1, replica_groups={{0,16,32,48,64,80,96,112},{128,144,160,176,192,208,224,240},{256,272,28..., dimensions={0} | all-to-all | bytes 196608 | tf_op jit(solution)/shard_map/all_to_all | solution.py:468
  95.3 0.6 broadcast_in_dim.6
  96.0 9.3 %all-to-all-start.2 = ((f32[4,48,128]{2,1,0:T(8,128)}), f32[4,48,128]{2,1,0:T(8,128)S(1)}, u32[]{:S(2)}, u32[]{:S(2)}) async-start(f32[4,48,128]{2,1,0:T(8,128)} %broadcast_in_dim.6), calls=%async_computation.2 | async-start | bytes 196608 | tf_op jit(solution)/shard_map/all_to_all | solution.py:468
  105.3 11.8 %back.1 = bf16[2,32,32,256]{3,2,1,0:T(8,128)(2,1)} custom-call(s32[1]{0:T(128)} %bitcast.own_ref, s32[2,8]{1,0:T(2,128)} %near_hbm.5, bf16[2,3,32,256]{3,2,1,0:T(8,128)(2,1)} %get-tuple-element.41.h0, bf16[4,3,32,256]{3,2,1,0:T(8,128)(2,1)} %copy-done, bf16[4,3,32,256]{3,2,1,0:T(8,128)(2,1)} %copy-done.1, bf16[3,3,32,256]{3,2,1,0:T(8,128)(2,1)} %copy-done.6, ...), custom_call_target="tpu_custom_call" | custom-call | flops 12000000000 | bytes 1000000 | tf_op jit(solution)/shard_map/back/pallas_call | solution.py:439
  117.1 0.8 all-to-all-done.2
  118.0 10.9 %all_to_all.21.in_ref = bf16[8,48,128]{2,1,0:T(8,128)(2,1)S(1)} all-to-all(bf16[8,48,128]{2,1,0:T(8,128)(2,1)S(1)} %broadcast_in_dim.8), channel_id=1, replica_groups={{0,16,32,48,64,80,96,112},{128,144,160,176,192,208,224,240},{256,272,28..., dimensions={0} | all-to-all | bytes 196608 | tf_op jit(solution)/shard_map/all_to_all | solution.py:468
  128.9 0.8 last.1
  (23 shorter events, 0.1 us)
Async XLA Ops:
  3.0 17.0 %collective-permute-start = (bf16[4,3,32,256]{3,2,1,0:T(8,128)(2,1)}, bf16[4,3,32,256]{3,2,1,0:T(8,128)(2,1)S(1)}, u32[]{:S(2)}, u32[]{:S(2)}) collective-permute-start(bf16[4,3,32,256]{3,2,1,0:T(8,128)(2,1)} %get-tuple-element.30), channel_id=1, source_target_pairs={{0,16},{16,32},{32,48},{48,64},{64,80},{80,96},{96,112},{112,128},... | collective-permute-start | bytes 589832 | tf_op jit(solution)/shard_map/ppermute | solution.py:455
  6.0 14.0 %collective-permute-start.1 = (bf16[4,3,32,256]{3,2,1,0:T(8,128)(2,1)}, bf16[4,3,32,256]{3,2,1,0:T(8,128)(2,1)S(1)}, u32[]{:S(2)}, u32[]{:S(2)}) collective-permute-start(bf16[4,3,32,256]{3,2,1,0:T(8,128)(2,1)} %get-tuple-element.31), channel_id=1, source_target_pairs={{0,496},{16,0},{32,16},{48,32},{64,48},{80,64},{96,80},{112,96},{1... | collective-permute-start | bytes 589832 | tf_op jit(solution)/shard_map/ppermute | solution.py:455
  9.9 8.5 %collective-permute-start.2 = (bf16[3,3,32,256]{3,2,1,0:T(8,128)(2,1)}, bf16[3,3,32,256]{3,2,1,0:T(8,128)(2,1)S(1)}, u32[]{:S(2)}, u32[]{:S(2)}) collective-permute-start(bf16[3,3,32,256]{3,2,1,0:T(8,128)(2,1)} %get-tuple-element.32), channel_id=1, source_target_pairs={{0,32},{16,48},{32,64},{48,80},{64,96},{80,112},{96,128},{112,144}... | collective-permute-start | bytes 442376 | tf_op jit(solution)/shard_map/ppermute | solution.py:455
  11.8 8.2 %collective-permute-start.3 = (bf16[3,3,32,256]{3,2,1,0:T(8,128)(2,1)}, bf16[3,3,32,256]{3,2,1,0:T(8,128)(2,1)S(1)}, u32[]{:S(2)}, u32[]{:S(2)}) collective-permute-start(bf16[3,3,32,256]{3,2,1,0:T(8,128)(2,1)} %get-tuple-element.33), channel_id=1, source_target_pairs={{0,480},{16,496},{32,0},{48,16},{64,32},{80,48},{96,64},{112,80},{... | collective-permute-start | bytes 442376 | tf_op jit(solution)/shard_map/ppermute | solution.py:455
  18.4 1.6 %copy-start.10 = (bf16[3,3,32,256]{3,2,1,0:T(8,128)(2,1)}, bf16[3,3,32,256]{3,2,1,0:T(8,128)(2,1)S(1)}, u32[]{:S(2)}) copy-start(bf16[3,3,32,256]{3,2,1,0:T(8,128)(2,1)S(1)} %collective-permute-done.2.h3) | copy-start | bytes 442372
  20.0 0.7 copy-start.11
  20.0 0.8 copy-start.4
  20.0 0.8 copy-start.5
  54.1 6.9 %copy-start.3 = (bf16[4,3,32,256]{3,2,1,0:T(8,128)(2,1)S(1)}, bf16[4,3,32,256]{3,2,1,0:T(8,128)(2,1)}, u32[]{:S(2)}) copy-start(bf16[4,3,32,256]{3,2,1,0:T(8,128)(2,1)} %get-tuple-element.36) | copy-start | bytes 589828
  54.1 9.2 %copy-start.2 = (bf16[4,3,32,256]{3,2,1,0:T(8,128)(2,1)S(1)}, bf16[4,3,32,256]{3,2,1,0:T(8,128)(2,1)}, u32[]{:S(2)}) copy-start(bf16[4,3,32,256]{3,2,1,0:T(8,128)(2,1)} %get-tuple-element.37) | copy-start | bytes 589828
  54.1 10.8 %copy-start.9 = (bf16[3,3,32,256]{3,2,1,0:T(8,128)(2,1)S(1)}, bf16[3,3,32,256]{3,2,1,0:T(8,128)(2,1)}, u32[]{:S(2)}) copy-start(bf16[3,3,32,256]{3,2,1,0:T(8,128)(2,1)} %get-tuple-element.38) | copy-start | bytes 442372
  54.1 12.7 %copy-start.8 = (bf16[3,3,32,256]{3,2,1,0:T(8,128)(2,1)S(1)}, bf16[3,3,32,256]{3,2,1,0:T(8,128)(2,1)}, u32[]{:S(2)}) copy-start(bf16[3,3,32,256]{3,2,1,0:T(8,128)(2,1)} %get-tuple-element.39) | copy-start | bytes 442372
  54.1 26.4 %all-to-all-start = ((bf16[16,384,128]{2,1,0:T(8,128)(2,1)}), bf16[16,384,128]{2,1,0:T(8,128)(2,1)S(1)}, u32[]{:S(2)}, u32[]{:S(2)}) async-start(bf16[16,384,128]{2,1,0:T(8,128)(2,1)} %get-tuple-element.34), calls=%async_computation | async-start | bytes 3145728 | tf_op jit(solution)/shard_map/all_to_all | solution.py:500
  61.0 13.1 %collective-permute-start.4 = (bf16[4,3,32,256]{3,2,1,0:T(8,128)(2,1)S(1)}, bf16[4,3,32,256]{3,2,1,0:T(8,128)(2,1)S(1)}, u32[]{:S(2)}, u32[]{:S(2)}) collective-permute-start(bf16[4,3,32,256]{3,2,1,0:T(8,128)(2,1)S(1)} %copy-done.3), channel_id=1, source_target_pairs={{0,16},{16,32},{32,48},{48,64},{64,80},{80,96},{96,112},{112,128},... | collective-permute-start | bytes 589832 | tf_op jit(solution)/shard_map/ppermute | solution.py:455
  63.3 10.9 %collective-permute-start.5 = (bf16[4,3,32,256]{3,2,1,0:T(8,128)(2,1)S(1)}, bf16[4,3,32,256]{3,2,1,0:T(8,128)(2,1)S(1)}, u32[]{:S(2)}, u32[]{:S(2)}) collective-permute-start(bf16[4,3,32,256]{3,2,1,0:T(8,128)(2,1)S(1)} %copy-done.2), channel_id=1, source_target_pairs={{0,496},{16,0},{32,16},{48,32},{64,48},{80,64},{96,80},{112,96},{1... | collective-permute-start | bytes 589832 | tf_op jit(solution)/shard_map/ppermute | solution.py:455
  64.9 8.0 %collective-permute-start.6 = (bf16[3,3,32,256]{3,2,1,0:T(8,128)(2,1)S(1)}, bf16[3,3,32,256]{3,2,1,0:T(8,128)(2,1)S(1)}, u32[]{:S(2)}, u32[]{:S(2)}) collective-permute-start(bf16[3,3,32,256]{3,2,1,0:T(8,128)(2,1)S(1)} %copy-done.9), channel_id=1, source_target_pairs={{0,32},{16,48},{32,64},{48,80},{64,96},{80,112},{96,128},{112,144}... | collective-permute-start | bytes 442376 | tf_op jit(solution)/shard_map/ppermute | solution.py:455
  66.8 7.3 %collective-permute-start.7 = (bf16[3,3,32,256]{3,2,1,0:T(8,128)(2,1)S(1)}, bf16[3,3,32,256]{3,2,1,0:T(8,128)(2,1)S(1)}, u32[]{:S(2)}, u32[]{:S(2)}) collective-permute-start(bf16[3,3,32,256]{3,2,1,0:T(8,128)(2,1)S(1)} %copy-done.8), channel_id=1, source_target_pairs={{0,480},{16,496},{32,0},{48,16},{64,32},{80,48},{96,64},{112,80},{... | collective-permute-start | bytes 442376 | tf_op jit(solution)/shard_map/ppermute | solution.py:455
  72.9 32.4 %copy-start.6 = (bf16[3,3,32,256]{3,2,1,0:T(8,128)(2,1)}, bf16[3,3,32,256]{3,2,1,0:T(8,128)(2,1)S(1)}, u32[]{:S(2)}) copy-start(bf16[3,3,32,256]{3,2,1,0:T(8,128)(2,1)S(1)} %collective-permute-done.6.h3) | copy-start | bytes 442372
  74.1 31.2 %copy-start.7 = (bf16[3,3,32,256]{3,2,1,0:T(8,128)(2,1)}, bf16[3,3,32,256]{3,2,1,0:T(8,128)(2,1)S(1)}, u32[]{:S(2)}) copy-start(bf16[3,3,32,256]{3,2,1,0:T(8,128)(2,1)S(1)} %collective-permute-done.7.h4) | copy-start | bytes 442372
  74.1 31.2 %copy-start = (bf16[4,3,32,256]{3,2,1,0:T(8,128)(2,1)}, bf16[4,3,32,256]{3,2,1,0:T(8,128)(2,1)S(1)}, u32[]{:S(2)}) copy-start(bf16[4,3,32,256]{3,2,1,0:T(8,128)(2,1)S(1)} %collective-permute-done.4.h1) | copy-start | bytes 589828
  74.1 31.2 %copy-start.1 = (bf16[4,3,32,256]{3,2,1,0:T(8,128)(2,1)}, bf16[4,3,32,256]{3,2,1,0:T(8,128)(2,1)S(1)}, u32[]{:S(2)}) copy-start(bf16[4,3,32,256]{3,2,1,0:T(8,128)(2,1)S(1)} %collective-permute-done.5.h2) | copy-start | bytes 589828
  96.0 21.9 %all-to-all-start.2 = ((f32[4,48,128]{2,1,0:T(8,128)}), f32[4,48,128]{2,1,0:T(8,128)S(1)}, u32[]{:S(2)}, u32[]{:S(2)}) async-start(f32[4,48,128]{2,1,0:T(8,128)} %broadcast_in_dim.6), calls=%async_computation.2 | async-start | bytes 196608 | tf_op jit(solution)/shard_map/all_to_all | solution.py:468

commit v5 on v4

--- a/solution.py
+++ b/solution.py
@@ -19,7 +19,7 @@
 NEAR_GROUP = 8
 PIECE = 48
 PART_ROWS = 64
-ROWS = 256
+ROWS = 512
 F32 = jnp.float32
 BF16 = jnp.bfloat16
 OFFSETS = (0, -1, 1, -2, 2)
@@ -124,10 +124,14 @@
     return 4 * s + rim
 
 
-def send_strips(near_ids, own, slots, rims, outs):
+def send_strips(near_ids, own, slots, rims, outs, sems):
+    copies = []
     for out, offset, pairs in zip(outs, OFFSETS, PAIRS):
         for k, (s, t) in enumerate(pairs):
-            out[k] = rims[pick_rim(near_ids, own, slots, s, offset, t)]
+            rim = rims.at[pick_rim(near_ids, own, slots, s, offset, t)]
+            copies.append(pltpu.make_async_copy(rim, out.at[k], sems.at[len(copies)]))
+            copies[-1].start()
+    return copies
 
 
 def spread_taps(kernel_ref, taps):
@@ -174,7 +178,7 @@
 
 
 def rim_kernel(own_ref, near_hbm, tile_hbm, *rest, slots):
-    outs, (near_ids, tile_ref, rims, stage, sems) = rest[:5], rest[5:]
+    outs, (near_ids, tile_ref, rims, stage, sems, out_sems) = rest[:5], rest[5:]
     wait_all(load((near_hbm, tile_hbm), (near_ids, tile_ref), sems))
     for s in range(2):
         rims[4 * s] = tile_ref[s, 0:RIM]
@@ -184,14 +188,14 @@
                 stage[part] = tile_ref[s, :, first : first + 16, lanes_of(part)].astype(F32).reshape(SIZE * 16, 128)
                 for k in range(RIM):
                     rims[4 * s + side, k, :, lanes_of(part)] = stage[part, pl.ds(row + k, SIZE, stride=16), :].astype(BF16)
-    send_strips(near_ids, own_ref[0], slots, rims, outs)
+    wait_all(send_strips(near_ids, own_ref[0], slots, rims, outs, out_sems))
 
 
 def main_kernel(own_ref, near_hbm, h0, h1, h2, h3, h4, tile_hbm, kernel_hbm, gain_hbm, w_in_hbm, w_out_hbm, cot_hbm,
                 share_hbm, grad_hbm, o0, o1, o2, o3, o4,
                 near_ids, s0, s1, s2, s3, s4, tile_ref, kernel_ref, gain_ref, w_in_ref, w_out_ref, cot_ref,
                 grid, near, taps, conv, gwi, gwo, rims, normed_ref, xhat_ref, inv_ref, gn_ref,
-                acc, share_ref, grad_grid, grad_ref, sems, out_sems, *, slots):
+                acc, share_ref, grad_grid, grad_ref, sems, out_sems, strip_sems, *, slots):
     own = own_ref[0]
     copies = load(
         (tile_hbm, near_hbm, h0, h1, h2, h3, h4, kernel_hbm, gain_hbm, w_in_hbm, w_out_hbm, cot_hbm),
@@ -210,7 +214,7 @@
     lines = ROWS // SIZE
 
     def where(n):
-        return (n % 2) * lines, place((n // 2) % 2, n // 4, 0)
+        return 0, place(n % 2, n // 2, 0)
 
     def normalise(n, carry):
         first, spot = where(n)
@@ -323,8 +327,7 @@
                         for half in range(2)
                     ]
                     rims[4 * t + side, k, :, lanes] = jnp.concatenate(both, axis=0).astype(BF16)
-    send_strips(near_ids, own, slots, rims, (o0, o1, o2, o3, o4))
-    wait_all(results)
+    wait_all(results + send_strips(near_ids, own, slots, rims, (o0, o1, o2, o3, o4), strip_sems))
 
 
 def tap_gradients(grid3, grad3, ggain, acc, share_ref):
@@ -404,6 +407,7 @@
 CONV = pltpu.VMEM((HALF * SIZE * 8, 128), F32)
 
 
+STRIP_SEMS = pltpu.SemaphoreType.DMA((sum(COUNTS),))
 IDS = pltpu.SMEM((2, 8), jnp.int32)
 TILES = pltpu.VMEM((2, SIZE, SIZE, CH), BF16)
 LANDED = (IDS, *(pltpu.VMEM(x.shape, BF16) for x in STRIPS), TILES, pltpu.VMEM((KW, KW, CH), F32))
@@ -430,6 +434,7 @@
     pltpu.VMEM((CELLS, CH), BF16),
     pltpu.SemaphoreType.DMA((12,)),
     pltpu.SemaphoreType.DMA((1 + 2 * NEAR_GROUP,)),
+    STRIP_SEMS,
 )
 
 
@@ -480,8 +485,9 @@
         STRIPS,
         own,
         (),
-        (IDS, TILES, RIMS, stage, pltpu.SemaphoreType.DMA((2,))),
+        (IDS, TILES, RIMS, stage, pltpu.SemaphoreType.DMA((2,)), STRIP_SEMS),
         far=(neighbours, tiles),
+        far_outs=5,
         vmem_mib=60,
     )
     got = exchange(sent)
@@ -493,7 +499,7 @@
         (),
         MAIN_SCRATCH,
         far=(neighbours, *got, tiles, kernel, gain.reshape(1, CH), w_in, w_out, cot.reshape(CELLS, CH)),
-        far_outs=2,
+        far_outs=7,
         flops=40 * 10**9,
         vmem_mib=60,
     )

time: 130 us -> 129 us (level)
  no operation moved by 1% of the time
where the time goes in v5:
time: 129 us; the launch traced here: 128 us
  Pallas kernels  47.2 us (37%)
  starting transfers between devices  41.7 us (32%)
  blocking collectives  25.5 us (20%)
  waiting for transfers between devices  11.7 us (9%)
  local copies, waits for them, and re-layouts  1.45 us (1%)
    pallas_call x5, Pallas kernels, call(): pl.pallas_call(kernel, out_shape=out, in_specs=[SMEM] * len(scalars) + [v...  47.2 us
    all_to_all x2, blocking collectives, group_exchange(): lax.all_to_all(pieces, 'tiles', 0, 0, tiled=True, axis_index_groups=groups)  25.5 us
    ppermute x8, starting transfers between devices, exchange(): lax.ppermute(strip, 'tiles', [(i, (i + off) % n) for i in range(n)])  25.5 us
    all_to_all x1, starting transfers between devices, group_exchange(): lax.all_to_all(pieces, 'tiles', 0, 0, tiled=True, axis_index_groups=groups)  9.27 us
    all_to_all x1, starting transfers between devices, body(): share = lax.all_to_all(share, 'dp', 0, 0, tiled=True)  6.9 us
    all_to_all x1, waiting for transfers between devices, body(): share = lax.all_to_all(share, 'dp', 0, 0, tiled=True)  6.37 us
    ppermute x8, waiting for transfers between devices, exchange(): lax.ppermute(strip, 'tiles', [(i, (i + off) % n) for i in range(n)])  4.48 us
  transfers between devices with their start and end apart: 10, of which 6 were waited for; matrix products, arithmetic and copies ran while one was open for 0% of the time, Pallas kernels for 9%

profile of v5, /device:TPU:1, one launch (start us, length us, event | category | flops | bytes accessed | tf_op | source)
XLA Modules:
  0.0 128.4 jit_solution(1603261304683843050)
XLA Ops:
  0.6 2.5 %rims.1 = (bf16[2,3,32,256]{3,2,1,0:T(8,128)(2,1)}, bf16[4,3,32,256]{3,2,1,0:T(8,128)(2,1)}, bf16[4,3,32,256]{3,2,1,0:T(8,128)(2,1)}, bf16[3,3,32,256]{3,2,1,0:T(8,128)(2,1)}, bf16[3,3,32,256]{3,2,1,0:T(8,128)(2,1)}) custom-call(s32[1]{0:T(128)} %bitcast.own_ref, s32[2,8]{1,0:T(2,128)} %near_hbm.5, bf16[2,32,32,256]{3,2,1,0:T(8,128)(2,1)} %bitcast.11), custom_call_target="tpu_custom_call" | custom-call | flops 1000000 | bytes 1000000 | tf_op jit(solution)/shard_map/rims/pallas_call | solution.py:444
  3.1 3.0 %collective-permute-start = (bf16[4,3,32,256]{3,2,1,0:T(8,128)(2,1)}, bf16[4,3,32,256]{3,2,1,0:T(8,128)(2,1)S(1)}, u32[]{:S(2)}, u32[]{:S(2)}) collective-permute-start(bf16[4,3,32,256]{3,2,1,0:T(8,128)(2,1)} %get-tuple-element.30), channel_id=1, source_target_pairs={{0,16},{16,32},{32,48},{48,64},{64,80},{80,96},{96,112},{112,128},... | collective-permute-start | bytes 589832 | tf_op jit(solution)/shard_map/ppermute | solution.py:460
  6.2 3.9 %collective-permute-start.1 = (bf16[4,3,32,256]{3,2,1,0:T(8,128)(2,1)}, bf16[4,3,32,256]{3,2,1,0:T(8,128)(2,1)S(1)}, u32[]{:S(2)}, u32[]{:S(2)}) collective-permute-start(bf16[4,3,32,256]{3,2,1,0:T(8,128)(2,1)} %get-tuple-element.31), channel_id=1, source_target_pairs={{0,496},{16,0},{32,16},{48,32},{64,48},{80,64},{96,80},{112,96},{1... | collective-permute-start | bytes 589832 | tf_op jit(solution)/shard_map/ppermute | solution.py:460
  10.0 1.9 %collective-permute-start.2 = (bf16[3,3,32,256]{3,2,1,0:T(8,128)(2,1)}, bf16[3,3,32,256]{3,2,1,0:T(8,128)(2,1)S(1)}, u32[]{:S(2)}, u32[]{:S(2)}) collective-permute-start(bf16[3,3,32,256]{3,2,1,0:T(8,128)(2,1)} %get-tuple-element.32), channel_id=1, source_target_pairs={{0,32},{16,48},{32,64},{48,80},{64,96},{80,112},{96,128},{112,144}... | collective-permute-start | bytes 442376 | tf_op jit(solution)/shard_map/ppermute | solution.py:460
  11.9 5.7 %collective-permute-start.3 = (bf16[3,3,32,256]{3,2,1,0:T(8,128)(2,1)}, bf16[3,3,32,256]{3,2,1,0:T(8,128)(2,1)S(1)}, u32[]{:S(2)}, u32[]{:S(2)}) collective-permute-start(bf16[3,3,32,256]{3,2,1,0:T(8,128)(2,1)} %get-tuple-element.33), channel_id=1, source_target_pairs={{0,480},{16,496},{32,0},{48,16},{64,32},{80,48},{96,64},{112,80},{... | collective-permute-start | bytes 442376 | tf_op jit(solution)/shard_map/ppermute | solution.py:460
  17.7 0.8 collective-permute-done.2.h3
  18.5 1.6 %collective-permute-done.3.h4 = bf16[3,3,32,256]{3,2,1,0:T(8,128)(2,1)S(1)} collective-permute-done((bf16[3,3,32,256]{3,2,1,0:T(8,128)(2,1)}, bf16[3,3,32,256]{3,2,1,0:T(8,128)(2,1)S(1)}, u32[]{:S(2)}, u32[]{:S(2)}) %collective-permute-start.3) | collective-permute-done | bytes 147488 | tf_op jit(solution)/shard_map/ppermute | solution.py:460
  20.1 0.0 collective-permute-done.h1
  20.1 0.0 collective-permute-done.1.h2
  20.1 0.0 copy-start.5
  20.1 0.6 copy-done.11
  20.8 0.1 copy-done.4
  20.9 0.0 copy-done.5
  20.9 32.0 %main.1 = (bf16[16,384,128]{2,1,0:T(8,128)(2,1)}, bf16[2048,256]{1,0:T(8,128)(2,1)}, bf16[2,3,32,256]{3,2,1,0:T(8,128)(2,1)}, bf16[4,3,32,256]{3,2,1,0:T(8,128)(...) custom-call(s32[1]{0:T(128)} %bitcast.own_ref, ...), custom_call_target="tpu_custom_call" | custom-call | flops 40000000000 | bytes 1000000 | tf_op jit(solution)/shard_map/main/pallas_call | solution.py:444
  52.9 6.9 %all-to-all-start = ((bf16[16,384,128]{2,1,0:T(8,128)(2,1)}), bf16[16,384,128]{2,1,0:T(8,128)(2,1)S(1)}, u32[]{:S(2)}, u32[]{:S(2)}) async-start(bf16[16,384,128]{2,1,0:T(8,128)(2,1)} %get-tuple-element.34), calls=%async_computation | async-start | bytes 3145728 | tf_op jit(solution)/shard_map/all_to_all | solution.py:506
  59.8 2.2 %collective-permute-start.4 = (bf16[4,3,32,256]{3,2,1,0:T(8,128)(2,1)S(1)}, bf16[4,3,32,256]{3,2,1,0:T(8,128)(2,1)S(1)}, u32[]{:S(2)}, u32[]{:S(2)}) collective-permute-start(bf16[4,3,32,256]{3,2,1,0:T(8,128)(2,1)S(1)} %copy-done.3), channel_id=1, source_target_pairs={{0,16},{16,32},{32,48},{48,64},{64,80},{80,96},{96,112},{112,128},... | collective-permute-start | bytes 589832 | tf_op jit(solution)/shard_map/ppermute | solution.py:460
  62.1 1.6 %collective-permute-start.5 = (bf16[4,3,32,256]{3,2,1,0:T(8,128)(2,1)S(1)}, bf16[4,3,32,256]{3,2,1,0:T(8,128)(2,1)S(1)}, u32[]{:S(2)}, u32[]{:S(2)}) collective-permute-start(bf16[4,3,32,256]{3,2,1,0:T(8,128)(2,1)S(1)} %copy-done.2), channel_id=1, source_target_pairs={{0,496},{16,0},{32,16},{48,32},{64,48},{80,64},{96,80},{112,96},{1... | collective-permute-start | bytes 589832 | tf_op jit(solution)/shard_map/ppermute | solution.py:460
  63.7 1.9 %collective-permute-start.6 = (bf16[3,3,32,256]{3,2,1,0:T(8,128)(2,1)S(1)}, bf16[3,3,32,256]{3,2,1,0:T(8,128)(2,1)S(1)}, u32[]{:S(2)}, u32[]{:S(2)}) collective-permute-start(bf16[3,3,32,256]{3,2,1,0:T(8,128)(2,1)S(1)} %copy-done.9), channel_id=1, source_target_pairs={{0,32},{16,48},{32,64},{48,80},{64,96},{80,112},{96,128},{112,144}... | collective-permute-start | bytes 442376 | tf_op jit(solution)/shard_map/ppermute | solution.py:460
  65.6 5.2 %collective-permute-start.7 = (bf16[3,3,32,256]{3,2,1,0:T(8,128)(2,1)S(1)}, bf16[3,3,32,256]{3,2,1,0:T(8,128)(2,1)S(1)}, u32[]{:S(2)}, u32[]{:S(2)}) collective-permute-start(bf16[3,3,32,256]{3,2,1,0:T(8,128)(2,1)S(1)} %copy-done.8), channel_id=1, source_target_pairs={{0,480},{16,496},{32,0},{48,16},{64,32},{80,48},{96,64},{112,80},{... | collective-permute-start | bytes 442376 | tf_op jit(solution)/shard_map/ppermute | solution.py:460
  70.8 0.9 collective-permute-done.6.h3
  71.7 1.2 collective-permute-done.7.h4
  72.9 0.0 collective-permute-done.4.h1
  72.9 0.0 collective-permute-done.5.h2
  72.9 6.4 %all-to-all-done.in_ref = bf16[16,384,128]{2,1,0:T(8,128)(2,1)S(1)} async-done(((bf16[16,384,128]{2,1,0:T(8,128)(2,1)}), bf16[16,384,128]{2,1,0:T(8,128)(2,1)S(1)}, u32[]{:S(2)}, u32[]{:S(2)}) %all-to-all-start) | async-done | bytes 1572896 | tf_op jit(solution)/shard_map/all_to_all | solution.py:506
  79.3 0.2 sum_dp.1
  79.5 14.6 %all_to_all.20 = bf16[8,48,128]{2,1,0:T(8,128)(2,1)S(1)} all-to-all(bf16[8,48,128]{2,1,0:T(8,128)(2,1)S(1)} %bitcast.10), channel_id=1, replica_groups={{0,16,32,48,64,80,96,112},{128,144,160,176,192,208,224,240},{256,272,28..., dimensions={0} | all-to-all | bytes 196608 | tf_op jit(solution)/shard_map/all_to_all | solution.py:473
  94.1 0.6 broadcast_in_dim.6
  94.8 9.3 %all-to-all-start.2 = ((f32[4,48,128]{2,1,0:T(8,128)}), f32[4,48,128]{2,1,0:T(8,128)S(1)}, u32[]{:S(2)}, u32[]{:S(2)}) async-start(f32[4,48,128]{2,1,0:T(8,128)} %broadcast_in_dim.6), calls=%async_computation.2 | async-start | bytes 196608 | tf_op jit(solution)/shard_map/all_to_all | solution.py:473
  104.1 11.8 %back.1 = bf16[2,32,32,256]{3,2,1,0:T(8,128)(2,1)} custom-call(s32[1]{0:T(128)} %bitcast.own_ref, s32[2,8]{1,0:T(2,128)} %near_hbm.5, bf16[2,3,32,256]{3,2,1,0:T(8,128)(2,1)} %get-tuple-element.41.h0, bf16[4,3,32,256]{3,2,1,0:T(8,128)(2,1)} %copy-done, bf16[4,3,32,256]{3,2,1,0:T(8,128)(2,1)} %copy-done.1, bf16[3,3,32,256]{3,2,1,0:T(8,128)(2,1)} %copy-done.6, ...), custom_call_target="tpu_custom_call" | custom-call | flops 12000000000 | bytes 1000000 | tf_op jit(solution)/shard_map/back/pallas_call | solution.py:444
  115.9 0.8 all-to-all-done.2
  116.8 10.9 %all_to_all.21.in_ref = bf16[8,48,128]{2,1,0:T(8,128)(2,1)S(1)} all-to-all(bf16[8,48,128]{2,1,0:T(8,128)(2,1)S(1)} %broadcast_in_dim.8), channel_id=1, replica_groups={{0,16,32,48,64,80,96,112},{128,144,160,176,192,208,224,240},{256,272,28..., dimensions={0} | all-to-all | bytes 196608 | tf_op jit(solution)/shard_map/all_to_all | solution.py:473
  127.7 0.8 last.1
  (23 shorter events, 0.1 us)
Async XLA Ops:
  3.1 17.0 %collective-permute-start = (bf16[4,3,32,256]{3,2,1,0:T(8,128)(2,1)}, bf16[4,3,32,256]{3,2,1,0:T(8,128)(2,1)S(1)}, u32[]{:S(2)}, u32[]{:S(2)}) collective-permute-start(bf16[4,3,32,256]{3,2,1,0:T(8,128)(2,1)} %get-tuple-element.30), channel_id=1, source_target_pairs={{0,16},{16,32},{32,48},{48,64},{64,80},{80,96},{96,112},{112,128},... | collective-permute-start | bytes 589832 | tf_op jit(solution)/shard_map/ppermute | solution.py:460
  6.2 14.0 %collective-permute-start.1 = (bf16[4,3,32,256]{3,2,1,0:T(8,128)(2,1)}, bf16[4,3,32,256]{3,2,1,0:T(8,128)(2,1)S(1)}, u32[]{:S(2)}, u32[]{:S(2)}) collective-permute-start(bf16[4,3,32,256]{3,2,1,0:T(8,128)(2,1)} %get-tuple-element.31), channel_id=1, source_target_pairs={{0,496},{16,0},{32,16},{48,32},{64,48},{80,64},{96,80},{112,96},{1... | collective-permute-start | bytes 589832 | tf_op jit(solution)/shard_map/ppermute | solution.py:460
  10.0 8.5 %collective-permute-start.2 = (bf16[3,3,32,256]{3,2,1,0:T(8,128)(2,1)}, bf16[3,3,32,256]{3,2,1,0:T(8,128)(2,1)S(1)}, u32[]{:S(2)}, u32[]{:S(2)}) collective-permute-start(bf16[3,3,32,256]{3,2,1,0:T(8,128)(2,1)} %get-tuple-element.32), channel_id=1, source_target_pairs={{0,32},{16,48},{32,64},{48,80},{64,96},{80,112},{96,128},{112,144}... | collective-permute-start | bytes 442376 | tf_op jit(solution)/shard_map/ppermute | solution.py:460
  11.9 8.2 %collective-permute-start.3 = (bf16[3,3,32,256]{3,2,1,0:T(8,128)(2,1)}, bf16[3,3,32,256]{3,2,1,0:T(8,128)(2,1)S(1)}, u32[]{:S(2)}, u32[]{:S(2)}) collective-permute-start(bf16[3,3,32,256]{3,2,1,0:T(8,128)(2,1)} %get-tuple-element.33), channel_id=1, source_target_pairs={{0,480},{16,496},{32,0},{48,16},{64,32},{80,48},{96,64},{112,80},{... | collective-permute-start | bytes 442376 | tf_op jit(solution)/shard_map/ppermute | solution.py:460
  18.5 1.6 %copy-start.10 = (bf16[3,3,32,256]{3,2,1,0:T(8,128)(2,1)}, bf16[3,3,32,256]{3,2,1,0:T(8,128)(2,1)S(1)}, u32[]{:S(2)}) copy-start(bf16[3,3,32,256]{3,2,1,0:T(8,128)(2,1)S(1)} %collective-permute-done.2.h3) | copy-start | bytes 442372
  20.1 0.7 copy-start.11
  20.1 0.8 copy-start.4
  20.1 0.8 copy-start.5
  52.9 7.0 %copy-start.3 = (bf16[4,3,32,256]{3,2,1,0:T(8,128)(2,1)S(1)}, bf16[4,3,32,256]{3,2,1,0:T(8,128)(2,1)}, u32[]{:S(2)}) copy-start(bf16[4,3,32,256]{3,2,1,0:T(8,128)(2,1)} %get-tuple-element.36) | copy-start | bytes 589828
  52.9 9.2 %copy-start.2 = (bf16[4,3,32,256]{3,2,1,0:T(8,128)(2,1)S(1)}, bf16[4,3,32,256]{3,2,1,0:T(8,128)(2,1)}, u32[]{:S(2)}) copy-start(bf16[4,3,32,256]{3,2,1,0:T(8,128)(2,1)} %get-tuple-element.37) | copy-start | bytes 589828
  52.9 10.8 %copy-start.9 = (bf16[3,3,32,256]{3,2,1,0:T(8,128)(2,1)S(1)}, bf16[3,3,32,256]{3,2,1,0:T(8,128)(2,1)}, u32[]{:S(2)}) copy-start(bf16[3,3,32,256]{3,2,1,0:T(8,128)(2,1)} %get-tuple-element.38) | copy-start | bytes 442372
  52.9 12.7 %copy-start.8 = (bf16[3,3,32,256]{3,2,1,0:T(8,128)(2,1)S(1)}, bf16[3,3,32,256]{3,2,1,0:T(8,128)(2,1)}, u32[]{:S(2)}) copy-start(bf16[3,3,32,256]{3,2,1,0:T(8,128)(2,1)} %get-tuple-element.39) | copy-start | bytes 442372
  52.9 26.4 %all-to-all-start = ((bf16[16,384,128]{2,1,0:T(8,128)(2,1)}), bf16[16,384,128]{2,1,0:T(8,128)(2,1)S(1)}, u32[]{:S(2)}, u32[]{:S(2)}) async-start(bf16[16,384,128]{2,1,0:T(8,128)(2,1)} %get-tuple-element.34), calls=%async_computation | async-start | bytes 3145728 | tf_op jit(solution)/shard_map/all_to_all | solution.py:506
  59.8 13.1 %collective-permute-start.4 = (bf16[4,3,32,256]{3,2,1,0:T(8,128)(2,1)S(1)}, bf16[4,3,32,256]{3,2,1,0:T(8,128)(2,1)S(1)}, u32[]{:S(2)}, u32[]{:S(2)}) collective-permute-start(bf16[4,3,32,256]{3,2,1,0:T(8,128)(2,1)S(1)} %copy-done.3), channel_id=1, source_target_pairs={{0,16},{16,32},{32,48},{48,64},{64,80},{80,96},{96,112},{112,128},... | collective-permute-start | bytes 589832 | tf_op jit(solution)/shard_map/ppermute | solution.py:460
  62.1 10.8 %collective-permute-start.5 = (bf16[4,3,32,256]{3,2,1,0:T(8,128)(2,1)S(1)}, bf16[4,3,32,256]{3,2,1,0:T(8,128)(2,1)S(1)}, u32[]{:S(2)}, u32[]{:S(2)}) collective-permute-start(bf16[4,3,32,256]{3,2,1,0:T(8,128)(2,1)S(1)} %copy-done.2), channel_id=1, source_target_pairs={{0,496},{16,0},{32,16},{48,32},{64,48},{80,64},{96,80},{112,96},{1... | collective-permute-start | bytes 589832 | tf_op jit(solution)/shard_map/ppermute | solution.py:460
  63.7 8.0 %collective-permute-start.6 = (bf16[3,3,32,256]{3,2,1,0:T(8,128)(2,1)S(1)}, bf16[3,3,32,256]{3,2,1,0:T(8,128)(2,1)S(1)}, u32[]{:S(2)}, u32[]{:S(2)}) collective-permute-start(bf16[3,3,32,256]{3,2,1,0:T(8,128)(2,1)S(1)} %copy-done.9), channel_id=1, source_target_pairs={{0,32},{16,48},{32,64},{48,80},{64,96},{80,112},{96,128},{112,144}... | collective-permute-start | bytes 442376 | tf_op jit(solution)/shard_map/ppermute | solution.py:460
  65.6 7.3 %collective-permute-start.7 = (bf16[3,3,32,256]{3,2,1,0:T(8,128)(2,1)S(1)}, bf16[3,3,32,256]{3,2,1,0:T(8,128)(2,1)S(1)}, u32[]{:S(2)}, u32[]{:S(2)}) collective-permute-start(bf16[3,3,32,256]{3,2,1,0:T(8,128)(2,1)S(1)} %copy-done.8), channel_id=1, source_target_pairs={{0,480},{16,496},{32,0},{48,16},{64,32},{80,48},{96,64},{112,80},{... | collective-permute-start | bytes 442376 | tf_op jit(solution)/shard_map/ppermute | solution.py:460
  71.7 32.4 %copy-start.6 = (bf16[3,3,32,256]{3,2,1,0:T(8,128)(2,1)}, bf16[3,3,32,256]{3,2,1,0:T(8,128)(2,1)S(1)}, u32[]{:S(2)}) copy-start(bf16[3,3,32,256]{3,2,1,0:T(8,128)(2,1)S(1)} %collective-permute-done.6.h3) | copy-start | bytes 442372
  72.9 31.2 %copy-start.7 = (bf16[3,3,32,256]{3,2,1,0:T(8,128)(2,1)}, bf16[3,3,32,256]{3,2,1,0:T(8,128)(2,1)S(1)}, u32[]{:S(2)}) copy-start(bf16[3,3,32,256]{3,2,1,0:T(8,128)(2,1)S(1)} %collective-permute-done.7.h4) | copy-start | bytes 442372
  72.9 31.2 %copy-start = (bf16[4,3,32,256]{3,2,1,0:T(8,128)(2,1)}, bf16[4,3,32,256]{3,2,1,0:T(8,128)(2,1)S(1)}, u32[]{:S(2)}) copy-start(bf16[4,3,32,256]{3,2,1,0:T(8,128)(2,1)S(1)} %collective-permute-done.4.h1) | copy-start | bytes 589828
  72.9 31.2 %copy-start.1 = (bf16[4,3,32,256]{3,2,1,0:T(8,128)(2,1)}, bf16[4,3,32,256]{3,2,1,0:T(8,128)(2,1)S(1)}, u32[]{:S(2)}) copy-start(bf16[4,3,32,256]{3,2,1,0:T(8,128)(2,1)S(1)} %collective-permute-done.5.h2) | copy-start | bytes 589828
  94.8 21.9 %all-to-all-start.2 = ((f32[4,48,128]{2,1,0:T(8,128)}), f32[4,48,128]{2,1,0:T(8,128)S(1)}, u32[]{:S(2)}, u32[]{:S(2)}) async-start(f32[4,48,128]{2,1,0:T(8,128)} %broadcast_in_dim.6), calls=%async_computation.2 | async-start | bytes 196608 | tf_op jit(solution)/shard_map/all_to_all | solution.py:473

commit v6 on v5

--- a/solution.py
+++ b/solution.py
@@ -179,8 +179,10 @@
 
 def rim_kernel(own_ref, near_hbm, tile_hbm, *rest, slots):
     outs, (near_ids, tile_ref, rims, stage, sems, out_sems) = rest[:5], rest[5:]
-    wait_all(load((near_hbm, tile_hbm), (near_ids, tile_ref), sems))
+    copies = load((near_hbm, tile_hbm.at[0], tile_hbm.at[1]), (near_ids, tile_ref.at[0], tile_ref.at[1]), sems)
+    copies[0].wait()
     for s in range(2):
+        copies[1 + s].wait()
         rims[4 * s] = tile_ref[s, 0:RIM]
         rims[4 * s + 1] = tile_ref[s, SIZE - RIM : SIZE]
         for side, first, row in ((2, 0, 0), (3, 16, 16 - RIM)):
@@ -236,7 +238,7 @@
         normed_ref[cells, :] = (xhat * gain).astype(BF16)
         return carry
 
-    lax.fori_loop(0, 2 * SIZE * SIZE // ROWS, normalise, 0)
+    lax.fori_loop(0, 2 * SIZE * SIZE // ROWS, normalise, 0, unroll=True)
     wait_all(copies[9:])
     steps = [(t, slice(f * 256, f * 256 + 256)) for t in range(2) for f in range(FF // 256)]
     cells_of = [slice(t * SIZE * SIZE, (t + 1) * SIZE * SIZE) for t in range(2)]
@@ -291,7 +293,7 @@
                 grad_grid[pl.ds(at + part, SIZE, stride=8), :] = piece[:, lanes_of(part)]
         return ggain
 
-    ggain = lax.fori_loop(0, 2 * SIZE * SIZE // ROWS, denormalise, jnp.zeros((8, CH), F32))
+    ggain = lax.fori_loop(0, 2 * SIZE * SIZE // ROWS, denormalise, jnp.zeros((8, CH), F32), unroll=True)
     results = [pltpu.make_async_copy(grad_ref, grad_hbm, out_sems.at[0])]
     results[0].start()
 
@@ -485,7 +487,7 @@
         STRIPS,
         own,
         (),
-        (IDS, TILES, RIMS, stage, pltpu.SemaphoreType.DMA((2,)), STRIP_SEMS),
+        (IDS, TILES, RIMS, stage, pltpu.SemaphoreType.DMA((3,)), STRIP_SEMS),
         far=(neighbours, tiles),
         far_outs=5,
         vmem_mib=60,

time: 129 us -> 128 us (level)
  no operation moved by 1% of the time
where the time goes in v6:
time: 128 us; the launch traced here: 127 us
  Pallas kernels  46.2 us (36%)
  starting transfers between devices  41.7 us (33%)
  blocking collectives  25.5 us (20%)
  waiting for transfers between devices  11.7 us (9%)
  local copies, waits for them, and re-layouts  1.45 us (1%)
    pallas_call x5, Pallas kernels, call(): pl.pallas_call(kernel, out_shape=out, in_specs=[SMEM] * len(scalars) + [v...  46.2 us
    ppermute x8, starting transfers between devices, exchange(): lax.ppermute(strip, 'tiles', [(i, (i + off) % n) for i in range(n)])  25.5 us
    all_to_all x2, blocking collectives, group_exchange(): lax.all_to_all(pieces, 'tiles', 0, 0, tiled=True, axis_index_groups=groups)  25.5 us
    all_to_all x1, starting transfers between devices, group_exchange(): lax.all_to_all(pieces, 'tiles', 0, 0, tiled=True, axis_index_groups=groups)  9.29 us
    all_to_all x1, starting transfers between devices, body(): share = lax.all_to_all(share, 'dp', 0, 0, tiled=True)  6.9 us
    all_to_all x1, waiting for transfers between devices, body(): share = lax.all_to_all(share, 'dp', 0, 0, tiled=True)  6.36 us
    ppermute x8, waiting for transfers between devices, exchange(): lax.ppermute(strip, 'tiles', [(i, (i + off) % n) for i in range(n)])  4.48 us
  transfers between devices with their start and end apart: 10, of which 6 were waited for; matrix products, arithmetic and copies ran while one was open for 0% of the time, Pallas kernels for 9%

profile of v6, /device:TPU:1, one launch (start us, length us, event | category | flops | bytes accessed | tf_op | source)
XLA Modules:
  0.0 127.4 jit_solution(14224135723093405028)
XLA Ops:
  0.6 2.4 %rims.1 = (bf16[2,3,32,256]{3,2,1,0:T(8,128)(2,1)}, bf16[4,3,32,256]{3,2,1,0:T(8,128)(2,1)}, bf16[4,3,32,256]{3,2,1,0:T(8,128)(2,1)}, bf16[3,3,32,256]{3,2,1,0:T(8,128)(2,1)}, bf16[3,3,32,256]{3,2,1,0:T(8,128)(2,1)}) custom-call(s32[1]{0:T(128)} %bitcast.own_ref, s32[2,8]{1,0:T(2,128)} %near_hbm.5, bf16[2,32,32,256]{3,2,1,0:T(8,128)(2,1)} %bitcast.11), custom_call_target="tpu_custom_call" | custom-call | flops 1000000 | bytes 1000000 | tf_op jit(solution)/shard_map/rims/pallas_call | solution.py:446
  3.0 3.0 %collective-permute-start = (bf16[4,3,32,256]{3,2,1,0:T(8,128)(2,1)}, bf16[4,3,32,256]{3,2,1,0:T(8,128)(2,1)S(1)}, u32[]{:S(2)}, u32[]{:S(2)}) collective-permute-start(bf16[4,3,32,256]{3,2,1,0:T(8,128)(2,1)} %get-tuple-element.30), channel_id=1, source_target_pairs={{0,16},{16,32},{32,48},{48,64},{64,80},{80,96},{96,112},{112,128},... | collective-permute-start | bytes 589832 | tf_op jit(solution)/shard_map/ppermute | solution.py:462
  6.0 3.9 %collective-permute-start.1 = (bf16[4,3,32,256]{3,2,1,0:T(8,128)(2,1)}, bf16[4,3,32,256]{3,2,1,0:T(8,128)(2,1)S(1)}, u32[]{:S(2)}, u32[]{:S(2)}) collective-permute-start(bf16[4,3,32,256]{3,2,1,0:T(8,128)(2,1)} %get-tuple-element.31), channel_id=1, source_target_pairs={{0,496},{16,0},{32,16},{48,32},{64,48},{80,64},{96,80},{112,96},{1... | collective-permute-start | bytes 589832 | tf_op jit(solution)/shard_map/ppermute | solution.py:462
  9.9 1.9 %collective-permute-start.2 = (bf16[3,3,32,256]{3,2,1,0:T(8,128)(2,1)}, bf16[3,3,32,256]{3,2,1,0:T(8,128)(2,1)S(1)}, u32[]{:S(2)}, u32[]{:S(2)}) collective-permute-start(bf16[3,3,32,256]{3,2,1,0:T(8,128)(2,1)} %get-tuple-element.32), channel_id=1, source_target_pairs={{0,32},{16,48},{32,64},{48,80},{64,96},{80,112},{96,128},{112,144}... | collective-permute-start | bytes 442376 | tf_op jit(solution)/shard_map/ppermute | solution.py:462
  11.8 5.7 %collective-permute-start.3 = (bf16[3,3,32,256]{3,2,1,0:T(8,128)(2,1)}, bf16[3,3,32,256]{3,2,1,0:T(8,128)(2,1)S(1)}, u32[]{:S(2)}, u32[]{:S(2)}) collective-permute-start(bf16[3,3,32,256]{3,2,1,0:T(8,128)(2,1)} %get-tuple-element.33), channel_id=1, source_target_pairs={{0,480},{16,496},{32,0},{48,16},{64,32},{80,48},{96,64},{112,80},{... | collective-permute-start | bytes 442376 | tf_op jit(solution)/shard_map/ppermute | solution.py:462
  17.6 0.8 collective-permute-done.2.h3
  18.4 1.6 %collective-permute-done.3.h4 = bf16[3,3,32,256]{3,2,1,0:T(8,128)(2,1)S(1)} collective-permute-done((bf16[3,3,32,256]{3,2,1,0:T(8,128)(2,1)}, bf16[3,3,32,256]{3,2,1,0:T(8,128)(2,1)S(1)}, u32[]{:S(2)}, u32[]{:S(2)}) %collective-permute-start.3) | collective-permute-done | bytes 147488 | tf_op jit(solution)/shard_map/ppermute | solution.py:462
  20.0 0.0 collective-permute-done.h1
  20.0 0.0 collective-permute-done.1.h2
  20.0 0.0 copy-start.5
  20.0 0.6 copy-done.11
  20.6 0.1 copy-done.4
  20.7 0.0 copy-done.5
  20.8 31.0 %main.1 = (bf16[16,384,128]{2,1,0:T(8,128)(2,1)}, bf16[2048,256]{1,0:T(8,128)(2,1)}, bf16[2,3,32,256]{3,2,1,0:T(8,128)(2,1)}, bf16[4,3,32,256]{3,2,1,0:T(8,128)(...) custom-call(s32[1]{0:T(128)} %bitcast.own_ref, ...), custom_call_target="tpu_custom_call" | custom-call | flops 40000000000 | bytes 1000000 | tf_op jit(solution)/shard_map/main/pallas_call | solution.py:446
  51.9 6.9 %all-to-all-start = ((bf16[16,384,128]{2,1,0:T(8,128)(2,1)}), bf16[16,384,128]{2,1,0:T(8,128)(2,1)S(1)}, u32[]{:S(2)}, u32[]{:S(2)}) async-start(bf16[16,384,128]{2,1,0:T(8,128)(2,1)} %get-tuple-element.34), calls=%async_computation | async-start | bytes 3145728 | tf_op jit(solution)/shard_map/all_to_all | solution.py:508
  58.8 2.2 %collective-permute-start.4 = (bf16[4,3,32,256]{3,2,1,0:T(8,128)(2,1)S(1)}, bf16[4,3,32,256]{3,2,1,0:T(8,128)(2,1)S(1)}, u32[]{:S(2)}, u32[]{:S(2)}) collective-permute-start(bf16[4,3,32,256]{3,2,1,0:T(8,128)(2,1)S(1)} %copy-done.3), channel_id=1, source_target_pairs={{0,16},{16,32},{32,48},{48,64},{64,80},{80,96},{96,112},{112,128},... | collective-permute-start | bytes 589832 | tf_op jit(solution)/shard_map/ppermute | solution.py:462
  61.0 1.6 %collective-permute-start.5 = (bf16[4,3,32,256]{3,2,1,0:T(8,128)(2,1)S(1)}, bf16[4,3,32,256]{3,2,1,0:T(8,128)(2,1)S(1)}, u32[]{:S(2)}, u32[]{:S(2)}) collective-permute-start(bf16[4,3,32,256]{3,2,1,0:T(8,128)(2,1)S(1)} %copy-done.2), channel_id=1, source_target_pairs={{0,496},{16,0},{32,16},{48,32},{64,48},{80,64},{96,80},{112,96},{1... | collective-permute-start | bytes 589832 | tf_op jit(solution)/shard_map/ppermute | solution.py:462
  62.6 1.9 %collective-permute-start.6 = (bf16[3,3,32,256]{3,2,1,0:T(8,128)(2,1)S(1)}, bf16[3,3,32,256]{3,2,1,0:T(8,128)(2,1)S(1)}, u32[]{:S(2)}, u32[]{:S(2)}) collective-permute-start(bf16[3,3,32,256]{3,2,1,0:T(8,128)(2,1)S(1)} %copy-done.9), channel_id=1, source_target_pairs={{0,32},{16,48},{32,64},{48,80},{64,96},{80,112},{96,128},{112,144}... | collective-permute-start | bytes 442376 | tf_op jit(solution)/shard_map/ppermute | solution.py:462
  64.5 5.2 %collective-permute-start.7 = (bf16[3,3,32,256]{3,2,1,0:T(8,128)(2,1)S(1)}, bf16[3,3,32,256]{3,2,1,0:T(8,128)(2,1)S(1)}, u32[]{:S(2)}, u32[]{:S(2)}) collective-permute-start(bf16[3,3,32,256]{3,2,1,0:T(8,128)(2,1)S(1)} %copy-done.8), channel_id=1, source_target_pairs={{0,480},{16,496},{32,0},{48,16},{64,32},{80,48},{96,64},{112,80},{... | collective-permute-start | bytes 442376 | tf_op jit(solution)/shard_map/ppermute | solution.py:462
  69.8 0.9 collective-permute-done.6.h3
  70.6 1.2 collective-permute-done.7.h4
  71.9 0.0 collective-permute-done.4.h1
  71.9 0.0 collective-permute-done.5.h2
  71.9 6.4 %all-to-all-done.in_ref = bf16[16,384,128]{2,1,0:T(8,128)(2,1)S(1)} async-done(((bf16[16,384,128]{2,1,0:T(8,128)(2,1)}), bf16[16,384,128]{2,1,0:T(8,128)(2,1)S(1)}, u32[]{:S(2)}, u32[]{:S(2)}) %all-to-all-start) | async-done | bytes 1572896 | tf_op jit(solution)/shard_map/all_to_all | solution.py:508
  78.2 0.2 sum_dp.1
  78.4 14.6 %all_to_all.20 = bf16[8,48,128]{2,1,0:T(8,128)(2,1)S(1)} all-to-all(bf16[8,48,128]{2,1,0:T(8,128)(2,1)S(1)} %bitcast.10), channel_id=1, replica_groups={{0,16,32,48,64,80,96,112},{128,144,160,176,192,208,224,240},{256,272,28..., dimensions={0} | all-to-all | bytes 196608 | tf_op jit(solution)/shard_map/all_to_all | solution.py:475
  93.1 0.6 broadcast_in_dim.6
  93.7 9.3 %all-to-all-start.2 = ((f32[4,48,128]{2,1,0:T(8,128)}), f32[4,48,128]{2,1,0:T(8,128)S(1)}, u32[]{:S(2)}, u32[]{:S(2)}) async-start(f32[4,48,128]{2,1,0:T(8,128)} %broadcast_in_dim.6), calls=%async_computation.2 | async-start | bytes 196608 | tf_op jit(solution)/shard_map/all_to_all | solution.py:475
  103.0 11.8 %back.1 = bf16[2,32,32,256]{3,2,1,0:T(8,128)(2,1)} custom-call(s32[1]{0:T(128)} %bitcast.own_ref, s32[2,8]{1,0:T(2,128)} %near_hbm.5, bf16[2,3,32,256]{3,2,1,0:T(8,128)(2,1)} %get-tuple-element.41.h0, bf16[4,3,32,256]{3,2,1,0:T(8,128)(2,1)} %copy-done, bf16[4,3,32,256]{3,2,1,0:T(8,128)(2,1)} %copy-done.1, bf16[3,3,32,256]{3,2,1,0:T(8,128)(2,1)} %copy-done.6, ...), custom_call_target="tpu_custom_call" | custom-call | flops 12000000000 | bytes 1000000 | tf_op jit(solution)/shard_map/back/pallas_call | solution.py:446
  114.8 0.8 all-to-all-done.2
  115.7 10.9 %all_to_all.21.in_ref = bf16[8,48,128]{2,1,0:T(8,128)(2,1)S(1)} all-to-all(bf16[8,48,128]{2,1,0:T(8,128)(2,1)S(1)} %broadcast_in_dim.8), channel_id=1, replica_groups={{0,16,32,48,64,80,96,112},{128,144,160,176,192,208,224,240},{256,272,28..., dimensions={0} | all-to-all | bytes 196608 | tf_op jit(solution)/shard_map/all_to_all | solution.py:475
  126.6 0.8 last.1
  (23 shorter events, 0.1 us)
Async XLA Ops:
  3.0 17.0 %collective-permute-start = (bf16[4,3,32,256]{3,2,1,0:T(8,128)(2,1)}, bf16[4,3,32,256]{3,2,1,0:T(8,128)(2,1)S(1)}, u32[]{:S(2)}, u32[]{:S(2)}) collective-permute-start(bf16[4,3,32,256]{3,2,1,0:T(8,128)(2,1)} %get-tuple-element.30), channel_id=1, source_target_pairs={{0,16},{16,32},{32,48},{48,64},{64,80},{80,96},{96,112},{112,128},... | collective-permute-start | bytes 589832 | tf_op jit(solution)/shard_map/ppermute | solution.py:462
  6.0 14.0 %collective-permute-start.1 = (bf16[4,3,32,256]{3,2,1,0:T(8,128)(2,1)}, bf16[4,3,32,256]{3,2,1,0:T(8,128)(2,1)S(1)}, u32[]{:S(2)}, u32[]{:S(2)}) collective-permute-start(bf16[4,3,32,256]{3,2,1,0:T(8,128)(2,1)} %get-tuple-element.31), channel_id=1, source_target_pairs={{0,496},{16,0},{32,16},{48,32},{64,48},{80,64},{96,80},{112,96},{1... | collective-permute-start | bytes 589832 | tf_op jit(solution)/shard_map/ppermute | solution.py:462
  9.9 8.5 %collective-permute-start.2 = (bf16[3,3,32,256]{3,2,1,0:T(8,128)(2,1)}, bf16[3,3,32,256]{3,2,1,0:T(8,128)(2,1)S(1)}, u32[]{:S(2)}, u32[]{:S(2)}) collective-permute-start(bf16[3,3,32,256]{3,2,1,0:T(8,128)(2,1)} %get-tuple-element.32), channel_id=1, source_target_pairs={{0,32},{16,48},{32,64},{48,80},{64,96},{80,112},{96,128},{112,144}... | collective-permute-start | bytes 442376 | tf_op jit(solution)/shard_map/ppermute | solution.py:462
  11.8 8.2 %collective-permute-start.3 = (bf16[3,3,32,256]{3,2,1,0:T(8,128)(2,1)}, bf16[3,3,32,256]{3,2,1,0:T(8,128)(2,1)S(1)}, u32[]{:S(2)}, u32[]{:S(2)}) collective-permute-start(bf16[3,3,32,256]{3,2,1,0:T(8,128)(2,1)} %get-tuple-element.33), channel_id=1, source_target_pairs={{0,480},{16,496},{32,0},{48,16},{64,32},{80,48},{96,64},{112,80},{... | collective-permute-start | bytes 442376 | tf_op jit(solution)/shard_map/ppermute | solution.py:462
  18.4 1.6 %copy-start.10 = (bf16[3,3,32,256]{3,2,1,0:T(8,128)(2,1)}, bf16[3,3,32,256]{3,2,1,0:T(8,128)(2,1)S(1)}, u32[]{:S(2)}) copy-start(bf16[3,3,32,256]{3,2,1,0:T(8,128)(2,1)S(1)} %collective-permute-done.2.h3) | copy-start | bytes 442372
  20.0 0.7 copy-start.11
  20.0 0.8 copy-start.4
  20.0 0.8 copy-start.5
  51.8 6.9 %copy-start.3 = (bf16[4,3,32,256]{3,2,1,0:T(8,128)(2,1)S(1)}, bf16[4,3,32,256]{3,2,1,0:T(8,128)(2,1)}, u32[]{:S(2)}) copy-start(bf16[4,3,32,256]{3,2,1,0:T(8,128)(2,1)} %get-tuple-element.36) | copy-start | bytes 589828
  51.8 9.2 %copy-start.2 = (bf16[4,3,32,256]{3,2,1,0:T(8,128)(2,1)S(1)}, bf16[4,3,32,256]{3,2,1,0:T(8,128)(2,1)}, u32[]{:S(2)}) copy-start(bf16[4,3,32,256]{3,2,1,0:T(8,128)(2,1)} %get-tuple-element.37) | copy-start | bytes 589828
  51.8 10.8 %copy-start.9 = (bf16[3,3,32,256]{3,2,1,0:T(8,128)(2,1)S(1)}, bf16[3,3,32,256]{3,2,1,0:T(8,128)(2,1)}, u32[]{:S(2)}) copy-start(bf16[3,3,32,256]{3,2,1,0:T(8,128)(2,1)} %get-tuple-element.38) | copy-start | bytes 442372
  51.9 12.7 %copy-start.8 = (bf16[3,3,32,256]{3,2,1,0:T(8,128)(2,1)S(1)}, bf16[3,3,32,256]{3,2,1,0:T(8,128)(2,1)}, u32[]{:S(2)}) copy-start(bf16[3,3,32,256]{3,2,1,0:T(8,128)(2,1)} %get-tuple-element.39) | copy-start | bytes 442372
  51.9 26.4 %all-to-all-start = ((bf16[16,384,128]{2,1,0:T(8,128)(2,1)}), bf16[16,384,128]{2,1,0:T(8,128)(2,1)S(1)}, u32[]{:S(2)}, u32[]{:S(2)}) async-start(bf16[16,384,128]{2,1,0:T(8,128)(2,1)} %get-tuple-element.34), calls=%async_computation | async-start | bytes 3145728 | tf_op jit(solution)/shard_map/all_to_all | solution.py:508
  58.8 13.1 %collective-permute-start.4 = (bf16[4,3,32,256]{3,2,1,0:T(8,128)(2,1)S(1)}, bf16[4,3,32,256]{3,2,1,0:T(8,128)(2,1)S(1)}, u32[]{:S(2)}, u32[]{:S(2)}) collective-permute-start(bf16[4,3,32,256]{3,2,1,0:T(8,128)(2,1)S(1)} %copy-done.3), channel_id=1, source_target_pairs={{0,16},{16,32},{32,48},{48,64},{64,80},{80,96},{96,112},{112,128},... | collective-permute-start | bytes 589832 | tf_op jit(solution)/shard_map/ppermute | solution.py:462
  61.0 10.9 %collective-permute-start.5 = (bf16[4,3,32,256]{3,2,1,0:T(8,128)(2,1)S(1)}, bf16[4,3,32,256]{3,2,1,0:T(8,128)(2,1)S(1)}, u32[]{:S(2)}, u32[]{:S(2)}) collective-permute-start(bf16[4,3,32,256]{3,2,1,0:T(8,128)(2,1)S(1)} %copy-done.2), channel_id=1, source_target_pairs={{0,496},{16,0},{32,16},{48,32},{64,48},{80,64},{96,80},{112,96},{1... | collective-permute-start | bytes 589832 | tf_op jit(solution)/shard_map/ppermute | solution.py:462
  62.6 8.0 %collective-permute-start.6 = (bf16[3,3,32,256]{3,2,1,0:T(8,128)(2,1)S(1)}, bf16[3,3,32,256]{3,2,1,0:T(8,128)(2,1)S(1)}, u32[]{:S(2)}, u32[]{:S(2)}) collective-permute-start(bf16[3,3,32,256]{3,2,1,0:T(8,128)(2,1)S(1)} %copy-done.9), channel_id=1, source_target_pairs={{0,32},{16,48},{32,64},{48,80},{64,96},{80,112},{96,128},{112,144}... | collective-permute-start | bytes 442376 | tf_op jit(solution)/shard_map/ppermute | solution.py:462
  64.5 7.3 %collective-permute-start.7 = (bf16[3,3,32,256]{3,2,1,0:T(8,128)(2,1)S(1)}, bf16[3,3,32,256]{3,2,1,0:T(8,128)(2,1)S(1)}, u32[]{:S(2)}, u32[]{:S(2)}) collective-permute-start(bf16[3,3,32,256]{3,2,1,0:T(8,128)(2,1)S(1)} %copy-done.8), channel_id=1, source_target_pairs={{0,480},{16,496},{32,0},{48,16},{64,32},{80,48},{96,64},{112,80},{... | collective-permute-start | bytes 442376 | tf_op jit(solution)/shard_map/ppermute | solution.py:462
  70.6 32.4 %copy-start.6 = (bf16[3,3,32,256]{3,2,1,0:T(8,128)(2,1)}, bf16[3,3,32,256]{3,2,1,0:T(8,128)(2,1)S(1)}, u32[]{:S(2)}) copy-start(bf16[3,3,32,256]{3,2,1,0:T(8,128)(2,1)S(1)} %collective-permute-done.6.h3) | copy-start | bytes 442372
  71.9 31.1 %copy-start.7 = (bf16[3,3,32,256]{3,2,1,0:T(8,128)(2,1)}, bf16[3,3,32,256]{3,2,1,0:T(8,128)(2,1)S(1)}, u32[]{:S(2)}) copy-start(bf16[3,3,32,256]{3,2,1,0:T(8,128)(2,1)S(1)} %collective-permute-done.7.h4) | copy-start | bytes 442372
  71.9 31.1 %copy-start = (bf16[4,3,32,256]{3,2,1,0:T(8,128)(2,1)}, bf16[4,3,32,256]{3,2,1,0:T(8,128)(2,1)S(1)}, u32[]{:S(2)}) copy-start(bf16[4,3,32,256]{3,2,1,0:T(8,128)(2,1)S(1)} %collective-permute-done.4.h1) | copy-start | bytes 589828
  71.9 31.1 %copy-start.1 = (bf16[4,3,32,256]{3,2,1,0:T(8,128)(2,1)}, bf16[4,3,32,256]{3,2,1,0:T(8,128)(2,1)S(1)}, u32[]{:S(2)}) copy-start(bf16[4,3,32,256]{3,2,1,0:T(8,128)(2,1)S(1)} %collective-permute-done.5.h2) | copy-start | bytes 589828
  93.7 22.0 %all-to-all-start.2 = ((f32[4,48,128]{2,1,0:T(8,128)}), f32[4,48,128]{2,1,0:T(8,128)S(1)}, u32[]{:S(2)}, u32[]{:S(2)}) async-start(f32[4,48,128]{2,1,0:T(8,128)} %broadcast_in_dim.6), calls=%async_computation.2 | async-start | bytes 196608 | tf_op jit(solution)/shard_map/all_to_all | solution.py:475
